TPU v7x, 32 devices: a whole 2x2x4 slice. The times are simulated.
32 devices in a mesh: grp: 4 (over y, core), seq: 8 (over z, x).
Axes of the slice: x: 2, y: 2, z: 4, core: 2. Of those that a mesh axis runs over, the one named last changes fastest.
Arguments:
- tokens: bfloat16 [8, 2048, 1024], P('grp', 'seq'), may hold values from -6 to 6
- seq_lens: int32 [4, 2], P('grp'), may hold values from 1 to 2048, 2560 in all within a row
- norm_attn: bfloat16 [2, 1024], P(None, ('grp', 'seq')), may hold values from 0.25 to 1.75
- w_qkv: bfloat16 [2, 1024, 3072], P(None, ('grp', 'seq')), may hold values from -0.1875 to 0.1875
- w_out: bfloat16 [2, 1024, 1024], P(None, ('grp', 'seq')), may hold values from -3 to 3
- norm_ffn: bfloat16 [2, 1024], P(None, ('grp', 'seq')), may hold values from 0.25 to 1.75
- w_gate: bfloat16 [2, 1024, 2816], P(None, ('grp', 'seq')), may hold values from -0.1875 to 0.1875
- w_up: bfloat16 [2, 1024, 2816], P(None, ('grp', 'seq')), may hold values from -0.1875 to 0.1875
- w_down: bfloat16 [2, 2816, 1024], P(None, ('grp', 'seq')), may hold values from -0.109375 to 0.109375
- cotangent: bfloat16 [8, 2048, 1024], P('grp', 'seq'), may hold values from -6 to 6
Outputs:
- layer_out: bfloat16 [8, 2048, 1024], P('grp', 'seq')
- input_grad: float32 [8, 2048, 1024], P('grp', 'seq')
- norm_attn_grad: float32 [2, 1024], P(None, ('grp', 'seq'))
- w_qkv_grad: float32 [2, 1024, 3072], P(None, ('grp', 'seq'))
- w_out_grad: float32 [2, 1024, 1024], P(None, ('grp', 'seq'))
- norm_ffn_grad: float32 [2, 1024], P(None, ('grp', 'seq'))
- w_gate_grad: float32 [2, 1024, 2816], P(None, ('grp', 'seq'))
- w_up_grad: float32 [2, 1024, 2816], P(None, ('grp', 'seq'))
- w_down_grad: float32 [2, 2816, 1024], P(None, ('grp', 'seq'))
Inputs may be any that keep to these rules, and one draw needn't show every extreme that they name: `seq_lens`: in each row the 2 lengths add up to 2560.
All inputs are finite; a program needn't handle non-finite values.
Results may differ from a plain program's by a relative error of at most 0.02.
Values may be sent and summed in bfloat16 or wider, within the bound.
No kernel may reach another device: no remote copies, remote signals or barrier semaphores. Data moves between devices by JAX's collectives and lax.ppermute only.
A program may use at most 640 MiB of HBM per device.

v0:
```python
import jax
import jax.numpy as jnp
from jax import lax
from jax.sharding import PartitionSpec as P

HEADS = 16


EPSILON = 1e-06
NEGATIVE = -1e30
PRECISE = lax.Precision.HIGHEST


def block_spans(total_rows):
    return [(offset, min(512, total_rows - offset)) for offset in range(0, total_rows, 512)]


def rotate(field, cosine, sine_table):
    half_dim = field.shape[-1] // 2
    first_half = field[..., :half_dim]
    second_half = field[..., half_dim:]
    return jnp.concatenate(
        [
            first_half * cosine - second_half * sine_table,
            second_half * cosine + first_half * sine_table,
        ],
        axis=-1,
    )


def allowed(query_pos, key_pos, lengths):
    causal = key_pos[None, None, :] <= query_pos[None, :, None]
    inside = key_pos[None, None, :] < lengths[:, None, None]
    return (causal & inside)[:, None, :, :]


def attend(q_heads, k_flat, v_flat, lengths, positions, score_scale):
    seq_count, stretch_len, head_count, head_dim = q_heads.shape
    first_row = jnp.int32(0)
    k_piece = lax.all_gather(k_flat, "seq", axis=1, tiled=True)
    v_piece = lax.all_gather(v_flat, "seq", axis=1, tiled=True)
    running_max = jnp.full((seq_count, head_count, stretch_len), NEGATIVE, jnp.float32)
    row_total = jnp.zeros((seq_count, head_count, stretch_len), jnp.float32)
    weighted = jnp.zeros((seq_count, stretch_len, head_count, head_dim), jnp.float32)
    for offset, block_len in block_spans(k_piece.shape[1]):
        k_block = k_piece[:, offset : offset + block_len].reshape(
            seq_count, block_len, head_count, head_dim
        )
        v_block = (
            v_piece[:, offset : offset + block_len]
            .reshape(seq_count, block_len, head_count, head_dim)
            .astype(jnp.float32)
        )
        key_pos = first_row + offset + jnp.arange(block_len, dtype=jnp.int32)
        allowed_mask = allowed(positions, key_pos, lengths)
        logits = (
            jnp.einsum("sqhd,skhd->shqk", q_heads, k_block, preferred_element_type=jnp.float32)
            * score_scale
        )
        new_max = jnp.maximum(
            running_max, jnp.max(jnp.where(allowed_mask, logits, NEGATIVE), axis=-1)
        )
        probs = jnp.where(allowed_mask, jnp.exp(logits - new_max[..., None]), 0.0)
        rescale = jnp.exp(running_max - new_max)
        row_total = row_total * rescale + jnp.sum(probs, axis=-1)
        weighted = weighted * jnp.transpose(rescale, (0, 2, 1))[..., None] + jnp.einsum(
            "shqk,skhd->sqhd", probs, v_block, precision=PRECISE, preferred_element_type=jnp.float32
        )
        running_max = new_max
    running_max, row_total, weighted = (running_max, row_total, weighted)
    attended = weighted / jnp.transpose(row_total, (0, 2, 1))[..., None]
    return (attended, running_max + jnp.log(row_total))


def attend_back(
    q_heads,
    k_heads,
    v_heads,
    q_flat,
    k_flat,
    v_flat,
    grad_heads,
    grad_flat,
    log_total,
    delta_rows,
    lengths,
    positions,
    score_scale,
):
    seq_count, stretch_len, head_count, head_dim = q_heads.shape
    zeros_heads = jnp.zeros((seq_count, stretch_len, head_count, head_dim), jnp.float32)
    carry = zeros_heads
    first_row = jnp.int32(0)
    k_piece = lax.all_gather(k_flat, "seq", axis=1, tiled=True)
    v_piece = lax.all_gather(v_flat, "seq", axis=1, tiled=True)
    for offset, block_len in block_spans(k_piece.shape[1]):
        k_block = k_piece[:, offset : offset + block_len].reshape(
            seq_count, block_len, head_count, head_dim
        )
        v_block = v_piece[:, offset : offset + block_len].reshape(
            seq_count, block_len, head_count, head_dim
        )
        key_pos = first_row + offset + jnp.arange(block_len, dtype=jnp.int32)
        allowed_mask = allowed(positions, key_pos, lengths)
        logits = (
            jnp.einsum("sqhd,skhd->shqk", q_heads, k_block, preferred_element_type=jnp.float32)
            * score_scale
        )
        probs = jnp.where(allowed_mask, jnp.exp(logits - log_total[..., None]), 0.0)
        grad_probs = jnp.einsum(
            "sqhd,skhd->shqk", grad_heads, v_block, preferred_element_type=jnp.float32
        )
        grad_logits = (probs * (grad_probs - delta_rows[..., None])).astype(jnp.bfloat16)
        carry = (
            carry
            + jnp.einsum(
                "shqk,skhd->sqhd", grad_logits, k_block, preferred_element_type=jnp.float32
            )
            * score_scale
        )
    gathered_stats = (
        lax.all_gather(log_total, "seq", axis=2, tiled=True),
        lax.all_gather(delta_rows, "seq", axis=2, tiled=True),
    )
    first_row = jnp.int32(0)
    q_piece = lax.all_gather(q_flat, "seq", axis=1, tiled=True)
    g_piece = lax.all_gather(grad_flat, "seq", axis=1, tiled=True)
    grad_key = zeros_heads
    grad_value = zeros_heads
    for offset, block_len in block_spans(q_piece.shape[1]):
        q_block = q_piece[:, offset : offset + block_len].reshape(
            seq_count, block_len, head_count, head_dim
        )
        g_block = g_piece[:, offset : offset + block_len].reshape(
            seq_count, block_len, head_count, head_dim
        )
        query_pos = first_row + offset + jnp.arange(block_len, dtype=jnp.int32)
        allowed_mask = allowed(query_pos, positions, lengths)
        lse_block = lax.dynamic_slice_in_dim(gathered_stats[0], offset, block_len, 2)
        delta_block = lax.dynamic_slice_in_dim(gathered_stats[1], offset, block_len, 2)
        logits = (
            jnp.einsum("sqhd,skhd->shqk", q_block, k_heads, preferred_element_type=jnp.float32)
            * score_scale
        )
        probs = jnp.where(allowed_mask, jnp.exp(logits - lse_block[..., None]), 0.0)
        grad_value = grad_value + jnp.einsum(
            "shqk,sqhd->skhd",
            probs,
            g_block.astype(jnp.float32),
            precision=PRECISE,
            preferred_element_type=jnp.float32,
        )
        grad_probs = jnp.einsum(
            "sqhd,skhd->shqk", g_block, v_heads, preferred_element_type=jnp.float32
        )
        grad_logits = (probs * (grad_probs - delta_block[..., None])).astype(jnp.bfloat16)
        grad_key = (
            grad_key
            + jnp.einsum(
                "shqk,sqhd->skhd", grad_logits, q_block, preferred_element_type=jnp.float32
            )
            * score_scale
        )
    grad_key, grad_value = (grad_key, grad_value)
    return (carry, grad_key, grad_value)


def body(tokens, seq_lens, norm_attn, w_qkv, w_out, norm_ffn, w_gate, w_up, w_down, cotangent):
    seq_count, stretch_len, model_width = tokens.shape
    head_count = HEADS
    head_dim = model_width // head_count
    score_scale = head_dim ** (-0.5)
    lengths = seq_lens[0]
    positions = lax.axis_index("seq") * stretch_len + jnp.arange(stretch_len, dtype=jnp.int32)
    half_dim = head_dim // 2
    freqs = 10000.0 ** (-jnp.arange(half_dim, dtype=jnp.float32) / half_dim)
    angle = positions.astype(jnp.float32)[:, None] * freqs[None, :]
    cosine = jnp.cos(angle)[:, None, :]
    sine_table = jnp.sin(angle)[:, None, :]

    def heads_of(field):
        return field.reshape(seq_count, stretch_len, head_count, head_dim)

    def gather_layer(layer_index):
        return (
            lax.all_gather(norm_attn[layer_index], ("grp", "seq"), axis=0, tiled=True),
            lax.all_gather(w_qkv[layer_index], ("grp", "seq"), axis=0, tiled=True),
            lax.all_gather(w_out[layer_index], ("grp", "seq"), axis=0, tiled=True),
            lax.all_gather(norm_ffn[layer_index], ("grp", "seq"), axis=0, tiled=True),
            lax.all_gather(w_gate[layer_index], ("grp", "seq"), axis=0, tiled=True),
            lax.all_gather(w_up[layer_index], ("grp", "seq"), axis=0, tiled=True),
            lax.all_gather(w_down[layer_index], ("grp", "seq"), axis=0, tiled=True),
        )

    def gather_again(layer_index):
        return (
            lax.all_gather(norm_attn[layer_index], ("grp", "seq"), axis=0, tiled=True),
            lax.all_gather(w_qkv[layer_index], ("grp", "seq"), axis=0, tiled=True),
            lax.all_gather(w_out[layer_index], ("grp", "seq"), axis=0, tiled=True),
            lax.all_gather(norm_ffn[layer_index], ("grp", "seq"), axis=0, tiled=True),
            lax.all_gather(w_gate[layer_index], ("grp", "seq"), axis=0, tiled=True),
            lax.all_gather(w_up[layer_index], ("grp", "seq"), axis=0, tiled=True),
            lax.all_gather(w_down[layer_index], ("grp", "seq"), axis=0, tiled=True),
        )

    def forward_layer(inputs, params, first_value):
        gain_one, mat_qkv, mat_out, gain_two, mat_gate, mat_up, mat_down = params
        rms_one = lax.rsqrt(jnp.mean(inputs * inputs, axis=-1, keepdims=True) + EPSILON)
        normed = (inputs * rms_one * gain_one.astype(jnp.float32)).astype(jnp.bfloat16)
        projected = jnp.dot(normed, mat_qkv, preferred_element_type=jnp.float32)
        query_raw = projected[:, :model_width]
        key_raw = projected[:, model_width : 2 * model_width]
        value_raw = projected[:, 2 * model_width :]
        if first_value is None:
            values = value_raw.astype(jnp.bfloat16)
        else:
            values = (0.5 * value_raw + 0.5 * first_value.astype(jnp.float32)).astype(jnp.bfloat16)
        query_rot = rotate(heads_of(query_raw), cosine, sine_table).astype(jnp.bfloat16)
        key_rot = rotate(heads_of(key_raw), cosine, sine_table).astype(jnp.bfloat16)
        attended, log_total = attend(
            query_rot,
            key_rot.reshape(seq_count, stretch_len, model_width),
            values.reshape(seq_count, stretch_len, model_width),
            lengths,
            positions,
            score_scale,
        )
        attn_low = attended.reshape(-1, model_width).astype(jnp.bfloat16)
        middle = inputs + jnp.dot(attn_low, mat_out, preferred_element_type=jnp.float32)
        rms_two = lax.rsqrt(jnp.mean(middle * middle, axis=-1, keepdims=True) + EPSILON)
        normed_two = (middle * rms_two * gain_two.astype(jnp.float32)).astype(jnp.bfloat16)
        gate_pre = jnp.dot(normed_two, mat_gate, preferred_element_type=jnp.float32)
        up_pre = jnp.dot(normed_two, mat_up, preferred_element_type=jnp.float32)
        hidden = (jax.nn.silu(gate_pre) * up_pre).astype(jnp.bfloat16)
        result = middle + jnp.dot(hidden, mat_down, preferred_element_type=jnp.float32)
        kept = (
            inputs,
            rms_one,
            normed,
            query_rot,
            key_rot,
            values,
            attended,
            attn_low,
            log_total,
            middle,
            rms_two,
            normed_two,
            gate_pre,
            up_pre,
            hidden,
        )
        return (result, values, kept)

    def backward_layer(grad_in, params, kept, first_grad):
        gain_one, mat_qkv, mat_out, gain_two, mat_gate, mat_up, mat_down = params
        (
            inputs,
            rms_one,
            normed,
            query_rot,
            key_rot,
            values,
            attended,
            attn_low,
            log_total,
            middle,
            rms_two,
            normed_two,
            gate_pre,
            up_pre,
            hidden,
        ) = kept
        grad_low = grad_in.astype(jnp.bfloat16)
        grad_down = jnp.einsum("nf,nd->fd", hidden, grad_low, preferred_element_type=jnp.float32)
        grad_hidden = jnp.einsum(
            "nd,fd->nf", grad_low, mat_down, preferred_element_type=jnp.float32
        )
        sigma = jax.nn.sigmoid(gate_pre)
        grad_gate_pre = (grad_hidden * up_pre * sigma * (1.0 + gate_pre * (1.0 - sigma))).astype(
            jnp.bfloat16
        )
        grad_up_pre = (grad_hidden * gate_pre * sigma).astype(jnp.bfloat16)
        grad_gate = jnp.einsum(
            "nd,nf->df", normed_two, grad_gate_pre, preferred_element_type=jnp.float32
        )
        grad_up = jnp.einsum(
            "nd,nf->df", normed_two, grad_up_pre, preferred_element_type=jnp.float32
        )
        grad_normed_two = jnp.einsum(
            "nf,df->nd", grad_gate_pre, mat_gate, preferred_element_type=jnp.float32
        ) + jnp.einsum("nf,df->nd", grad_up_pre, mat_up, preferred_element_type=jnp.float32)
        scaled_two = middle * rms_two
        grad_gain_two = jnp.sum(grad_normed_two * scaled_two, axis=0)
        weighted_two = grad_normed_two * gain_two.astype(jnp.float32)
        grad_middle = grad_in + rms_two * (
            weighted_two - scaled_two * jnp.mean(weighted_two * scaled_two, axis=-1, keepdims=True)
        )
        grad_attn = grad_middle.astype(jnp.bfloat16)
        grad_out_mat = jnp.einsum(
            "nd,ne->de", attn_low, grad_attn, preferred_element_type=jnp.float32
        )
        grad_attended = jnp.einsum(
            "ne,de->nd", grad_attn, mat_out, preferred_element_type=jnp.float32
        ).astype(jnp.bfloat16)
        grad_heads = heads_of(grad_attended)
        delta_rows = jnp.transpose(
            jnp.sum(grad_heads.astype(jnp.float32) * attended, axis=-1), (0, 2, 1)
        )
        grad_query, grad_key, grad_value = attend_back(
            query_rot,
            key_rot,
            heads_of(values),
            query_rot.reshape(seq_count, stretch_len, model_width),
            key_rot.reshape(seq_count, stretch_len, model_width),
            values.reshape(seq_count, stretch_len, model_width),
            grad_heads,
            grad_attended.reshape(seq_count, stretch_len, model_width),
            log_total,
            delta_rows,
            lengths,
            positions,
            score_scale,
        )
        grad_query_raw = rotate(grad_query, cosine, -sine_table).reshape(-1, model_width)
        grad_key_raw = rotate(grad_key, cosine, -sine_table).reshape(-1, model_width)
        grad_value_flat = grad_value.reshape(-1, model_width)
        if first_grad is None:
            grad_value_raw = 0.5 * grad_value_flat
            passed = 0.5 * grad_value_flat
        else:
            grad_value_raw = grad_value_flat + first_grad
            passed = None
        grad_proj = jnp.concatenate([grad_query_raw, grad_key_raw, grad_value_raw], axis=-1).astype(
            jnp.bfloat16
        )
        grad_qkv = jnp.einsum("nd,ne->de", normed, grad_proj, preferred_element_type=jnp.float32)
        grad_normed = jnp.einsum(
            "ne,de->nd", grad_proj, mat_qkv, preferred_element_type=jnp.float32
        )
        scaled_one = inputs * rms_one
        grad_gain_one = jnp.sum(grad_normed * scaled_one, axis=0)
        weighted_one = grad_normed * gain_one.astype(jnp.float32)
        grad_inputs = grad_middle + rms_one * (
            weighted_one - scaled_one * jnp.mean(weighted_one * scaled_one, axis=-1, keepdims=True)
        )
        return (
            grad_inputs,
            (grad_gain_one, grad_qkv, grad_out_mat, grad_gain_two, grad_gate, grad_up, grad_down),
            passed,
        )

    def reduce_layer(grads):
        return (
            lax.psum_scatter(grads[0], ("grp", "seq"), scatter_dimension=0, tiled=True),
            lax.psum_scatter(grads[1], ("grp", "seq"), scatter_dimension=0, tiled=True),
            lax.psum_scatter(grads[2], ("grp", "seq"), scatter_dimension=0, tiled=True),
            lax.psum_scatter(grads[3], ("grp", "seq"), scatter_dimension=0, tiled=True),
            lax.psum_scatter(grads[4], ("grp", "seq"), scatter_dimension=0, tiled=True),
            lax.psum_scatter(grads[5], ("grp", "seq"), scatter_dimension=0, tiled=True),
            lax.psum_scatter(grads[6], ("grp", "seq"), scatter_dimension=0, tiled=True),
        )

    state_zero = tokens.astype(jnp.float32).reshape(-1, model_width)
    params_one = gather_layer(0)
    state_one, first_value, kept_one = forward_layer(state_zero, params_one, None)
    params_two = gather_layer(1)
    state_two, unused_value, kept_two = forward_layer(state_one, params_two, first_value)
    layer_out = state_two.astype(jnp.bfloat16).reshape(seq_count, stretch_len, model_width)
    valid_mask = (positions[None, :] < lengths[:, None]).astype(jnp.float32)
    grad_state = (cotangent.astype(jnp.float32) * valid_mask[:, :, None]).reshape(-1, model_width)
    params_two = gather_again(1)
    grad_mid, grads_two, passed = backward_layer(grad_state, params_two, kept_two, None)
    shards_two = reduce_layer(grads_two)
    params_one = gather_again(0)
    grad_inputs, grads_one, unused_grad = backward_layer(grad_mid, params_one, kept_one, passed)
    shards_one = reduce_layer(grads_one)
    stacked = tuple((jnp.stack([shards_one[member], shards_two[member]]) for member in range(7)))
    input_grad = grad_inputs.reshape(seq_count, stretch_len, model_width)
    return (
        layer_out,
        input_grad,
        stacked[0],
        stacked[1],
        stacked[2],
        stacked[3],
        stacked[4],
        stacked[5],
        stacked[6],
    )


def solution(mesh):
    return jax.shard_map(
        body,
        mesh=mesh,
        in_specs=(
            P("grp", "seq", None),
            P("grp", None),
            P(None, ("grp", "seq")),
            P(None, ("grp", "seq"), None),
            P(None, ("grp", "seq"), None),
            P(None, ("grp", "seq")),
            P(None, ("grp", "seq"), None),
            P(None, ("grp", "seq"), None),
            P(None, ("grp", "seq"), None),
            P("grp", "seq", None),
        ),
        out_specs=(
            P("grp", "seq", None),
            P("grp", "seq", None),
            P(None, ("grp", "seq")),
            P(None, ("grp", "seq"), None),
            P(None, ("grp", "seq"), None),
            P(None, ("grp", "seq")),
            P(None, ("grp", "seq"), None),
            P(None, ("grp", "seq"), None),
            P(None, ("grp", "seq"), None),
        ),
        check_vma=False,
    )
```

profile of v0, /device:TPU:0, one launch (start us, length us, event | category | flops | bytes accessed | tf_op | source)
XLA Modules:
  0.0 3875.8 jit_solution(11259253353369076056)
XLA Ops:
  11.4 42.9 %all-reduce.9 = (bf16[1024]{0:T(1024)(128)(2,1)S(1)}, bf16[1024]{0:T(1024)(128)(2,1)S(1)}, bf16[1024]{0:T(1024)(128)(2,1)S(1)}, bf16[1024]{0:T(1024)(128)(2,1)}) all-reduce(bf16[1024]{0:T(1024)(128)(2,1)S(1)} %dynamic-update-slice, bf16[1024]{0:T(1024)(128)(2,1)S(1)} %dynamic-update-slice.1, ...), channel_id=2, replica_groups=mesh['grp'=4,'seq'=8] {'grp','seq'}, use_global_device_ids=true, to_apply=%add | all-reduce | flops 4096 | bytes 16384
  57.9 26.1 all-gather.49.cloned.1.call-done
  151.9 65.1 %all-gather.35.cloned.1.call-done = bf16[2,2048,1024]{2,1,0:T(8,128)(2,1)} async-done(((bf16[2,256,1024]{2,1,0:T(8,128)(2,1)}), bf16[2,2048,1024]{2,1,0:T(8,128)(2,1)}) %all-gather.35.cloned.1.call-update) | async-done | bytes 8388624 | tf_op jit(solution)/shard_map/all_gather | solution.py:41
  225.3 117.9 %all-gather.33.cloned.1.call-done = bf16[2,2048,1024]{1,2,0:T(8,128)(2,1)} async-done(((bf16[2,256,1024]{1,2,0:T(8,128)(2,1)}), bf16[2,2048,1024]{1,2,0:T(8,128)(2,1)}) %all-gather.33.cloned.1.call-update) | async-done | bytes 8388624 | tf_op jit(solution)/shard_map/all_gather | solution.py:40
  386.1 18.0 fusion.5
  432.8 15.9 fusion.3
  448.7 16.4 fusion.1
  465.1 17.5 fusion.358
  496.8 42.4 %all-gather.55.cloned.1.call-done = bf16[1,1024,2816]{2,1,0:T(8,128)(2,1)} async-done(((bf16[1,32,2816]{2,1,0:T(8,128)(2,1)}), bf16[1,1024,2816]{2,1,0:T(8,128)(2,1)}) %all-gather.55.cloned.1.call-update) | async-done | bytes 5767184 | tf_op jit(solution)/shard_map/all_gather | solution.py:191
  548.4 60.0 %all-gather.57.cloned.1.call-done = bf16[1,2816,1024]{2,1,0:T(8,128)(2,1)} async-done(((bf16[1,88,1024]{2,1,0:T(8,128)(2,1)}), bf16[1,2816,1024]{2,1,0:T(8,128)(2,1)}) %all-gather.57.cloned.1.call-update) | async-done | bytes 5767184 | tf_op jit(solution)/shard_map/all_gather | solution.py:192
  616.4 64.1 %all-gather.59.cloned.1.call-done = bf16[1,1024,3072]{2,1,0:T(8,128)(2,1)} async-done(((bf16[1,32,3072]{2,1,0:T(8,128)(2,1)}), bf16[1,1024,3072]{2,1,0:T(8,128)(2,1)}) %all-gather.59.cloned.1.call-update) | async-done | bytes 6291472 | tf_op jit(solution)/shard_map/all_gather | solution.py:187
  757.9 117.5 %all-gather.37.cloned.1.call-done = bf16[2,2048,1024]{1,2,0:T(8,128)(2,1)} async-done(((bf16[2,256,1024]{1,2,0:T(8,128)(2,1)}), bf16[2,2048,1024]{1,2,0:T(8,128)(2,1)}) %all-gather.37.cloned.1.call-update) | async-done | bytes 8388624 | tf_op jit(solution)/shard_map/all_gather | solution.py:40
  923.0 77.7 %all-gather.39.cloned.1.call-done = bf16[2,2048,1024]{2,1,0:T(8,128)(2,1)} async-done(((bf16[2,256,1024]{2,1,0:T(8,128)(2,1)}), bf16[2,2048,1024]{2,1,0:T(8,128)(2,1)}) %all-gather.39.cloned.1.call-update) | async-done | bytes 8388624 | tf_op jit(solution)/shard_map/all_gather | solution.py:41
  1040.6 18.3 fusion.13
  1073.2 17.9 fusion.9
  1091.2 16.9 fusion.359
  1135.9 60.4 %all-gather.63.cloned.1.call-done = bf16[1,1024,2816]{2,1,0:T(8,128)(2,1)} async-done(((bf16[1,32,2816]{2,1,0:T(8,128)(2,1)}), bf16[1,1024,2816]{2,1,0:T(8,128)(2,1)}) %all-gather.63.cloned.1.call-update) | async-done | bytes 5767184 | tf_op jit(solution)/shard_map/all_gather | solution.py:190
  1237.8 33.8 all_gather.117
  1271.6 36.5 all_gather.115
  1398.2 57.4 %all-gather.43.cloned.1.call-done = bf16[2,2048,1024]{2,1,0:T(8,128)(2,1)} async-done(((bf16[2,256,1024]{2,1,0:T(8,128)(2,1)}), bf16[2,2048,1024]{2,1,0:T(8,128)(2,1)}) %all-gather.43.cloned.1.call-update) | async-done | bytes 8388624 | tf_op jit(solution)/shard_map/all_gather | solution.py:127
  1690.0 32.1 all_gather.119
  1764.8 31.1 all_gather.121
  2008.1 32.2 reduce-scatter.15.cloned.1.call-done
  2051.1 44.7 %all-reduce.8 = (f32[1024]{0:T(1024)S(1)}, f32[1024]{0:T(1024)S(1)}, f32[1024]{0:T(1024)S(1)}, f32[1024]{0:T(1024)S(1)}) all-reduce(f32[1024]{0:T(1024)S(1)} %copy-done.198, f32[1024]{0:T(1024)S(1)} %get-tuple-element.15, f32[1024]{0:T(1024)S(1)} %copy-done.197, ...), channel_id=17, replica_groups=mesh['grp'=4,'seq'=8] {'grp','seq'}, use_global_device_ids=true, to_apply=%region_29.30.clone | all-reduce | flops 4096 | bytes 32768
  2100.7 190.6 %reduce-scatter.29.cloned.1.call-done = f32[88,1024]{1,0:T(8,128)} async-done(((f32[2816,1024]{1,0:T(8,128)}), f32[88,1024]{1,0:T(8,128)}) %reduce-scatter.29.cloned.1.call-update) | async-done | bytes 360464 | tf_op jit(solution)/shard_map/reduce_scatter | solution.py:361
  2291.3 250.9 %reduce-scatter.27.cloned.1.call-done = f32[88,1024]{1,0:T(8,128)} async-done(((f32[2816,1024]{1,0:T(8,128)}), f32[88,1024]{1,0:T(8,128)}) %reduce-scatter.27.cloned.1.call-update) | async-done | bytes 360464 | tf_op jit(solution)/shard_map/reduce_scatter | solution.py:361
  2544.3 248.7 %reduce-scatter.21.cloned.1.call-done = f32[32,2816]{1,0:T(8,128)} async-done(((f32[1024,2816]{1,0:T(8,128)}), f32[32,2816]{1,0:T(8,128)}) %reduce-scatter.21.cloned.1.call-update) | async-done | bytes 360464 | tf_op jit(solution)/shard_map/reduce_scatter | solution.py:359
  2793.0 251.6 %reduce-scatter.19.cloned.1.call-done = f32[32,2816]{1,0:T(8,128)} async-done(((f32[1024,2816]{1,0:T(8,128)}), f32[32,2816]{1,0:T(8,128)}) %reduce-scatter.19.cloned.1.call-update) | async-done | bytes 360464 | tf_op jit(solution)/shard_map/reduce_scatter | solution.py:359
  3046.5 248.7 %reduce-scatter.25.cloned.1.call-done = f32[32,2816]{1,0:T(8,128)} async-done(((f32[1024,2816]{1,0:T(8,128)}), f32[32,2816]{1,0:T(8,128)}) %reduce-scatter.25.cloned.1.call-update) | async-done | bytes 360464 | tf_op jit(solution)/shard_map/reduce_scatter | solution.py:360
  3295.3 249.2 %reduce-scatter.23.cloned.1.call-done = f32[32,2816]{1,0:T(8,128)} async-done(((f32[1024,2816]{1,0:T(8,128)}), f32[32,2816]{1,0:T(8,128)}) %reduce-scatter.23.cloned.1.call-update) | async-done | bytes 360464 | tf_op jit(solution)/shard_map/reduce_scatter | solution.py:360
  3546.5 158.7 %reduce-scatter.13.cloned.1.call-done = f32[32,3072]{1,0:T(8,128)} async-done(((f32[1024,3072]{1,0:T(8,128)}), f32[32,3072]{1,0:T(8,128)}) %reduce-scatter.13.cloned.1.call-update) | async-done | bytes 393232 | tf_op jit(solution)/shard_map/reduce_scatter | solution.py:356
  3705.2 161.5 %reduce-scatter.11.cloned.1.call-done = f32[32,3072]{1,0:T(8,128)} async-done(((f32[1024,3072]{1,0:T(8,128)}), f32[32,3072]{1,0:T(8,128)}) %reduce-scatter.11.cloned.1.call-update) | async-done | bytes 393232 | tf_op jit(solution)/shard_map/reduce_scatter | solution.py:356
  (776 shorter events, 1035.7 us)
Async XLA Ops:
  7.2 76.9 %all-gather.49.cloned.1.call-start = ((), (), s32[]{:S(2)}) async-start(), calls=%async_computation.28 | async-start | bytes 6488064 | tf_op jit(solution)/shard_map/all_gather | solution.py:187
  9.0 207.9 %all-gather.35.cloned.1.call-start = ((), (), s32[]{:S(2)}) async-start(), calls=%async_computation.11 | async-start | bytes 9437184 | tf_op jit(solution)/shard_map/all_gather | solution.py:41
  93.4 249.8 %all-gather.33.cloned.1.call-start = ((), (), s32[]{:S(2)}) async-start(), calls=%async_computation.10 | async-start | bytes 9437184 | tf_op jit(solution)/shard_map/all_gather | solution.py:40
  141.3 228.9 %copy-start.8 = (bf16[2,256,16,32]{1,3,2,0:T(8,128)(2,1)}, bf16[2,256,16,32]{1,3,2,0:T(8,128)(2,1)S(1)}, u32[]{:S(2)}) copy-start(bf16[2,256,16,32]{1,3,2,0:T(8,128)(2,1)S(1)} %get-tuple-element.139) | copy-start | bytes 1572868
  141.3 228.9 %copy-start.10 = (bf16[2,256,16,32]{1,3,2,0:T(8,128)(2,1)}, bf16[2,256,16,32]{1,3,2,0:T(8,128)(2,1)S(1)}, u32[]{:S(2)}) copy-start(bf16[2,256,16,32]{1,3,2,0:T(8,128)(2,1)S(1)} %get-tuple-element.140) | copy-start | bytes 1572868
  143.2 341.7 %all-gather.51.cloned.1.call-start = ((), (), s32[]{:S(2)}) async-start(), calls=%async_computation.29 | async-start | bytes 2162688 | tf_op jit(solution)/shard_map/all_gather | solution.py:188
  143.9 344.6 %all-gather.53.cloned.1.call-start = ((), (), s32[]{:S(2)}) async-start(), calls=%async_computation.30 | async-start | bytes 5947392 | tf_op jit(solution)/shard_map/all_gather | solution.py:190
  144.8 394.4 %all-gather.55.cloned.1.call-start = ((), (), s32[]{:S(2)}) async-start(), calls=%async_computation.31 | async-start | bytes 5947392 | tf_op jit(solution)/shard_map/all_gather | solution.py:191
  145.7 462.7 %all-gather.57.cloned.1.call-start = ((), (), s32[]{:S(2)}) async-start(), calls=%async_computation.32 | async-start | bytes 5947392 | tf_op jit(solution)/shard_map/all_gather | solution.py:192
  146.5 533.9 %all-gather.59.cloned.1.call-start = ((), (), s32[]{:S(2)}) async-start(), calls=%async_computation.33 | async-start | bytes 6488064 | tf_op jit(solution)/shard_map/all_gather | solution.py:187
  147.3 601.9 %all-gather.67.cloned.1.call-start = ((), (), s32[]{:S(2)}) async-start(), calls=%async_computation.37 | async-start | bytes 5947392 | tf_op jit(solution)/shard_map/all_gather | solution.py:192
  148.0 727.4 %all-gather.37.cloned.1.call-start = ((), (), s32[]{:S(2)}) async-start(), calls=%async_computation.12 | async-start | bytes 9437184 | tf_op jit(solution)/shard_map/all_gather | solution.py:40
  149.1 339.1 %copy-start.174 = (f32[1024]{0:T(1024)}, f32[1024]{0:T(1024)S(1)}, u32[]{:S(2)}) copy-start(f32[1024]{0:T(1024)S(1)} %convert_element_type.268) | copy-start | bytes 12292
  149.1 531.3 %copy-start.193 = (f32[1024]{0:T(1024)}, f32[1024]{0:T(1024)S(1)}, u32[]{:S(2)}) copy-start(f32[1024]{0:T(1024)S(1)} %convert_element_type.269) | copy-start | bytes 12292
  735.1 265.6 %all-gather.39.cloned.1.call-start = ((), (), s32[]{:S(2)}) async-start(), calls=%async_computation.13 | async-start | bytes 9437184 | tf_op jit(solution)/shard_map/all_gather | solution.py:41
  735.9 374.6 %all-gather.61.cloned.1.call-start = ((), (), s32[]{:S(2)}) async-start(), calls=%async_computation.34 | async-start | bytes 2162688 | tf_op jit(solution)/shard_map/all_gather | solution.py:188
  736.4 390.9 %all-gather.65.cloned.1.call-start = ((), (), s32[]{:S(2)}) async-start(), calls=%async_computation.36 | async-start | bytes 5947392 | tf_op jit(solution)/shard_map/all_gather | solution.py:191
  737.2 459.2 %all-gather.63.cloned.1.call-start = ((), (), s32[]{:S(2)}) async-start(), calls=%async_computation.35 | async-start | bytes 5947392 | tf_op jit(solution)/shard_map/all_gather | solution.py:190
  737.8 607.7 %all-gather.41.cloned.1.call-start = ((), (), s32[]{:S(2)}) async-start(), calls=%async_computation.14 | async-start | bytes 9437184 | tf_op jit(solution)/shard_map/all_gather | solution.py:126
  757.9 697.7 %all-gather.43.cloned.1.call-start = ((), (), s32[]{:S(2)}) async-start(), calls=%async_computation.15 | async-start | bytes 9437184 | tf_op jit(solution)/shard_map/all_gather | solution.py:127
  1221.0 501.7 %all-gather.45.cloned.1.call-start = ((), (), s32[]{:S(2)}) async-start(), calls=%async_computation.16 | async-start | bytes 9437184 | tf_op jit(solution)/shard_map/all_gather | solution.py:126
  1223.9 633.9 %all-gather.47.cloned.1.call-start = ((), (), s32[]{:S(2)}) async-start(), calls=%async_computation.17 | async-start | bytes 9437184 | tf_op jit(solution)/shard_map/all_gather | solution.py:127
  1623.3 384.8 %reduce-scatter.17.cloned.1.call-start = ((), (), s32[]{:S(2)}) async-start(), calls=%async_computation.21 | async-start | bytes 4325376 | tf_op jit(solution)/shard_map/reduce_scatter | solution.py:357
  1626.6 413.7 %reduce-scatter.15.cloned.1.call-start = ((), (), s32[]{:S(2)}) async-start(), calls=%async_computation.20 | async-start | bytes 4325376 | tf_op jit(solution)/shard_map/reduce_scatter | solution.py:357
  1631.6 659.7 %reduce-scatter.29.cloned.1.call-start = ((), (), s32[]{:S(2)}) async-start(), calls=%async_computation.27 | async-start | bytes 11894784 | tf_op jit(solution)/shard_map/reduce_scatter | solution.py:361
  1640.8 901.4 %reduce-scatter.27.cloned.1.call-start = ((), (), s32[]{:S(2)}) async-start(), calls=%async_computation.26 | async-start | bytes 11894784 | tf_op jit(solution)/shard_map/reduce_scatter | solution.py:361
  1650.2 1142.8 %reduce-scatter.21.cloned.1.call-start = ((), (), s32[]{:S(2)}) async-start(), calls=%async_computation.23 | async-start | bytes 11894784 | tf_op jit(solution)/shard_map/reduce_scatter | solution.py:359
  1659.7 1384.9 %reduce-scatter.19.cloned.1.call-start = ((), (), s32[]{:S(2)}) async-start(), calls=%async_computation.22 | async-start | bytes 11894784 | tf_op jit(solution)/shard_map/reduce_scatter | solution.py:359
  1668.5 1626.7 %reduce-scatter.25.cloned.1.call-start = ((), (), s32[]{:S(2)}) async-start(), calls=%async_computation.25 | async-start | bytes 11894784 | tf_op jit(solution)/shard_map/reduce_scatter | solution.py:360
  1676.9 1867.6 %reduce-scatter.23.cloned.1.call-start = ((), (), s32[]{:S(2)}) async-start(), calls=%async_computation.24 | async-start | bytes 11894784 | tf_op jit(solution)/shard_map/reduce_scatter | solution.py:360
  1684.9 2020.3 %reduce-scatter.13.cloned.1.call-start = ((), (), s32[]{:S(2)}) async-start(), calls=%async_computation.19 | async-start | bytes 12976128 | tf_op jit(solution)/shard_map/reduce_scatter | solution.py:356
  1818.0 2048.7 %reduce-scatter.11.cloned.1.call-start = ((), (), s32[]{:S(2)}) async-start(), calls=%async_computation.18 | async-start | bytes 12976128 | tf_op jit(solution)/shard_map/reduce_scatter | solution.py:356
  (228 other events, 3264.1 us)
Sparse Core Ops, SparseCore 0:
  11.6 72.4 all-gather.48
  93.5 123.3 all-gather.34
  219.6 123.5 all-gather.32
  346.0 54.7 all-gather.50
  404.1 66.0 all-gather.52
  473.0 66.2 all-gather.54
  542.1 66.1 all-gather.56
  611.9 68.4 all-gather.58
  683.3 65.7 all-gather.66
  751.0 124.3 all-gather.36
  877.6 123.0 all-gather.38
  1003.6 54.6 all-gather.60
  1061.2 66.1 all-gather.64
  1130.1 66.1 all-gather.62
  1198.2 132.1 all-gather.40
  1332.5 123.0 all-gather.42
  1457.5 123.5 all-gather.44
  1623.4 128.3 all-gather.46
  1754.1 142.1 reduce-scatter.16
  1898.4 141.8 reduce-scatter.14
  2042.6 248.6 reduce-scatter.28
  2293.6 248.5 reduce-scatter.26
  2544.6 248.3 reduce-scatter.20
  2795.2 249.3 reduce-scatter.18
  3046.9 248.3 reduce-scatter.24
  3297.5 246.9 reduce-scatter.22
  3550.3 154.8 reduce-scatter.12
  3712.2 154.4 reduce-scatter.10
where the time goes:
time: 3880 us
  waiting for transfers between devices  2510 us (65%)
  matrix products  770 us (20%)
  local copies, waits for them, and re-layouts  249 us (6%)
  blocking collectives  221 us (6%)
  other arithmetic  110 us (3%)
    reduce_scatter x2, waiting for transfers between devices, reduce_layer(): lax.psum_scatter(grads[4], ('grp', 'seq'), scatter_dimension=0, tiled=True)  500 us
    reduce_scatter x2, waiting for transfers between devices, reduce_layer(): lax.psum_scatter(grads[5], ('grp', 'seq'), scatter_dimension=0, tiled=True)  498 us
    reduce_scatter x2, waiting for transfers between devices, reduce_layer(): lax.psum_scatter(grads[6], ('grp', 'seq'), scatter_dimension=0, tiled=True)  441 us
    reduce_scatter x2, waiting for transfers between devices, reduce_layer(): lax.psum_scatter(grads[1], ('grp', 'seq'), scatter_dimension=0, tiled=True)  320 us
    all_gather x2, waiting for transfers between devices, attend(): k_piece = lax.all_gather(k_flat, 'seq', axis=1, tiled=True)  235 us
    all_gather x2, waiting for transfers between devices, attend(): v_piece = lax.all_gather(v_flat, 'seq', axis=1, tiled=True)  143 us
    dot_general x8, matrix products, attend(): jnp.einsum('shqk,skhd->sqhd', probs, v_block, precision=PRECISE, preferre...  135 us
    dot_general x8, matrix products, attend_back(): jnp.einsum('shqk,sqhd->skhd', probs, g_block.astype(jnp.float32), precisi...  111 us
  transfers between devices with their start and end apart: 28, of which 21 were waited for; matrix products, arithmetic and copies ran while one was open for 28% of the time, Pallas kernels for 0%

commit v1 on v0

--- a/solution.py
+++ b/solution.py
@@ -1,14 +1,527 @@
 import jax
 import jax.numpy as jnp
 from jax import lax
+from jax.experimental import pallas as pl
+from jax.experimental.pallas import tpu as pltpu
+from jax.sharding import Mesh
 from jax.sharding import PartitionSpec as P
 
 HEADS = 16
-
-
 EPSILON = 1e-06
 NEGATIVE = -1e30
 PRECISE = lax.Precision.HIGHEST
+BF = jnp.bfloat16
+F32 = jnp.float32
+ALL = ("y", "c", "z", "x")
+PLANE = ("c", "y", "x")
+VMEM_BYTES = 50 * 1024 * 1024
+ANY = pl.BlockSpec(memory_space=pl.ANY)
+SMEM = pl.BlockSpec(memory_space=pltpu.SMEM)
+NT = (((1,), (1,)), ((), ()))
+TN = (((0,), (0,)), ((), ()))
+
+
+def params(**more):
+    return pltpu.CompilerParams(vmem_limit_bytes=VMEM_BYTES, **more)
+
+
+def assemble(where, pieces, relative, with_x):
+    rows, cols = pieces[0].shape[1:]
+    count = len(pieces)
+    lead = (2, 2, 4, 2) if with_x else (2, 2, 4)
+
+    def kernel(where_ref, *rest):
+        ins, out, held, sems = rest[:count], rest[count], rest[count + 1], rest[count + 2]
+        y, c, z, x = (where_ref[n] for n in range(4))
+        copies, puts = [], []
+        for n in range(count):
+            dy, dc, dx = relative[n]
+            for dz in range(4):
+                slot = (y ^ dy, c ^ dc, z ^ dz) + ((x ^ dx,) if with_x else ())
+                spot = held.at[n, dz]
+                copies.append(pltpu.make_async_copy(ins[n].at[dz], spot, sems.at[0, n, dz]))
+                puts.append(pltpu.make_async_copy(spot, out.at[slot], sems.at[1, n, dz]))
+        for copy in copies:
+            copy.start()
+        for copy, put in zip(copies, puts):
+            copy.wait()
+            put.start()
+        for put in puts:
+            put.wait()
+
+    out = pl.pallas_call(
+        kernel,
+        in_specs=[SMEM] + [ANY] * count,
+        out_specs=ANY,
+        out_shape=jax.ShapeDtypeStruct(lead + (rows, cols), pieces[0].dtype),
+        scratch_shapes=[
+            pltpu.VMEM((count, 4, rows, cols), pieces[0].dtype),
+            pltpu.SemaphoreType.DMA((2, count, 4)),
+        ],
+        compiler_params=params(),
+        name="assemble",
+    )(where, *pieces)
+    return out.reshape(-1, cols)
+
+
+def swap(value, axis):
+    return lax.ppermute(value, axis, [(0, 1), (1, 0)])
+
+
+def hop(value, offset):
+    return lax.ppermute(value, "z", [(i, i ^ offset) for i in range(4)])
+
+
+def gather_z_first(where, shard, first, second):
+    stack = jnp.stack([shard] + [hop(shard, k) for k in (1, 2, 3)])
+    near = swap(stack, first)
+    ring = [((0, 0), stack), ((1, 0), near)]
+    ring += [((0, 1), swap(stack, second)), ((1, 1), swap(near, second))]
+    pieces, relative = [], []
+    for (one, two), piece in ring:
+        moved = {first: one, second: two}
+        for dc, held in ((0, piece), (1, swap(piece, "c"))):
+            pieces.append(held)
+            relative.append((moved["y"], dc, moved["x"]))
+    return assemble(where, pieces, relative, True)
+
+
+def gather_x_first(where, shard):
+    near = swap(shard, "x")
+    even = lax.axis_index("x") == 0
+    pair = jnp.concatenate([jnp.where(even, shard, near), jnp.where(even, near, shard)])
+    stack = jnp.stack([pair] + [hop(pair, k) for k in (1, 2, 3)])
+    pieces, relative = [], []
+    for dy, piece in ((0, stack), (1, swap(stack, "y"))):
+        for dc, held in ((0, piece), (1, swap(piece, "c"))):
+            pieces.append(held)
+            relative.append((dy, dc, 0))
+    return assemble(where, pieces, relative, False)
+
+
+def reduce_rows(partial, order):
+    names = ["y", "z", "x"]
+    for step, axis in enumerate(order):
+        dim = names.index(axis)
+        names.pop(dim)
+        here = lax.axis_index(axis)
+        last = step == len(order) - 1
+
+        def block(slot):
+            return lax.dynamic_index_in_dim(partial, slot, dim, keepdims=False)
+
+        if axis == "z":
+            moved = [hop(block(here ^ k), k) for k in (1, 2, 3)]
+        else:
+            moved = [swap(block(1 - here), axis)]
+        total = block(here).astype(F32)
+        for part in moved:
+            total = total + part.astype(F32)
+        partial = total if last else total.astype(BF)
+    return partial
+
+
+def turn(field, cosine, signed_sine):
+    lane = lax.broadcasted_iota(jnp.int32, field.shape, 1)
+    other = jnp.where(
+        lane % 64 < 32, pltpu.roll(field, 96, axis=1), pltpu.roll(field, 32, axis=1)
+    )
+    return field * cosine + other * signed_sine
+
+
+def project_qkv(normed, w_qk, w_vo, cosine, signed_sine, first_value):
+    rows, width = normed.shape
+
+    def kernel(normed_ref, w_qk_ref, w_vo_ref, cos_ref, sin_ref, *rest):
+        out_ref = rest[-1]
+        step = pl.program_id(0)
+
+        @pl.when(step < 8)
+        def _():
+            product = jnp.dot(normed_ref[...], w_qk_ref[...], preferred_element_type=F32)
+            for half in range(2):
+                field = product[:, 128 * half : 128 * half + 128]
+                out_ref[half, 0] = turn(field, cos_ref[...], sin_ref[...]).astype(BF)
+
+        @pl.when(step >= 8)
+        def _():
+            product = jnp.dot(normed_ref[...], w_vo_ref[...], preferred_element_type=F32)
+            for half in range(2):
+                field = product[:, 128 * half : 128 * half + 128]
+                if first_value is not None:
+                    field = 0.5 * field + 0.5 * rest[0][half, 0].astype(F32)
+                out_ref[half, 0] = field.astype(BF)
+
+    whole = lambda step: (0, 0)
+    in_specs = [
+        pl.BlockSpec((rows, width), whole),
+        pl.BlockSpec((width, 256), lambda step: (0, jnp.minimum(step, 7))),
+        pl.BlockSpec((width, 256), lambda step: (0, jnp.maximum(step - 8, 0))),
+        pl.BlockSpec((rows, 128), whole),
+        pl.BlockSpec((rows, 128), whole),
+    ]
+    operands = [normed, w_qk, w_vo, cosine, signed_sine]
+    if first_value is not None:
+        in_specs.append(
+            pl.BlockSpec((2, 1, rows, 128), lambda step: (jnp.maximum(step - 8, 0), 2, 0, 0))
+        )
+        operands.append(first_value)
+    return pl.pallas_call(
+        kernel,
+        grid=(12,),
+        in_specs=in_specs,
+        out_specs=pl.BlockSpec((2, 1, rows, 128), lambda step: (step % 4, step // 4, 0, 0)),
+        out_shape=jax.ShapeDtypeStruct((8, 3, rows, 128), BF),
+        compiler_params=params(dimension_semantics=("arbitrary",)),
+        name="project_qkv",
+    )(*operands)
+
+
+def weight_grad(left_own, left_near, right_own, right_near, tile):
+    rows, depth = left_own.shape
+    cols = right_own.shape[1]
+
+    def kernel(lo, ln, ro, rn, out_ref, flipped):
+        @pl.when(pl.program_id(0) == 0)
+        def _():
+            flipped[:, :rows] = lo[...].T
+            flipped[:, rows:] = ln[...].T
+
+        total = jnp.dot(flipped[:, :rows], ro[...], preferred_element_type=F32)
+        total += jnp.dot(flipped[:, rows:], rn[...], preferred_element_type=F32)
+        out_ref[...] = total.astype(BF)
+
+    whole = pl.BlockSpec((rows, depth), lambda n: (0, 0))
+    block = pl.BlockSpec((rows, tile), lambda n: (0, n))
+    return pl.pallas_call(
+        kernel,
+        grid=(cols // tile,),
+        in_specs=[whole, whole, block, block],
+        out_specs=pl.BlockSpec((depth, tile), lambda n: (0, n)),
+        out_shape=jax.ShapeDtypeStruct((depth, cols), BF),
+        scratch_shapes=[pltpu.VMEM((depth, 2 * rows), BF)],
+        compiler_params=params(dimension_semantics=("arbitrary",)),
+        name="weight_grad",
+    )(left_own, left_near, right_own, right_near)
+
+
+def rows_of(block):
+    return block.reshape(-1, 128)
+
+
+def attend(lengths, pieces):
+    tile = 256
+    slots = pieces.shape[3] * 128
+    tiles = slots // tile
+    per = tile // 128
+
+    def kernel(len_ref, piece_ref, out_ref, lse_ref, held, flipped, logit, sems):
+        seq, step = pl.program_id(0), pl.program_id(1)
+
+        def load(which, device):
+            return pltpu.make_async_copy(
+                piece_ref.at[device, :, which],
+                held.at[:, which, :, device],
+                sems.at[which, device],
+            )
+
+        @pl.when((seq == 0) & (step == 0))
+        def _():
+            for which in range(2):
+                for device in range(8):
+                    load(which, device).start()
+            for device in range(8):
+                load(0, device).wait()
+
+        @pl.when((seq == 1) & (step == 0))
+        def _():
+            for device in range(8):
+                load(1, device).wait()
+
+        @pl.when(step == 0)
+        def _():
+            for block in range(tiles):
+                key = rows_of(held[1, seq, pl.ds(per * block, per)])
+                flipped[block] = key.T
+
+        used = len_ref[seq]
+        query = rows_of(held[0, seq, pl.ds(per * step, per)]) * BF(0.125)
+        lane = lax.broadcasted_iota(jnp.int32, (tile, 128), 1)
+        low = lane < 64
+        zero = jnp.zeros_like(query)
+        queries = [jnp.where(low, query, zero), jnp.where(low, zero, query)]
+
+        def score(block, tops, masked):
+            key_t = flipped[block]
+            result = []
+            for head in range(2):
+                field = jnp.dot(queries[head], key_t, preferred_element_type=F32)
+                if masked:
+                    query_pos = step * tile + lax.broadcasted_iota(jnp.int32, field.shape, 0)
+                    key_pos = block * tile + lax.broadcasted_iota(jnp.int32, field.shape, 1)
+                    seen = (key_pos <= query_pos) & (key_pos < used)
+                    field = jnp.where(seen, field, NEGATIVE)
+                logit[head, block] = field
+                top = jnp.maximum(field[:, :128], field[:, 128:])
+                result.append(jnp.maximum(tops[head], top))
+            return tuple(result)
+
+        full = jnp.minimum(step, used // tile)
+        end = jnp.minimum(step + 1, (used + tile - 1) // tile)
+        low_top = jnp.full((tile, 128), NEGATIVE, F32)
+        tops = lax.fori_loop(0, full, lambda b, s: score(b, s, False), (low_top, low_top))
+        tops = lax.fori_loop(full, end, lambda b, s: score(b, s, True), tops)
+        tops = [jnp.max(top, axis=1, keepdims=True) for top in tops]
+        wide = [jnp.broadcast_to(top, (tile, tile)) for top in tops]
+        one = jnp.ones_like(query)
+
+        def mix(block, sums):
+            value = rows_of(held[2, seq, pl.ds(per * block, per)])
+            values = [jnp.where(low, value, one), jnp.where(low, one, value)]
+            result = []
+            for head in range(2):
+                probs = jnp.exp(logit[head, block] - wide[head]).astype(BF)
+                result.append(
+                    sums[head] + jnp.dot(probs, values[head], preferred_element_type=F32)
+                )
+            return tuple(result)
+
+        nothing = jnp.zeros((tile, 128), F32)
+        sums = lax.fori_loop(0, end, mix, (nothing, nothing))
+        totals = [sums[0][:, 64:65], sums[1][:, 0:1]]
+        out = jnp.where(low, sums[0] / totals[0], sums[1] / totals[1])
+        out = out.astype(BF).reshape(per, 8, 16, 128)
+        for device in range(8):
+            out_ref[device, seq, pl.ds(per * step, per)] = out[:, device]
+        level = jnp.where(low, tops[0] + jnp.log(totals[0]), tops[1] + jnp.log(totals[1])).T
+        start = pl.multiple_of(step * tile, tile)
+        lse_ref[seq, 0:1, pl.ds(start, tile)] = level[0:1]
+        lse_ref[seq, 1:2, pl.ds(start, tile)] = level[64:65]
+
+    return pl.pallas_call(
+        kernel,
+        grid=(2, tiles),
+        in_specs=[SMEM, ANY],
+        out_specs=[
+            pl.BlockSpec((8, 2) + pieces.shape[3:], lambda s, i: (0, 0, 0, 0, 0)),
+            pl.BlockSpec((2, 8, slots), lambda s, i: (0, 0, 0)),
+        ],
+        out_shape=[
+            jax.ShapeDtypeStruct((8, 2) + pieces.shape[3:], BF),
+            jax.ShapeDtypeStruct((2, 8, slots), F32),
+        ],
+        scratch_shapes=[
+            pltpu.VMEM((3, 2, slots // 128, 8, 16, 128), BF),
+            pltpu.VMEM((tiles, 128, tile), BF),
+            pltpu.VMEM((2, tiles, tile, tile), F32),
+            pltpu.SemaphoreType.DMA((2, 8)),
+        ],
+        compiler_params=params(dimension_semantics=("arbitrary", "arbitrary")),
+        name="attend",
+    )(lengths, pieces)
+
+
+def attend_back(lengths, pieces, attended, grads, lse, cosine, signed_sine, passed):
+    tile = 256
+    slots = pieces.shape[3] * 128
+    tiles = slots // tile
+    per = tile // 128
+    upper = passed is None
+
+    def kernel(*refs):
+        len_ref, piece_ref, att_ref, grad_ref, lse_ref, cos_ref, sin_ref = refs[:7]
+        refs = refs[7:]
+        if upper:
+            passed_ref = None
+            out_ref, give_ref = refs[:2]
+            refs = refs[2:]
+        else:
+            passed_ref, out_ref = refs[:2]
+            give_ref = None
+            refs = refs[2:]
+        held, att, grad, delta, level, query_acc, key_acc, value_acc, sems = refs
+        seq, step = pl.program_id(0), pl.program_id(1)
+        used = len_ref[seq]
+
+        def loads(which):
+            copies = []
+            for device in range(8):
+                copies.append(
+                    pltpu.make_async_copy(
+                        piece_ref.at[device, :, which],
+                        held.at[:, which, :, device],
+                        sems.at[0, which, device],
+                    )
+                )
+                copies.append(
+                    pltpu.make_async_copy(
+                        att_ref.at[device, which],
+                        att.at[which, :, device],
+                        sems.at[1, which, device],
+                    )
+                )
+                copies.append(
+                    pltpu.make_async_copy(
+                        grad_ref.at[device, which],
+                        grad.at[which, :, device],
+                        sems.at[2, which, device],
+                    )
+                )
+            return copies
+
+        @pl.when((seq == 0) & (step == 0))
+        def _():
+            for which in range(2):
+                for copy in loads(which):
+                    copy.start()
+            for copy in loads(0):
+                copy.wait()
+
+        @pl.when((seq == 1) & (step == 0))
+        def _():
+            for copy in loads(1):
+                copy.wait()
+
+        @pl.when(step == 0)
+        def _():
+            query_acc[...] = jnp.zeros_like(query_acc)
+            line = lax.broadcasted_iota(jnp.int32, (8, 128), 0)
+            lane = lax.broadcasted_iota(jnp.int32, (8, 128), 1)
+            pick = jnp.where(line == lane // 64, 1.0, 0.0).astype(F32)
+            for block in range(tiles):
+                span = slice(tile * block, tile * block + tile)
+                product = rows_of(grad[seq, pl.ds(per * block, per)]).astype(F32) * rows_of(
+                    att[seq, pl.ds(per * block, per)]
+                ).astype(F32)
+                delta[:, span] = lax.dot_general(
+                    pick, product, NT, precision=PRECISE, preferred_element_type=F32
+                )
+            place = lax.broadcasted_iota(jnp.int32, (8, slots), 1)
+            level[...] = jnp.where(place < used, lse_ref[seq], -NEGATIVE)
+
+        key = rows_of(held[1, seq, pl.ds(per * step, per)])
+        value = rows_of(held[2, seq, pl.ds(per * step, per)])
+        lane = lax.broadcasted_iota(jnp.int32, (tile, 128), 1)
+        low = lane < 64
+
+        def head_part(field, head):
+            keep = low if head == 0 else jnp.logical_not(low)
+            return jnp.where(keep, field, jnp.zeros_like(field))
+
+        scaled = key * BF(0.125)
+        keys = [head_part(scaled, head) for head in range(2)]
+        values = [head_part(value, head) for head in range(2)]
+        key_acc[...] = jnp.zeros_like(key_acc)
+        value_acc[...] = jnp.zeros_like(value_acc)
+
+        def visit(block, masked):
+            query = rows_of(held[0, seq, pl.ds(per * block, per)])
+            grad_out = rows_of(grad[seq, pl.ds(per * block, per)])
+            start = pl.multiple_of(block * tile, tile)
+            spans = pl.ds(start, tile)
+            query_sum = jnp.zeros((tile, 128), F32)
+            key_sum = jnp.zeros((tile, 128), F32)
+            value_sum = jnp.zeros((tile, 128), F32)
+            for head in range(2):
+                logits = lax.dot_general(keys[head], query, NT, preferred_element_type=F32)
+                probs = jnp.exp(logits - level[head : head + 1, spans])
+                if masked:
+                    key_pos = lax.broadcasted_iota(jnp.int32, probs.shape, 0)
+                    query_pos = lax.broadcasted_iota(jnp.int32, probs.shape, 1)
+                    probs = jnp.where(key_pos <= query_pos, probs, 0.0)
+                grad_probs = lax.dot_general(
+                    values[head], grad_out, NT, preferred_element_type=F32
+                )
+                grad_logits = (probs * (grad_probs - delta[head : head + 1, spans])).astype(BF)
+                value_sum += jnp.dot(
+                    probs.astype(BF), head_part(grad_out, head), preferred_element_type=F32
+                )
+                key_sum += jnp.dot(
+                    grad_logits, head_part(query, head), preferred_element_type=F32
+                )
+                query_sum += lax.dot_general(
+                    grad_logits, keys[head], TN, preferred_element_type=F32
+                )
+            query_acc[spans, :] += query_sum
+            key_acc[...] += key_sum
+            value_acc[...] += value_sum
+
+        end = (used + tile - 1) // tile
+
+        @pl.when(step < end)
+        def _():
+            visit(step, True)
+
+            def body(block, carry):
+                visit(block, False)
+                return carry
+
+            lax.fori_loop(step + 1, end, body, 0)
+
+        def put(member, block, field):
+            field = field.astype(BF).reshape(per, 8, 16, 128)
+            for device in range(8):
+                out_ref[device, member, seq, pl.ds(per * block, per)] = field[:, device]
+
+        start = pl.multiple_of(step * tile, tile)
+        spans = pl.ds(start, tile)
+        key_grad = key_acc[...] * 0.125
+        put(1, step, turn(key_grad, cos_ref[spans, :], -sin_ref[spans, :]))
+        if upper:
+            half = 0.5 * value_acc[...]
+            give_ref[seq, spans, :] = half
+            put(2, step, half)
+        else:
+            put(2, step, value_acc[...] + passed_ref[seq, spans, :])
+
+        @pl.when(step == tiles - 1)
+        def _():
+            for block in range(tiles):
+                part = slice(tile * block, tile * block + tile)
+                put(0, block, turn(query_acc[part, :], cos_ref[part, :], -sin_ref[part, :]))
+
+    flat = lambda s, i: (0, 0)
+    cube = lambda s, i: (0, 0, 0)
+    in_specs = [
+        SMEM,
+        ANY,
+        ANY,
+        ANY,
+        pl.BlockSpec((2, 8, slots), cube),
+        pl.BlockSpec((slots, 128), flat),
+        pl.BlockSpec((slots, 128), flat),
+    ]
+    operands = [lengths, pieces, attended, grads, lse, cosine, signed_sine]
+    out_specs = [pl.BlockSpec(pieces.shape, lambda s, i: (0, 0, 0, 0, 0, 0))]
+    out_shape = [jax.ShapeDtypeStruct(pieces.shape, BF)]
+    carried = pl.BlockSpec((2, slots, 128), cube)
+    if upper:
+        out_specs.append(carried)
+        out_shape.append(jax.ShapeDtypeStruct((2, slots, 128), F32))
+    else:
+        in_specs.append(carried)
+        operands.append(passed)
+    outs = pl.pallas_call(
+        kernel,
+        grid=(2, tiles),
+        in_specs=in_specs,
+        out_specs=out_specs,
+        out_shape=out_shape,
+        scratch_shapes=[
+            pltpu.VMEM((3, 2, slots // 128, 8, 16, 128), BF),
+            pltpu.VMEM((2, slots // 128, 8, 16, 128), BF),
+            pltpu.VMEM((2, slots // 128, 8, 16, 128), BF),
+            pltpu.VMEM((8, slots), F32),
+            pltpu.VMEM((8, slots), F32),
+            pltpu.VMEM((slots, 128), F32),
+            pltpu.VMEM((tile, 128), F32),
+            pltpu.VMEM((tile, 128), F32),
+            pltpu.SemaphoreType.DMA((3, 2, 8)),
+        ],
+        compiler_params=params(dimension_semantics=("arbitrary", "arbitrary")),
+        name="attend_back",
+    )(*operands)
+    return outs if upper else (outs[0], None)
 
 
 def block_spans(total_rows):
@@ -34,7 +547,7 @@
     return (causal & inside)[:, None, :, :]
 
 
-def attend(q_heads, k_flat, v_flat, lengths, positions, score_scale):
+def attend_gathered(q_heads, k_flat, v_flat, lengths, positions, score_scale):
     seq_count, stretch_len, head_count, head_dim = q_heads.shape
     first_row = jnp.int32(0)
     k_piece = lax.all_gather(k_flat, "seq", axis=1, tiled=True)
@@ -72,7 +585,7 @@
     return (attended, running_max + jnp.log(row_total))
 
 
-def attend_back(
+def attend_back_gathered(
     q_heads,
     k_heads,
     v_heads,
@@ -217,7 +730,7 @@
             values = (0.5 * value_raw + 0.5 * first_value.astype(jnp.float32)).astype(jnp.bfloat16)
         query_rot = rotate(heads_of(query_raw), cosine, sine_table).astype(jnp.bfloat16)
         key_rot = rotate(heads_of(key_raw), cosine, sine_table).astype(jnp.bfloat16)
-        attended, log_total = attend(
+        attended, log_total = attend_gathered(
             query_rot,
             key_rot.reshape(seq_count, stretch_len, model_width),
             values.reshape(seq_count, stretch_len, model_width),
@@ -307,7 +820,7 @@
         delta_rows = jnp.transpose(
             jnp.sum(grad_heads.astype(jnp.float32) * attended, axis=-1), (0, 2, 1)
         )
-        grad_query, grad_key, grad_value = attend_back(
+        grad_query, grad_key, grad_value = attend_back_gathered(
             query_rot,
             key_rot,
             heads_of(values),
@@ -390,32 +903,248 @@
     )
 
 
+def body_planes(
+    tokens, seq_lens, norm_attn, w_qkv, w_out, norm_ffn, w_gate, w_up, w_down, cotangent
+):
+    seqs, stretch, width = tokens.shape
+    y, c, z, x = (lax.axis_index(axis) for axis in ALL)
+    lane = c * 4 + y * 2 + x
+    where = jnp.stack([y, c, z, x]).astype(jnp.int32)
+    rows = seqs * stretch
+
+    def to_plane(field):
+        field = jnp.transpose(field.reshape(seqs, 2, 8, 16, width), (2, 0, 1, 3, 4))
+        field = lax.all_to_all(field, PLANE, 0, 0, tiled=True)
+        field = lax.all_to_all(field.reshape((4, 2) + field.shape[1:]), "z", 0, 0, tiled=True)
+        return jnp.transpose(field.reshape(8, seqs, 2, 16, width), (1, 0, 2, 3, 4)).reshape(rows, width)
+
+    def from_plane(field):
+        field = jnp.transpose(field.reshape(seqs, 8, 2, 16, width), (1, 0, 2, 3, 4))
+        field = lax.all_to_all(field.reshape((4, 2) + field.shape[1:]), "z", 0, 0, tiled=True)
+        field = lax.all_to_all(field.reshape(8, seqs, 2, 16, width), PLANE, 0, 0, tiled=True)
+        return jnp.transpose(field, (1, 2, 0, 3, 4)).reshape(seqs, stretch, width)
+
+    def gather_attn(layer):
+        gain = jnp.stack([norm_attn[layer], norm_ffn[layer]], axis=1)
+        gain = jnp.pad(gain, ((0, 0), (0, 126)))
+        shard = jnp.concatenate([w_qkv[layer, :, : 2 * width], gain], axis=1)
+        w_qk = gather_z_first(where, shard, "x", "y")
+        shard = jnp.concatenate([w_qkv[layer, :, 2 * width :], w_out[layer]], axis=1)
+        w_vo = gather_z_first(where, shard, "y", "x")
+        gain = jnp.transpose(w_qk[:, 2 * width : 2 * width + 128])[:2].astype(F32)
+        return w_qk, w_vo, gain
+
+    def gather_ffn(layer):
+        shard = jnp.concatenate([w_gate[layer], w_up[layer]], axis=1)
+        w_gu = gather_z_first(where, shard, "y", "x")
+        w_d = gather_x_first(where, w_down[layer])
+        return w_gu, w_d
+
+    route = []
+    for sy in range(2):
+        for sc in range(2):
+            for sb in range(8):
+                ty, tc, tx = (sb >> 1) & 1, sb >> 2, sb & 1
+                route.append(((sy * 2 + sc) * 8 + sb, ((ty * 2 + tc) * 4 + 2 * sc + sy) * 2 + tx))
+    lengths = lax.ppermute(seq_lens, ALL, route)[0]
+    slots = stretch * 8
+    half_dim = width // HEADS // 2
+    freqs = 10000.0 ** (-jnp.arange(half_dim, dtype=F32) / half_dim)
+    angle = jnp.arange(slots, dtype=F32)[:, None] * freqs[None, :]
+    cosine, sine = jnp.cos(angle), jnp.sin(angle)
+    cosine = jnp.concatenate([cosine] * 4, axis=1)
+    sine = jnp.concatenate([-sine, sine] * 2, axis=1)
+
+    def mine(table):
+        own = lax.dynamic_index_in_dim(
+            table.reshape(slots // 128, 8, 16, 128), lane, 1, keepdims=False
+        )
+        return jnp.concatenate([own.reshape(stretch, 128)] * seqs)
+
+    my_cos, my_sin = mine(cosine), mine(sine)
+    step = jnp.arange(stretch, dtype=jnp.int32)
+    places = (step // 16) * 128 + lane * 16 + step % 16
+    valid = (places[None, :] < lengths[:, None]).astype(F32).reshape(rows, 1)
+
+    def exchange(field):
+        return lax.all_to_all(field, PLANE, 0, 0, tiled=True)
+
+    def forward_layer(inputs, layer, w_attn, w_ffn, first_value):
+        w_qk, w_vo, gain_all = w_attn
+        w_gu, w_d = w_ffn
+        ffn = w_gu.shape[1] // 2
+        rms_one = lax.rsqrt(jnp.mean(inputs * inputs, axis=-1, keepdims=True) + EPSILON)
+        normed = (inputs * rms_one * gain_all[0]).astype(BF)
+        parts = project_qkv(normed, w_qk, w_vo, my_cos, my_sin, first_value)
+        pieces = exchange(parts).reshape(8, 3, seqs, stretch // 16, 16, 128)
+        attended, lse = attend(lengths, pieces)
+        attn_low = exchange(attended.reshape(8, rows, 128))
+        attn_low = jnp.transpose(attn_low, (1, 0, 2)).reshape(rows, width)
+        middle = inputs + jnp.dot(attn_low, w_vo[:, width:], preferred_element_type=F32)
+        rms_two = lax.rsqrt(jnp.mean(middle * middle, axis=-1, keepdims=True) + EPSILON)
+        normed_two = (middle * rms_two * gain_all[1]).astype(BF)
+        gate = jnp.dot(normed_two, w_gu[:, :ffn], preferred_element_type=F32)
+        up = jnp.dot(normed_two, w_gu[:, ffn:], preferred_element_type=F32)
+        hidden = (jax.nn.silu(gate) * up).astype(BF)
+        result = middle + jnp.dot(hidden, w_d, preferred_element_type=F32)
+        kept = (
+            inputs, rms_one, normed, pieces, attended, attn_low, lse, middle, rms_two,
+            normed_two, gate, up, hidden,
+        )
+        return result, parts, kept
+
+    def own_half(field):
+        view = field.reshape(rows, 2, 2, -1)
+        own = lax.dynamic_index_in_dim(view, c, 2, keepdims=False).reshape(rows, -1)
+        other = lax.dynamic_index_in_dim(view, 1 - c, 2, keepdims=False).reshape(rows, -1)
+        return own, swap(other, "c")
+
+    def row_grad(left, right, right_near, tile):
+        own, near = own_half(left)
+        grad = weight_grad(own, near, right, right_near, tile)
+        return grad.reshape(2, 4, 2, -1, grad.shape[1])
+
+    def norm_back(grad_normed, source, rms, gain):
+        scaled = source * rms
+        grad_gain = jnp.sum(grad_normed * scaled, axis=0)
+        weighted = grad_normed * gain
+        grad = rms * (weighted - scaled * jnp.mean(weighted * scaled, axis=-1, keepdims=True))
+        return grad, grad_gain
+
+    def backward_layer(grad_in, layer, w_attn, w_ffn, kept, passed):
+        w_qk, w_vo, gain_all = w_attn
+        w_gu, w_d = w_ffn
+        ffn = w_gu.shape[1] // 2
+        (
+            inputs, rms_one, normed, pieces, attended, attn_low, lse, middle, rms_two,
+            normed_two, gate, up, hidden,
+        ) = kept
+        grad_low = grad_in.astype(BF)
+        near_low = swap(grad_low, "c")
+        grad_hidden = lax.dot_general(grad_low, w_d, NT, preferred_element_type=F32)
+        sigma = jax.nn.sigmoid(gate)
+        grad_gate = (grad_hidden * up * sigma * (1.0 + gate * (1.0 - sigma))).astype(BF)
+        grad_up = (grad_hidden * gate * sigma).astype(BF)
+        near_gate, near_up = swap(grad_gate, "c"), swap(grad_up, "c")
+        down = reduce_rows(row_grad(hidden, grad_low, near_low, 512).reshape(2, 4, 2, -1, width), "yzx")
+        gates = reduce_rows(row_grad(normed_two, grad_gate, near_gate, 256), "xyz")
+        ups = reduce_rows(row_grad(normed_two, grad_up, near_up, 256), "yxz")
+        grad_normed = lax.dot_general(
+            grad_gate, w_gu[:, :ffn], NT, preferred_element_type=F32
+        ) + lax.dot_general(grad_up, w_gu[:, ffn:], NT, preferred_element_type=F32)
+        grad, gain_two = norm_back(grad_normed, middle, rms_two, gain_all[1])
+        grad_middle = grad_in + grad
+        grad_attn = grad_middle.astype(BF)
+        near_attn = swap(grad_attn, "c")
+        out = reduce_rows(row_grad(attn_low, grad_attn, near_attn, 512), "xyz")
+        grad_o = lax.dot_general(
+            grad_attn, w_vo[:, width:], NT, preferred_element_type=F32
+        ).astype(BF)
+        grad_o = jnp.transpose(grad_o.reshape(rows, 8, 128), (1, 0, 2))
+        grad_o = exchange(grad_o).reshape(attended.shape)
+        parts, passed = attend_back(
+            lengths, pieces, attended, grad_o, lse, cosine, sine, passed
+        )
+        parts = exchange(parts.reshape(8, 3, rows, 128))
+        grad_proj = jnp.transpose(parts, (2, 1, 0, 3)).reshape(rows, 3 * width)
+        near_proj = swap(grad_proj, "c")
+        half = 3 * width // 2
+        left, near_left = own_half(normed)
+
+        def qkv_grad(lo, order):
+            grad = weight_grad(
+                left, near_left, grad_proj[:, lo : lo + half], near_proj[:, lo : lo + half], 512
+            )
+            return reduce_rows(grad.reshape(2, 4, 2, -1, half), order)
+
+        qkv = jnp.concatenate([qkv_grad(0, "yxz"), qkv_grad(half, "xyz")], axis=1)
+        grad_normed = lax.dot_general(
+            grad_proj[:, : 2 * width], w_qk[:, : 2 * width], NT, preferred_element_type=F32
+        ) + lax.dot_general(
+            grad_proj[:, 2 * width :], w_vo[:, :width], NT, preferred_element_type=F32
+        )
+        grad, gain_one = norm_back(grad_normed, inputs, rms_one, gain_all[0])
+        return grad_middle + grad, (gain_one, qkv, out, gain_two, gates, ups, down), passed
+
+    state = to_plane(tokens).astype(F32)
+    attn_one = gather_attn(0)
+    ffn_one = gather_ffn(0)
+    attn_two = gather_attn(1)
+    ffn_two = gather_ffn(1)
+    grad = to_plane(cotangent).astype(F32) * valid
+    middle, first_value, kept_one = forward_layer(state, 0, attn_one, ffn_one, None)
+    final, _, kept_two = forward_layer(middle, 1, attn_two, ffn_two, first_value)
+    layer_out = from_plane(final.astype(BF))
+    grad, grads_two, passed = backward_layer(grad, 1, attn_two, ffn_two, kept_two, None)
+    grad, grads_one, _ = backward_layer(grad, 0, attn_one, ffn_one, kept_one, passed)
+    input_grad = from_plane(grad.astype(BF)).astype(F32)
+
+    sums = jnp.stack([grads_one[0], grads_two[0], grads_one[3], grads_two[3]])
+    sums = sums + swap(sums, "c")
+    sums = sums + swap(sums, "x")
+    sums = sums + swap(sums, "y")
+    sums = sums + hop(sums, 1)
+    sums = sums + hop(sums, 2)
+    sums = sums.reshape(4, 32, width // 32)
+    mine_sums = lax.dynamic_index_in_dim(
+        sums, ((y * 2 + c) * 4 + z) * 2 + x, 1, keepdims=False
+    )
+    pairs = [jnp.stack([one, two]) for one, two in zip(grads_one, grads_two)]
+    return (
+        layer_out,
+        input_grad,
+        mine_sums[:2],
+        pairs[1],
+        pairs[2],
+        mine_sums[2:],
+        pairs[4],
+        pairs[5],
+        pairs[6],
+    )
+
+
+IN_SPECS = (
+    ("grp", "seq", None),
+    ("grp", None),
+    (None, ("grp", "seq")),
+    (None, ("grp", "seq"), None),
+    (None, ("grp", "seq"), None),
+    (None, ("grp", "seq")),
+    (None, ("grp", "seq"), None),
+    (None, ("grp", "seq"), None),
+    (None, ("grp", "seq"), None),
+    ("grp", "seq", None),
+)
+OUT_SPECS = (
+    ("grp", "seq", None),
+    ("grp", "seq", None),
+    (None, ("grp", "seq")),
+    (None, ("grp", "seq"), None),
+    (None, ("grp", "seq"), None),
+    (None, ("grp", "seq")),
+    (None, ("grp", "seq"), None),
+    (None, ("grp", "seq"), None),
+    (None, ("grp", "seq"), None),
+)
+
+
 def solution(mesh):
+    if mesh.shape["grp"] == 4 and mesh.shape["seq"] == 8:
+        split = Mesh(mesh.devices.reshape(2, 2, 4, 2), ALL)
+        names = {"grp": ("y", "c"), "seq": ("z", "x"), ("grp", "seq"): ALL, None: None}
+        program = body_planes
+    else:
+        split = mesh
+        names = {"grp": "grp", "seq": "seq", ("grp", "seq"): ("grp", "seq"), None: None}
+        program = body
+
+    def specs(table):
+        return tuple(P(*(names[name] for name in row)) for row in table)
+
     return jax.shard_map(
-        body,
-        mesh=mesh,
-        in_specs=(
-            P("grp", "seq", None),
-            P("grp", None),
-            P(None, ("grp", "seq")),
-            P(None, ("grp", "seq"), None),
-            P(None, ("grp", "seq"), None),
-            P(None, ("grp", "seq")),
-            P(None, ("grp", "seq"), None),
-            P(None, ("grp", "seq"), None),
-            P(None, ("grp", "seq"), None),
-            P("grp", "seq", None),
-        ),
-        out_specs=(
-            P("grp", "seq", None),
-            P("grp", "seq", None),
-            P(None, ("grp", "seq")),
-            P(None, ("grp", "seq"), None),
-            P(None, ("grp", "seq"), None),
-            P(None, ("grp", "seq")),
-            P(None, ("grp", "seq"), None),
-            P(None, ("grp", "seq"), None),
-            P(None, ("grp", "seq"), None),
-        ),
+        program,
+        mesh=split,
+        in_specs=specs(IN_SPECS),
+        out_specs=specs(OUT_SPECS),
         check_vma=False,
     )

time: 3880 us -> 1430 us (0.37)
  waiting for transfers between devices: 2510 us -> 457 us
  matrix products: 770 us -> 99.9 us
  Pallas kernels: 0 us -> 310 us
  starting transfers between devices: 1.96 us -> 269 us
  blocking collectives: 221 us -> 0 us
  local copies, waits for them, and re-layouts: 249 us -> 188 us
    reduce_scatter x10 -> x0, waiting for transfers between devices: 1790 us -> none  [the longest x2 500 us: reduce_layer(): lax.psum_scatter(grads[4], ('grp', 'seq'), scatter_dimension=0, tiled=True)]
    all_gather x18 -> x0, waiting for transfers between devices: 710 us -> none  [the longest x2 235 us: attend(): k_piece = lax.all_gather(k_flat, 'seq', axis=1, tiled=True)]
    dot_general x78 -> x20, matrix products: 770 us -> 99.9 us  [the longest x2 19 us: backward_layer(): grad_hidden = lax.dot_general(grad_low, w_d, NT, preferred_element_type=F32)]
    ppermute x0 -> x158, waiting for transfers between devices: none -> 451 us  [the longest x95 326 us: swap(): return lax.ppermute(value, axis, [(0, 1), (1, 0)])]
    pallas_call x0 -> x26, Pallas kernels: none -> 310 us  [the longest x2 79.5 us: attend(): pl.pallas_call(kernel, grid=(2, tiles), in_specs=[SMEM, ANY], out_specs=[...]
    ppermute x0 -> x158, starting transfers between devices: none -> 195 us  [the longest x62 130 us: hop(): return lax.ppermute(value, 'z', [(i, i ^ offset) for i in range(4)])]
    all_gather x4 -> x0, blocking collectives: 133 us -> none  [the longest x2 68.5 us: attend_back(): lax.all_gather(log_total, 'seq', axis=2, tiled=True)]
    slice x35 -> x7, local copies, waits for them, and re-layouts: 138 us -> 13 us  [the longest x2 7.64 us: qkv_grad(): near_proj[:, lo:lo + half]]
  transfers between devices with their start and end apart: 28 -> 174, of which waited for: 21 -> 47; matrix products, arithmetic and copies ran while one was open for 28% -> 22% of each run, Pallas kernels for 0% -> 22%
where the time goes in v1:
time: 1430 us; the launch traced here: 1420 us
  waiting for transfers between devices  457 us (32%)
  Pallas kernels  310 us (22%)
  starting transfers between devices  269 us (19%)
  local copies, waits for them, and re-layouts  188 us (13%)
  matrix products  99.9 us (7%)
  other arithmetic  88.9 us (6%)
    ppermute x95, waiting for transfers between devices, swap(): return lax.ppermute(value, axis, [(0, 1), (1, 0)])  326 us
    ppermute x62, starting transfers between devices, hop(): return lax.ppermute(value, 'z', [(i, i ^ offset) for i in range(4)])  130 us
    ppermute x62, waiting for transfers between devices, hop(): return lax.ppermute(value, 'z', [(i, i ^ offset) for i in range(4)])  125 us
    pallas_call x2, Pallas kernels, attend(): pl.pallas_call(kernel, grid=(2, tiles), in_specs=[SMEM, ANY], out_specs=[...  79.5 us
    pallas_call x12, Pallas kernels, weight_grad(): pl.pallas_call(kernel, grid=(cols // tile,), in_specs=[whole, whole, bloc...  75.7 us
    pallas_call x2, Pallas kernels, attend_back(): pl.pallas_call(kernel, grid=(2, tiles), in_specs=in_specs, out_specs=out_...  68.8 us
    ppermute x95, starting transfers between devices, swap(): return lax.ppermute(value, axis, [(0, 1), (1, 0)])  64.9 us
    pallas_call x8, Pallas kernels, assemble(): pl.pallas_call(kernel, in_specs=[SMEM] + [ANY] * count, out_specs=ANY, ou...  61.4 us
  transfers between devices with their start and end apart: 174, of which 47 were waited for; matrix products, arithmetic and copies ran while one was open for 22% of the time, Pallas kernels for 22%

profile of v1, /device:TPU:0, one launch (start us, length us, event | category | flops | bytes accessed | tf_op | source)
XLA Modules:
  0.0 1417.0 jit_solution(237439789961064172)
XLA Ops:
  49.6 15.9 %collective-permute-done.68 = bf16[88,1024]{1,0:T(8,128)(2,1)S(1)} collective-permute-done((bf16[88,1024]{1,0:T(8,128)(2,1)S(1)}, bf16[88,1024]{1,0:T(8,128)(2,1)S(1)}, u32[]{:S(2)}, u32[]{:S(2)}) %collective-permute-start.68) | collective-permute-done | bytes 180256 | tf_op jit(solution)/shard_map/ppermute | solution.py:68
  135.4 12.1 project_qkv.2.rest_0_
  152.3 13.4 collective-permute-done.22
  165.7 9.6 collective-permute-start.32
  188.3 23.7 %collective-permute-done.33 = bf16[176,1024]{1,0:T(8,128)(2,1)S(1)} collective-permute-done((bf16[176,1024]{1,0:T(8,128)(2,1)}, bf16[176,1024]{1,0:T(8,128)(2,1)S(1)}, u32[]{:S(2)}, u32[]{:S(2)}) %collective-permute-start.33) | collective-permute-done | bytes 360480 | tf_op jit(solution)/shard_map/ppermute | solution.py:72
  218.8 11.7 collective-permute-done.42.rest_2_
  231.4 25.5 %collective-permute-done.44.rest_4_ = bf16[4,32,2176]{2,1,0:T(8,128)(2,1)S(1)} collective-permute-done((bf16[4,32,2176]{2,1,0:T(8,128)(2,1)S(1)}, bf16[4,32,2176]{2,1,0:T(8,128)(2,1)S(1)}, u32[]{:S(2)}, u32[]{:S(2)}) %collective-permute-start.44) | collective-permute-done | bytes 557088 | tf_op jit(solution)/shard_map/ppermute | solution.py:68
  263.4 10.1 collective-permute-done.46.rest_6_
  283.9 12.9 collective-permute-done.27.rest_4_
  297.3 10.8 collective-permute-done.36.rest_2_
  308.7 19.0 %collective-permute-done.29.rest_6_ = bf16[4,32,5632]{2,1,0:T(8,128)(2,1)} collective-permute-done((bf16[4,32,5632]{2,1,0:T(8,128)(2,1)}, bf16[4,32,5632]{2,1,0:T(8,128)(2,1)}, u32[]{:S(2)}, u32[]{:S(2)}) %collective-permute-start.29) | collective-permute-done | bytes 1441824 | tf_op jit(solution)/shard_map/ppermute | solution.py:68
  329.7 39.8 %attend.2 = (bf16[8,2,16,16,128]{4,3,2,1,0:T(8,128)(2,1)S(1)}, f32[2,8,2048]{2,1,0:T(8,128)S(1)}) custom-call(s32[2]{0:T(128)S(1)} %bitcast.558, bf16[8,3,2,16,16,128]{5,4,3,2,1,0:T(8,128)(2,1)} %bitcast.31.piece_ref.refs_1_), custom_call_target="tpu_custom_call" | custom-call | tf_op jit(solution)/shard_map/attend/pallas_call | solution.py:301
  409.7 9.5 assemble.10
  448.0 12.3 project_qkv.3
  472.2 61.3 %collective-permute-done.73.rest_2_ = bf16[4,176,1024]{2,1,0:T(8,128)(2,1)} collective-permute-done((bf16[4,176,1024]{2,1,0:T(8,128)(2,1)}, bf16[4,176,1024]{2,1,0:T(8,128)(2,1)}, u32[]{:S(2)}, u32[]{:S(2)}) %collective-permute-start.73) | collective-permute-done | bytes 1441824 | tf_op jit(solution)/shard_map/ppermute | solution.py:68
  534.7 29.8 %collective-permute-done.66.rest_6_ = bf16[4,32,5632]{2,1,0:T(8,128)(2,1)} collective-permute-done((bf16[4,32,5632]{2,1,0:T(8,128)(2,1)}, bf16[4,32,5632]{2,1,0:T(8,128)(2,1)}, u32[]{:S(2)}, u32[]{:S(2)}) %collective-permute-start.66) | collective-permute-done | bytes 1441824 | tf_op jit(solution)/shard_map/ppermute | solution.py:68
  568.7 39.7 %attend.3 = (bf16[8,2,16,16,128]{4,3,2,1,0:T(8,128)(2,1)S(1)}, f32[2,8,2048]{2,1,0:T(8,128)S(1)}) custom-call(s32[2]{0:T(128)S(1)} %bitcast.561, bf16[8,3,2,16,16,128]{5,4,3,2,1,0:T(8,128)(2,1)} %bitcast.64.piece_ref.refs_1_), custom_call_target="tpu_custom_call" | custom-call | tf_op jit(solution)/shard_map/attend/pallas_call | solution.py:301
  632.9 9.5 assemble.14
  654.4 10.8 multiply_convert_fusion.3
  681.4 9.4 multiply_reduce_fusion
  795.0 34.3 %attend_back.2 = (bf16[8,3,2,16,16,128]{5,4,3,2,1,0:T(8,128)(2,1)}, f32[2,2048,128]{2,1,0:T(8,128)}) custom-call(s32[2]{0:T(128)S(1)} %bitcast.562, bf16[8,3,2,16,16,128]{5,4,3,2,1,0:T(8,128)(2,1)} %bitcast.64.piece_ref.refs_1_, bf16[8,2,16,16,128]{4,3,2,1,0:T(8,128)(2,1)S(1)} %copy-done.18, bf16[8,2,16,16,128]{4,3,2,1,0:T(8,128)(2,1)} %bitcast.97.refs_3_, ...), custom_call_target="tpu_custom_call" | custom-call | tf_op jit(solution)/shard_map/attend_back/pallas_call | solution.py:504
  881.5 9.3 weight_grad.21
  893.4 9.6 weight_grad.19
  926.5 11.4 multiply_convert_fusion.1
  979.3 34.5 %attend_back.3 = bf16[8,3,2,16,16,128]{5,4,3,2,1,0:T(8,128)(2,1)} custom-call(s32[2]{0:T(128)S(1)} %bitcast.563, bf16[8,3,2,16,16,128]{5,4,3,2,1,0:T(8,128)(2,1)} %bitcast.31.piece_ref.refs_1_, bf16[8,2,16,16,128]{4,3,2,1,0:T(8,128)(2,1)S(1)} %copy-done.14, bf16[8,2,16,16,128]{4,3,2,1,0:T(8,128)(2,1)} %bitcast.101.refs_3_, f32[2,8,2048]{2,1,0:T(8,128)S(1)} %copy-done.56, ...), custom_call_target="tpu_custom_call" | custom-call | tf_op jit(solution)/shard_map/attend_back/pallas_call | solution.py:504
  1043.4 27.9 %collective-permute-done.128 = bf16[4,32,2816]{2,1,0:T(8,128)(2,1)S(1)} collective-permute-done((bf16[4,32,2816]{2,1,0:T(8,128)(2,1)}, bf16[4,32,2816]{2,1,0:T(8,128)(2,1)S(1)}, u32[]{:S(2)}, u32[]{:S(2)}) %collective-permute-start.128) | collective-permute-done | bytes 720928 | tf_op jit(solution)/shard_map/ppermute | solution.py:68
  1078.5 28.9 %collective-permute-done.107 = bf16[4,32,1024]{2,1,0:T(8,128)(2,1)S(1)} collective-permute-done((bf16[4,32,1024]{2,1,0:T(8,128)(2,1)S(1)}, bf16[4,32,1024]{2,1,0:T(8,128)(2,1)S(1)}, u32[]{:S(2)}, u32[]{:S(2)}) %collective-permute-start.107) | collective-permute-done | bytes 262176 | tf_op jit(solution)/shard_map/ppermute | solution.py:68
  1143.9 10.2 collective-permute-done.147
  1157.8 11.4 collective-permute-done.148
  1173.3 9.3 weight_grad.20
  1262.2 14.1 collective-permute-done.99
  1369.9 11.6 collective-permute-done.82
  (926 shorter events, 813.6 us)
Async XLA Ops:
  147.5 131.8 %all-to-all-start.2 = ((bf16[8,3,512,128]{3,2,1,0:T(8,128)(2,1)}), bf16[8,3,512,128]{3,2,1,0:T(8,128)(2,1)}, u32[]{:S(2)}, u32[]{:S(2)}) async-start(bf16[8,3,512,128]{3,2,1,0:T(8,128)(2,1)} %project_qkv.2.rest_0_), calls=%async_computation.2 | async-start | bytes 6291456 | tf_op jit(solution)/shard_map/all_to_all | solution.py:970
  279.2 91.6 %all-to-all-start.8 = ((bf16[8,2,2,16,1024]{4,3,2,1,0:T(8,128)(2,1)}), bf16[8,2,2,16,1024]{4,3,2,1,0:T(8,128)(2,1)}, u32[]{:S(2)}, u32[]{:S(2)}) async-start(bf16[8,2,2,16,1024]{4,3,2,1,0:T(8,128)(2,1)} %copy.377), calls=%async_computation.8 | async-start | bytes 2097152 | tf_op jit(solution)/shard_map/all_to_all | solution.py:917
  296.8 106.6 %collective-permute-start.24 = (bf16[4,32,5632]{2,1,0:T(8,128)(2,1)S(1)}, bf16[4,32,5632]{2,1,0:T(8,128)(2,1)}, u32[]{:S(2)}, u32[]{:S(2)}) collective-permute-start(bf16[4,32,5632]{2,1,0:T(8,128)(2,1)S(1)} %pad_maximum_fusion.rest_0_), channel_id=1, source_target_pairs={{0,8},{8,0},{1,9},{9,1},{2,10},{10,2},{3,11},{11,3},{4,12},{12,4},... | collective-permute-start | bytes 4325384 | tf_op jit(solution)/shard_map/ppermute | solution.py:68
  296.8 108.6 %collective-permute-start.26 = (bf16[4,32,5632]{2,1,0:T(8,128)(2,1)}, bf16[4,32,5632]{2,1,0:T(8,128)(2,1)}, u32[]{:S(2)}, u32[]{:S(2)}) collective-permute-start(bf16[4,32,5632]{2,1,0:T(8,128)(2,1)} %collective-permute-done.25.rest_2_), channel_id=1, source_target_pairs={{0,8},{8,0},{1,9},{9,1},{2,10},{10,2},{3,11},{11,3},{4,12},{12,4},... | collective-permute-start | bytes 4325384 | tf_op jit(solution)/shard_map/ppermute | solution.py:68
  308.2 99.7 %collective-permute-start.28 = (bf16[4,32,5632]{2,1,0:T(8,128)(2,1)}, bf16[4,32,5632]{2,1,0:T(8,128)(2,1)}, u32[]{:S(2)}, u32[]{:S(2)}) collective-permute-start(bf16[4,32,5632]{2,1,0:T(8,128)(2,1)} %collective-permute-done.27.rest_4_), channel_id=1, source_target_pairs={{0,8},{8,0},{1,9},{9,1},{2,10},{10,2},{3,11},{11,3},{4,12},{12,4},... | collective-permute-start | bytes 4325384 | tf_op jit(solution)/shard_map/ppermute | solution.py:68
  308.2 89.2 %collective-permute-start.37 = (bf16[4,176,1024]{2,1,0:T(8,128)(2,1)}, bf16[4,176,1024]{2,1,0:T(8,128)(2,1)}, u32[]{:S(2)}, u32[]{:S(2)}) collective-permute-start(bf16[4,176,1024]{2,1,0:T(8,128)(2,1)} %collective-permute-done.36.rest_2_), channel_id=1, source_target_pairs={{0,8},{8,0},{1,9},{9,1},{2,10},{10,2},{3,11},{11,3},{4,12},{12,4},... | collective-permute-start | bytes 4325384 | tf_op jit(solution)/shard_map/ppermute | solution.py:68
  327.7 82.0 %collective-permute-start.30 = (bf16[4,32,5632]{2,1,0:T(8,128)(2,1)}, bf16[4,32,5632]{2,1,0:T(8,128)(2,1)}, u32[]{:S(2)}, u32[]{:S(2)}) collective-permute-start(bf16[4,32,5632]{2,1,0:T(8,128)(2,1)} %collective-permute-done.29.rest_6_), channel_id=1, source_target_pairs={{0,8},{8,0},{1,9},{9,1},{2,10},{10,2},{3,11},{11,3},{4,12},{12,4},... | collective-permute-start | bytes 4325384 | tf_op jit(solution)/shard_map/ppermute | solution.py:68
  461.2 107.4 %all-to-all-start.4 = ((bf16[8,3,512,128]{3,2,1,0:T(8,128)(2,1)}), bf16[8,3,512,128]{3,2,1,0:T(8,128)(2,1)}, u32[]{:S(2)}, u32[]{:S(2)}) async-start(bf16[8,3,512,128]{3,2,1,0:T(8,128)(2,1)} %project_qkv.3), calls=%async_computation.4 | async-start | bytes 6291456 | tf_op jit(solution)/shard_map/all_to_all | solution.py:970
  471.6 92.8 %collective-permute-start.66 = (bf16[4,32,5632]{2,1,0:T(8,128)(2,1)}, bf16[4,32,5632]{2,1,0:T(8,128)(2,1)}, u32[]{:S(2)}, u32[]{:S(2)}) collective-permute-start(bf16[4,32,5632]{2,1,0:T(8,128)(2,1)} %collective-permute-done.62.rest_2_), channel_id=1, source_target_pairs={{0,1},{1,0},{2,3},{3,2},{4,5},{5,4},{6,7},{7,6},{8,9},{9,8},{10,11... | collective-permute-start | bytes 4325384 | tf_op jit(solution)/shard_map/ppermute | solution.py:68
  533.5 85.9 %collective-permute-start.74 = (bf16[4,176,1024]{2,1,0:T(8,128)(2,1)}, bf16[4,176,1024]{2,1,0:T(8,128)(2,1)}, u32[]{:S(2)}, u32[]{:S(2)}) collective-permute-start(bf16[4,176,1024]{2,1,0:T(8,128)(2,1)} %collective-permute-done.73.rest_2_), channel_id=1, source_target_pairs={{0,8},{8,0},{1,9},{9,1},{2,10},{10,2},{3,11},{11,3},{4,12},{12,4},... | collective-permute-start | bytes 4325384 | tf_op jit(solution)/shard_map/ppermute | solution.py:68
  533.7 99.2 %collective-permute-start.61 = (bf16[4,32,5632]{2,1,0:T(8,128)(2,1)S(1)}, bf16[4,32,5632]{2,1,0:T(8,128)(2,1)}, u32[]{:S(2)}, u32[]{:S(2)}) collective-permute-start(bf16[4,32,5632]{2,1,0:T(8,128)(2,1)S(1)} %pad_maximum_fusion.2.rest_0_), channel_id=1, source_target_pairs={{0,8},{8,0},{1,9},{9,1},{2,10},{10,2},{3,11},{11,3},{4,12},{12,4},... | collective-permute-start | bytes 4325384 | tf_op jit(solution)/shard_map/ppermute | solution.py:68
  534.2 98.7 %collective-permute-start.63 = (bf16[4,32,5632]{2,1,0:T(8,128)(2,1)}, bf16[4,32,5632]{2,1,0:T(8,128)(2,1)}, u32[]{:S(2)}, u32[]{:S(2)}) collective-permute-start(bf16[4,32,5632]{2,1,0:T(8,128)(2,1)} %collective-permute-done.62.rest_2_), channel_id=1, source_target_pairs={{0,8},{8,0},{1,9},{9,1},{2,10},{10,2},{3,11},{11,3},{4,12},{12,4},... | collective-permute-start | bytes 4325384 | tf_op jit(solution)/shard_map/ppermute | solution.py:68
  534.3 98.6 %collective-permute-start.65 = (bf16[4,32,5632]{2,1,0:T(8,128)(2,1)}, bf16[4,32,5632]{2,1,0:T(8,128)(2,1)}, u32[]{:S(2)}, u32[]{:S(2)}) collective-permute-start(bf16[4,32,5632]{2,1,0:T(8,128)(2,1)} %collective-permute-done.64.rest_4_), channel_id=1, source_target_pairs={{0,8},{8,0},{1,9},{9,1},{2,10},{10,2},{3,11},{11,3},{4,12},{12,4},... | collective-permute-start | bytes 4325384 | tf_op jit(solution)/shard_map/ppermute | solution.py:68
  732.1 148.3 %collective-permute-start.138 = (bf16[512,2816]{1,0:T(8,128)(2,1)}, bf16[512,2816]{1,0:T(8,128)(2,1)}, u32[]{:S(2)}, u32[]{:S(2)}) collective-permute-start(bf16[512,2816]{1,0:T(8,128)(2,1)} %get-tuple-element.43.ro), channel_id=1, source_target_pairs={{0,8},{8,0},{1,9},{9,1},{2,10},{10,2},{3,11},{11,3},{4,12},{12,4},... | collective-permute-start | bytes 8650760 | tf_op jit(solution)/shard_map/ppermute | solution.py:68
  742.9 150.5 %collective-permute-start.126 = (bf16[512,2816]{1,0:T(8,128)(2,1)}, bf16[512,2816]{1,0:T(8,128)(2,1)}, u32[]{:S(2)}, u32[]{:S(2)}) collective-permute-start(bf16[512,2816]{1,0:T(8,128)(2,1)} %get-tuple-element.41.ro), channel_id=1, source_target_pairs={{0,8},{8,0},{1,9},{9,1},{2,10},{10,2},{3,11},{11,3},{4,12},{12,4},... | collective-permute-start | bytes 8650760 | tf_op jit(solution)/shard_map/ppermute | solution.py:68
  745.5 83.9 %all-to-all-start.7 = ((bf16[8,2,2,16,1024]{4,3,2,1,0:T(8,128)(2,1)}), bf16[8,2,2,16,1024]{4,3,2,1,0:T(8,128)(2,1)}, u32[]{:S(2)}, u32[]{:S(2)}) async-start(bf16[8,2,2,16,1024]{4,3,2,1,0:T(8,128)(2,1)} %bitcast.622), calls=%async_computation.7 | async-start | bytes 2097152 | tf_op jit(solution)/shard_map/all_to_all | solution.py:924
  786.7 87.7 %collective-permute-start.153 = (bf16[4,2,88,1024]{3,2,1,0:T(8,128)(2,1)}, bf16[4,2,88,1024]{3,2,1,0:T(8,128)(2,1)}, u32[]{:S(2)}, u32[]{:S(2)}) collective-permute-start(bf16[4,2,88,1024]{3,2,1,0:T(8,128)(2,1)} %dynamic-slice_bitcast_fusion), channel_id=1, source_target_pairs={{0,16},{16,0},{1,17},{17,1},{2,18},{18,2},{3,19},{19,3},{4,20},{20... | collective-permute-start | bytes 4325384 | tf_op jit(solution)/shard_map/ppermute | solution.py:68
  829.4 84.5 %all-to-all-start.11 = ((bf16[8,3,512,128]{3,2,1,0:T(8,128)(2,1)}), bf16[8,3,512,128]{3,2,1,0:T(8,128)(2,1)}, u32[]{:S(2)}, u32[]{:S(2)}) async-start(bf16[8,3,512,128]{3,2,1,0:T(8,128)(2,1)} %bitcast.625), calls=%async_computation.11 | async-start | bytes 6291456 | tf_op jit(solution)/shard_map/all_to_all | solution.py:970
  870.0 148.6 %collective-permute-start.144 = (bf16[512,1408]{1,0:T(8,128)(2,1)}, bf16[512,1408]{1,0:T(8,128)(2,1)}, u32[]{:S(2)}, u32[]{:S(2)}) collective-permute-start(bf16[512,1408]{1,0:T(8,128)(2,1)} %copy.430), channel_id=1, source_target_pairs={{0,8},{8,0},{1,9},{9,1},{2,10},{10,2},{3,11},{11,3},{4,12},{12,4},... | collective-permute-start | bytes 4325384 | tf_op jit(solution)/shard_map/ppermute | solution.py:68
  893.4 136.1 %collective-permute-start.104 = (bf16[512,512]{1,0:T(8,128)(2,1)}, bf16[512,512]{1,0:T(8,128)(2,1)}, u32[]{:S(2)}, u32[]{:S(2)}) collective-permute-start(bf16[512,512]{1,0:T(8,128)(2,1)} %copy.438), channel_id=1, source_target_pairs={{0,8},{8,0},{1,9},{9,1},{2,10},{10,2},{3,11},{11,3},{4,12},{12,4},... | collective-permute-start | bytes 1572872 | tf_op jit(solution)/shard_map/ppermute | solution.py:68
  926.5 92.7 %collective-permute-start.145 = (bf16[512,1024]{1,0:T(8,128)(2,1)}, bf16[512,1024]{1,0:T(8,128)(2,1)}, u32[]{:S(2)}, u32[]{:S(2)}) collective-permute-start(bf16[512,1024]{1,0:T(8,128)(2,1)} %get-tuple-element.35.ro), channel_id=1, source_target_pairs={{0,8},{8,0},{1,9},{9,1},{2,10},{10,2},{3,11},{11,3},{4,12},{12,4},... | collective-permute-start | bytes 3145736 | tf_op jit(solution)/shard_map/ppermute | solution.py:68
  965.5 69.4 %collective-permute-start.140 = (bf16[4,32,2816]{2,1,0:T(8,128)(2,1)}, bf16[4,32,2816]{2,1,0:T(8,128)(2,1)}, u32[]{:S(2)}, u32[]{:S(2)}) collective-permute-start(bf16[4,32,2816]{2,1,0:T(8,128)(2,1)} %dynamic-slice_bitcast_fusion.6), channel_id=1, source_target_pairs={{0,1},{1,0},{2,3},{3,2},{4,5},{5,4},{6,7},{7,6},{8,9},{9,8},{10,11... | collective-permute-start | bytes 2162696 | tf_op jit(solution)/shard_map/ppermute | solution.py:68
  1013.8 193.9 %all-to-all-start.13 = ((bf16[8,3,512,128]{3,2,1,0:T(8,128)(2,1)}), bf16[8,3,512,128]{3,2,1,0:T(8,128)(2,1)}, u32[]{:S(2)}, u32[]{:S(2)}) async-start(bf16[8,3,512,128]{3,2,1,0:T(8,128)(2,1)} %bitcast.592), calls=%async_computation.13 | async-start | bytes 6291456 | tf_op jit(solution)/shard_map/all_to_all | solution.py:970
  1018.6 152.6 %collective-permute-start.132 = (bf16[512,2816]{1,0:T(8,128)(2,1)}, bf16[512,2816]{1,0:T(8,128)(2,1)}, u32[]{:S(2)}, u32[]{:S(2)}) collective-permute-start(bf16[512,2816]{1,0:T(8,128)(2,1)} %copy-done.100), channel_id=1, source_target_pairs={{0,8},{8,0},{1,9},{9,1},{2,10},{10,2},{3,11},{11,3},{4,12},{12,4},... | collective-permute-start | bytes 8650760 | tf_op jit(solution)/shard_map/ppermute | solution.py:68
  1029.5 90.8 %collective-permute-start.146 = (bf16[4,2,88,1024]{3,2,1,0:T(8,128)(2,1)S(1)}, bf16[4,2,88,1024]{3,2,1,0:T(8,128)(2,1)S(1)}, u32[]{:S(2)}, u32[]{:S(2)}) collective-permute-start(bf16[4,2,88,1024]{3,2,1,0:T(8,128)(2,1)S(1)} %dynamic-slice_bitcast_fusion.1), channel_id=1, source_target_pairs={{0,16},{16,0},{1,17},{17,1},{2,18},{18,2},{3,19},{19,3},{4,20},{20... | collective-permute-start | bytes 4325384 | tf_op jit(solution)/shard_map/ppermute | solution.py:68
  1036.2 71.8 %collective-permute-start.141 = (bf16[32,2816]{1,0:T(8,128)(2,1)S(1)}, bf16[32,2816]{1,0:T(8,128)(2,1)S(1)}, u32[]{:S(2)}, u32[]{:S(2)}) collective-permute-start(bf16[32,2816]{1,0:T(8,128)(2,1)S(1)} %get-tuple-element.86), channel_id=1, source_target_pairs={{0,2},{2,0},{4,6},{6,4},{1,3},{3,1},{5,7},{7,5},{8,10},{10,8},{12,... | collective-permute-start | bytes 540680 | tf_op jit(solution)/shard_map/ppermute | solution.py:72
  1108.1 77.1 %collective-permute-start.119 = (bf16[512,2816]{1,0:T(8,128)(2,1)}, bf16[512,2816]{1,0:T(8,128)(2,1)}, u32[]{:S(2)}, u32[]{:S(2)}) collective-permute-start(bf16[512,2816]{1,0:T(8,128)(2,1)} %get-tuple-element.39.ro), channel_id=1, source_target_pairs={{0,8},{8,0},{1,9},{9,1},{2,10},{10,2},{3,11},{11,3},{4,12},{12,4},... | collective-permute-start | bytes 8650760 | tf_op jit(solution)/shard_map/ppermute | solution.py:68
  1170.0 183.1 %collective-permute-start.80 = (bf16[512,512]{1,0:T(8,128)(2,1)}, bf16[512,512]{1,0:T(8,128)(2,1)}, u32[]{:S(2)}, u32[]{:S(2)}) collective-permute-start(bf16[512,512]{1,0:T(8,128)(2,1)} %copy.393), channel_id=1, source_target_pairs={{0,8},{8,0},{1,9},{9,1},{2,10},{10,2},{3,11},{11,3},{4,12},{12,4},... | collective-permute-start | bytes 1572872 | tf_op jit(solution)/shard_map/ppermute | solution.py:68
  1185.2 101.6 %collective-permute-start.133 = (bf16[4,2,32,2816]{3,2,0,1:T(8,128)(2,1)}, bf16[4,2,32,2816]{3,2,0,1:T(8,128)(2,1)}, u32[]{:S(2)}, u32[]{:S(2)}) collective-permute-start(bf16[4,2,32,2816]{3,2,0,1:T(8,128)(2,1)} %bitcast.533), channel_id=1, source_target_pairs={{0,16},{16,0},{1,17},{17,1},{2,18},{18,2},{3,19},{19,3},{4,20},{20... | collective-permute-start | bytes 4325384 | tf_op jit(solution)/shard_map/ppermute | solution.py:68
  1196.1 93.9 %collective-permute-start.120 = (bf16[2,4,32,2816]{3,2,1,0:T(8,128)(2,1)}, bf16[2,4,32,2816]{3,2,1,0:T(8,128)(2,1)}, u32[]{:S(2)}, u32[]{:S(2)}) collective-permute-start(bf16[2,4,32,2816]{3,2,1,0:T(8,128)(2,1)} %dynamic-slice_bitcast_fusion.3), channel_id=1, source_target_pairs={{0,1},{1,0},{2,3},{3,2},{4,5},{5,4},{6,7},{7,6},{8,9},{9,8},{10,11... | collective-permute-start | bytes 4325384 | tf_op jit(solution)/shard_map/ppermute | solution.py:68
  1253.5 89.9 %all-to-all-start.14 = ((bf16[4,2,2,2,16,1024]{5,4,3,1,2,0:T(8,128)(2,1)}), bf16[4,2,2,2,16,1024]{5,4,3,1,2,0:T(8,128)(2,1)}, u32[]{:S(2)}, u32[]{:S(2)}) async-start(bf16[4,2,2,2,16,1024]{5,4,3,1,2,0:T(8,128)(2,1)} %copy.387), calls=%async_computation.14 | async-start | bytes 2097152 | tf_op jit(solution)/shard_map/all_to_all | solution.py:923
  1260.5 88.7 %collective-permute-start.81 = (bf16[512,3072]{1,0:T(8,128)(2,1)}, bf16[512,3072]{1,0:T(8,128)(2,1)}, u32[]{:S(2)}, u32[]{:S(2)}) collective-permute-start(bf16[512,3072]{1,0:T(8,128)(2,1)} %bitcast.588), channel_id=1, source_target_pairs={{0,8},{8,0},{1,9},{9,1},{2,10},{10,2},{3,11},{11,3},{4,12},{12,4},... | collective-permute-start | bytes 9437192 | tf_op jit(solution)/shard_map/ppermute | solution.py:68
  (309 other events, 5838.8 us)

commit v2 on v1

--- a/solution.py
+++ b/solution.py
@@ -86,39 +86,63 @@
     return assemble(where, pieces, relative, True)
 
 
-def gather_x_first(where, shard):
-    near = swap(shard, "x")
-    even = lax.axis_index("x") == 0
-    pair = jnp.concatenate([jnp.where(even, shard, near), jnp.where(even, near, shard)])
-    stack = jnp.stack([pair] + [hop(pair, k) for k in (1, 2, 3)])
-    pieces, relative = [], []
-    for dy, piece in ((0, stack), (1, swap(stack, "y"))):
-        for dc, held in ((0, piece), (1, swap(piece, "c"))):
-            pieces.append(held)
-            relative.append((dy, dc, 0))
-    return assemble(where, pieces, relative, False)
-
-
-def reduce_rows(partial, order):
-    names = ["y", "z", "x"]
-    for step, axis in enumerate(order):
-        dim = names.index(axis)
-        names.pop(dim)
+def fence(*values):
+    return lax.optimization_barrier(values)
+
+
+class Reduction:
+    def __init__(self, partial, order, names="zyx"):
+        self.partial = partial
+        self.order = order
+        self.names = list(names)
+        self.moved = None
+
+    def send(self):
+        axis, self.order = self.order[0], self.order[1:]
+        dim = self.names.index(axis)
+        self.names.pop(dim)
         here = lax.axis_index(axis)
-        last = step == len(order) - 1
 
         def block(slot):
-            return lax.dynamic_index_in_dim(partial, slot, dim, keepdims=False)
+            return lax.dynamic_index_in_dim(self.partial, slot, dim, keepdims=False)
 
         if axis == "z":
-            moved = [hop(block(here ^ k), k) for k in (1, 2, 3)]
+            self.moved = [hop(block(here ^ k), k) for k in (1, 2, 3)]
         else:
-            moved = [swap(block(1 - here), axis)]
-        total = block(here).astype(F32)
-        for part in moved:
+            self.moved = [swap(block(1 - here), axis)]
+        self.partial = block(here)
+
+    def add(self):
+        total = self.partial.astype(F32)
+        for part in self.moved:
             total = total + part.astype(F32)
-        partial = total if last else total.astype(BF)
-    return partial
+        self.moved = None
+        self.partial = total.astype(BF) if self.order else total
+
+
+def send_all(reductions, *others):
+    reductions = [r for r in reductions if r.order]
+    held = fence(*[r.partial for r in reductions], *others)
+    for reduction, partial in zip(reductions, held):
+        reduction.partial = partial
+        reduction.send()
+    return held[len(reductions) :]
+
+
+def add_all(reductions, *others):
+    reductions = [r for r in reductions if r.moved is not None]
+    flat = [part for r in reductions for part in r.moved]
+    held = fence(*flat, *others)
+    at = 0
+    for reduction in reductions:
+        count = len(reduction.moved)
+        reduction.moved = list(held[at : at + count])
+        at += count
+        reduction.add()
+    held = fence(*[r.partial for r in reductions], *held[at:])
+    for reduction, partial in zip(reductions, held):
+        reduction.partial = partial
+    return held[len(reductions) :]
 
 
 def turn(field, cosine, signed_sine):
@@ -129,123 +153,146 @@
     return field * cosine + other * signed_sine
 
 
-def project_qkv(normed, w_qk, w_vo, cosine, signed_sine, first_value):
+def project_qkv(normed, weights, cosine, signed_sine, first_value):
     rows, width = normed.shape
-
-    def kernel(normed_ref, w_qk_ref, w_vo_ref, cos_ref, sin_ref, *rest):
+    devices = width // 128
+
+    def kernel(normed_ref, w_q_ref, w_k_ref, w_v_ref, cos_ref, sin_ref, *rest):
         out_ref = rest[-1]
         step = pl.program_id(0)
 
-        @pl.when(step < 8)
+        def product(w_ref):
+            return jnp.dot(normed_ref[...], w_ref[...], preferred_element_type=F32)
+
+        def turned(w_ref):
+            field = product(w_ref)
+            for n in range(devices):
+                part = field[:, 128 * n : 128 * n + 128]
+                out_ref[n, 0] = turn(part, cos_ref[...], sin_ref[...]).astype(BF)
+
+        @pl.when(step == 0)
         def _():
-            product = jnp.dot(normed_ref[...], w_qk_ref[...], preferred_element_type=F32)
-            for half in range(2):
-                field = product[:, 128 * half : 128 * half + 128]
-                out_ref[half, 0] = turn(field, cos_ref[...], sin_ref[...]).astype(BF)
-
-        @pl.when(step >= 8)
+            turned(w_q_ref)
+
+        @pl.when(step == 1)
         def _():
-            product = jnp.dot(normed_ref[...], w_vo_ref[...], preferred_element_type=F32)
-            for half in range(2):
-                field = product[:, 128 * half : 128 * half + 128]
+            turned(w_k_ref)
+
+        @pl.when(step == 2)
+        def _():
+            field = product(w_v_ref)
+            for n in range(devices):
+                part = field[:, 128 * n : 128 * n + 128]
                 if first_value is not None:
-                    field = 0.5 * field + 0.5 * rest[0][half, 0].astype(F32)
-                out_ref[half, 0] = field.astype(BF)
+                    part = 0.5 * part + 0.5 * rest[0][n, 0].astype(F32)
+                out_ref[n, 0] = part.astype(BF)
 
     whole = lambda step: (0, 0)
-    in_specs = [
-        pl.BlockSpec((rows, width), whole),
-        pl.BlockSpec((width, 256), lambda step: (0, jnp.minimum(step, 7))),
-        pl.BlockSpec((width, 256), lambda step: (0, jnp.maximum(step - 8, 0))),
-        pl.BlockSpec((rows, 128), whole),
-        pl.BlockSpec((rows, 128), whole),
-    ]
-    operands = [normed, w_qk, w_vo, cosine, signed_sine]
+    in_specs = [pl.BlockSpec((rows, width), whole)]
+    for _, start in weights:
+        in_specs.append(pl.BlockSpec((width, width), lambda step, start=start: (0, start)))
+    in_specs += [pl.BlockSpec((rows, 128), whole)] * 2
+    operands = [normed] + [array for array, _ in weights] + [cosine, signed_sine]
     if first_value is not None:
-        in_specs.append(
-            pl.BlockSpec((2, 1, rows, 128), lambda step: (jnp.maximum(step - 8, 0), 2, 0, 0))
-        )
+        in_specs.append(pl.BlockSpec((devices, 1, rows, 128), lambda step: (0, 2, 0, 0)))
         operands.append(first_value)
     return pl.pallas_call(
         kernel,
-        grid=(12,),
+        grid=(3,),
         in_specs=in_specs,
-        out_specs=pl.BlockSpec((2, 1, rows, 128), lambda step: (step % 4, step // 4, 0, 0)),
-        out_shape=jax.ShapeDtypeStruct((8, 3, rows, 128), BF),
+        out_specs=pl.BlockSpec((devices, 1, rows, 128), lambda step: (0, step, 0, 0)),
+        out_shape=jax.ShapeDtypeStruct((devices, 3, rows, 128), BF),
         compiler_params=params(dimension_semantics=("arbitrary",)),
         name="project_qkv",
     )(*operands)
 
 
-def weight_grad(left_own, left_near, right_own, right_near, tile):
-    rows, depth = left_own.shape
+def weight_grad(core, left_own, left_near, right_own, right_near, tile):
+    rows, width = left_own.shape
     cols = right_own.shape[1]
-
-    def kernel(lo, ln, ro, rn, out_ref, flipped):
+    size = width // 4
+    window = -(-size // 128) * 128
+    slack = window - size
+
+    def kernel(core_ref, lo, ln, ro, rn, out_ref, held, flipped, sems):
         @pl.when(pl.program_id(0) == 0)
         def _():
-            flipped[:, :rows] = lo[...].T
-            flipped[:, rows:] = ln[...].T
-
-        total = jnp.dot(flipped[:, :rows], ro[...], preferred_element_type=F32)
-        total += jnp.dot(flipped[:, rows:], rn[...], preferred_element_type=F32)
-        out_ref[...] = total.astype(BF)
-
-    whole = pl.BlockSpec((rows, depth), lambda n: (0, 0))
+            copies = []
+            for side, ref in enumerate((lo, ln)):
+                for part in range(2):
+                    start = 2 * part * size + core_ref[0] * (size - slack)
+                    span = pl.ds(pl.multiple_of(start, 128), window)
+                    copies.append(
+                        pltpu.make_async_copy(
+                            ref.at[:, span], held.at[side, part], sems.at[side, part]
+                        )
+                    )
+            for copy in copies:
+                copy.start()
+            for copy in copies:
+                copy.wait()
+            for side in range(2):
+                for part in range(2):
+                    flipped[part, :, side * rows : side * rows + rows] = held[side, part].T
+
+        for part in range(2):
+            span = pl.ds(pl.multiple_of(core_ref[0] * slack, 16), size)
+            left = flipped[part, span, :]
+            total = jnp.dot(left[:, :rows], ro[...], preferred_element_type=F32)
+            total += jnp.dot(left[:, rows:], rn[...], preferred_element_type=F32)
+            out_ref[:, part] = total.astype(BF).reshape(4, size // 4, tile)
+
     block = pl.BlockSpec((rows, tile), lambda n: (0, n))
     return pl.pallas_call(
         kernel,
         grid=(cols // tile,),
-        in_specs=[whole, whole, block, block],
-        out_specs=pl.BlockSpec((depth, tile), lambda n: (0, n)),
-        out_shape=jax.ShapeDtypeStruct((depth, cols), BF),
-        scratch_shapes=[pltpu.VMEM((depth, 2 * rows), BF)],
+        in_specs=[SMEM, ANY, ANY, block, block],
+        out_specs=pl.BlockSpec((4, 2, size // 4, tile), lambda n: (0, 0, 0, n)),
+        out_shape=jax.ShapeDtypeStruct((4, 2, size // 4, cols), BF),
+        scratch_shapes=[
+            pltpu.VMEM((2, 2, rows, window), BF),
+            pltpu.VMEM((2, window, 2 * rows), BF),
+            pltpu.SemaphoreType.DMA((2, 2)),
+        ],
         compiler_params=params(dimension_semantics=("arbitrary",)),
         name="weight_grad",
-    )(left_own, left_near, right_own, right_near)
+    )(core, left_own, left_near, right_own, right_near)
 
 
 def rows_of(block):
     return block.reshape(-1, 128)
 
 
-def attend(lengths, pieces):
+def attend(length, pieces):
     tile = 256
-    slots = pieces.shape[3] * 128
+    slots = pieces.shape[2] * 128
     tiles = slots // tile
     per = tile // 128
 
     def kernel(len_ref, piece_ref, out_ref, lse_ref, held, flipped, logit, sems):
-        seq, step = pl.program_id(0), pl.program_id(1)
-
-        def load(which, device):
-            return pltpu.make_async_copy(
-                piece_ref.at[device, :, which],
-                held.at[:, which, :, device],
-                sems.at[which, device],
-            )
-
-        @pl.when((seq == 0) & (step == 0))
+        step = pl.program_id(0)
+
+        @pl.when(step == 0)
         def _():
-            for which in range(2):
-                for device in range(8):
-                    load(which, device).start()
-            for device in range(8):
-                load(0, device).wait()
-
-        @pl.when((seq == 1) & (step == 0))
-        def _():
-            for device in range(8):
-                load(1, device).wait()
+            copies = [
+                pltpu.make_async_copy(
+                    piece_ref.at[device], held.at[:, :, device], sems.at[device]
+                )
+                for device in range(8)
+            ]
+            for copy in copies:
+                copy.start()
+            for copy in copies:
+                copy.wait()
 
         @pl.when(step == 0)
         def _():
             for block in range(tiles):
-                key = rows_of(held[1, seq, pl.ds(per * block, per)])
+                key = rows_of(held[1, pl.ds(per * block, per)])
                 flipped[block] = key.T
 
-        used = len_ref[seq]
-        query = rows_of(held[0, seq, pl.ds(per * step, per)]) * BF(0.125)
+        used = len_ref[0]
+        query = rows_of(held[0, pl.ds(per * step, per)]) * BF(0.125)
         lane = lax.broadcasted_iota(jnp.int32, (tile, 128), 1)
         low = lane < 64
         zero = jnp.zeros_like(query)
@@ -276,7 +323,7 @@
         one = jnp.ones_like(query)
 
         def mix(block, sums):
-            value = rows_of(held[2, seq, pl.ds(per * block, per)])
+            value = rows_of(held[2, pl.ds(per * block, per)])
             values = [jnp.where(low, value, one), jnp.where(low, one, value)]
             result = []
             for head in range(2):
@@ -292,38 +339,38 @@
         out = jnp.where(low, sums[0] / totals[0], sums[1] / totals[1])
         out = out.astype(BF).reshape(per, 8, 16, 128)
         for device in range(8):
-            out_ref[device, seq, pl.ds(per * step, per)] = out[:, device]
+            out_ref[device, pl.ds(per * step, per)] = out[:, device]
         level = jnp.where(low, tops[0] + jnp.log(totals[0]), tops[1] + jnp.log(totals[1])).T
         start = pl.multiple_of(step * tile, tile)
-        lse_ref[seq, 0:1, pl.ds(start, tile)] = level[0:1]
-        lse_ref[seq, 1:2, pl.ds(start, tile)] = level[64:65]
+        lse_ref[0:1, pl.ds(start, tile)] = level[0:1]
+        lse_ref[1:2, pl.ds(start, tile)] = level[64:65]
 
     return pl.pallas_call(
         kernel,
-        grid=(2, tiles),
+        grid=(tiles,),
         in_specs=[SMEM, ANY],
         out_specs=[
-            pl.BlockSpec((8, 2) + pieces.shape[3:], lambda s, i: (0, 0, 0, 0, 0)),
-            pl.BlockSpec((2, 8, slots), lambda s, i: (0, 0, 0)),
+            pl.BlockSpec((8,) + pieces.shape[2:], lambda i: (0, 0, 0, 0)),
+            pl.BlockSpec((8, slots), lambda i: (0, 0)),
         ],
         out_shape=[
-            jax.ShapeDtypeStruct((8, 2) + pieces.shape[3:], BF),
-            jax.ShapeDtypeStruct((2, 8, slots), F32),
+            jax.ShapeDtypeStruct((8,) + pieces.shape[2:], BF),
+            jax.ShapeDtypeStruct((8, slots), F32),
         ],
         scratch_shapes=[
-            pltpu.VMEM((3, 2, slots // 128, 8, 16, 128), BF),
+            pltpu.VMEM((3, slots // 128, 8, 16, 128), BF),
             pltpu.VMEM((tiles, 128, tile), BF),
             pltpu.VMEM((2, tiles, tile, tile), F32),
-            pltpu.SemaphoreType.DMA((2, 8)),
+            pltpu.SemaphoreType.DMA((8,)),
         ],
-        compiler_params=params(dimension_semantics=("arbitrary", "arbitrary")),
+        compiler_params=params(dimension_semantics=("arbitrary",)),
         name="attend",
-    )(lengths, pieces)
-
-
-def attend_back(lengths, pieces, attended, grads, lse, cosine, signed_sine, passed):
+    )(length, pieces)
+
+
+def attend_back(length, pieces, attended, grads, lse, cosine, signed_sine, passed):
     tile = 256
-    slots = pieces.shape[3] * 128
+    slots = pieces.shape[2] * 128
     tiles = slots // tile
     per = tile // 128
     upper = passed is None
@@ -340,46 +387,24 @@
             give_ref = None
             refs = refs[2:]
         held, att, grad, delta, level, query_acc, key_acc, value_acc, sems = refs
-        seq, step = pl.program_id(0), pl.program_id(1)
-        used = len_ref[seq]
-
-        def loads(which):
+        step = pl.program_id(0)
+        used = len_ref[0]
+
+        @pl.when(step == 0)
+        def _():
             copies = []
             for device in range(8):
-                copies.append(
-                    pltpu.make_async_copy(
-                        piece_ref.at[device, :, which],
-                        held.at[:, which, :, device],
-                        sems.at[0, which, device],
+                for n, (source, target) in enumerate(
+                    (
+                        (grad_ref.at[device], grad.at[:, device]),
+                        (att_ref.at[device], att.at[:, device]),
+                        (piece_ref.at[device], held.at[:, :, device]),
                     )
-                )
-                copies.append(
-                    pltpu.make_async_copy(
-                        att_ref.at[device, which],
-                        att.at[which, :, device],
-                        sems.at[1, which, device],
-                    )
-                )
-                copies.append(
-                    pltpu.make_async_copy(
-                        grad_ref.at[device, which],
-                        grad.at[which, :, device],
-                        sems.at[2, which, device],
-                    )
-                )
-            return copies
-
-        @pl.when((seq == 0) & (step == 0))
-        def _():
-            for which in range(2):
-                for copy in loads(which):
-                    copy.start()
-            for copy in loads(0):
-                copy.wait()
-
-        @pl.when((seq == 1) & (step == 0))
-        def _():
-            for copy in loads(1):
+                ):
+                    copies.append(pltpu.make_async_copy(source, target, sems.at[n, device]))
+            for copy in copies:
+                copy.start()
+            for copy in copies:
                 copy.wait()
 
         @pl.when(step == 0)
@@ -390,17 +415,17 @@
             pick = jnp.where(line == lane // 64, 1.0, 0.0).astype(F32)
             for block in range(tiles):
                 span = slice(tile * block, tile * block + tile)
-                product = rows_of(grad[seq, pl.ds(per * block, per)]).astype(F32) * rows_of(
-                    att[seq, pl.ds(per * block, per)]
+                product = rows_of(grad[pl.ds(per * block, per)]).astype(F32) * rows_of(
+                    att[pl.ds(per * block, per)]
                 ).astype(F32)
                 delta[:, span] = lax.dot_general(
                     pick, product, NT, precision=PRECISE, preferred_element_type=F32
                 )
             place = lax.broadcasted_iota(jnp.int32, (8, slots), 1)
-            level[...] = jnp.where(place < used, lse_ref[seq], -NEGATIVE)
-
-        key = rows_of(held[1, seq, pl.ds(per * step, per)])
-        value = rows_of(held[2, seq, pl.ds(per * step, per)])
+            level[...] = jnp.where(place < used, lse_ref[...], -NEGATIVE)
+
+        key = rows_of(held[1, pl.ds(per * step, per)])
+        value = rows_of(held[2, pl.ds(per * step, per)])
         lane = lax.broadcasted_iota(jnp.int32, (tile, 128), 1)
         low = lane < 64
 
@@ -415,8 +440,8 @@
         value_acc[...] = jnp.zeros_like(value_acc)
 
         def visit(block, masked):
-            query = rows_of(held[0, seq, pl.ds(per * block, per)])
-            grad_out = rows_of(grad[seq, pl.ds(per * block, per)])
+            query = rows_of(held[0, pl.ds(per * block, per)])
+            grad_out = rows_of(grad[pl.ds(per * block, per)])
             start = pl.multiple_of(block * tile, tile)
             spans = pl.ds(start, tile)
             query_sum = jnp.zeros((tile, 128), F32)
@@ -461,7 +486,7 @@
         def put(member, block, field):
             field = field.astype(BF).reshape(per, 8, 16, 128)
             for device in range(8):
-                out_ref[device, member, seq, pl.ds(per * block, per)] = field[:, device]
+                out_ref[device, member, pl.ds(per * block, per)] = field[:, device]
 
         start = pl.multiple_of(step * tile, tile)
         spans = pl.ds(start, tile)
@@ -469,10 +494,10 @@
         put(1, step, turn(key_grad, cos_ref[spans, :], -sin_ref[spans, :]))
         if upper:
             half = 0.5 * value_acc[...]
-            give_ref[seq, spans, :] = half
+            give_ref[spans, :] = half
             put(2, step, half)
         else:
-            put(2, step, value_acc[...] + passed_ref[seq, spans, :])
+            put(2, step, value_acc[...] + passed_ref[spans, :])
 
         @pl.when(step == tiles - 1)
         def _():
@@ -480,45 +505,36 @@
                 part = slice(tile * block, tile * block + tile)
                 put(0, block, turn(query_acc[part, :], cos_ref[part, :], -sin_ref[part, :]))
 
-    flat = lambda s, i: (0, 0)
-    cube = lambda s, i: (0, 0, 0)
-    in_specs = [
-        SMEM,
-        ANY,
-        ANY,
-        ANY,
-        pl.BlockSpec((2, 8, slots), cube),
-        pl.BlockSpec((slots, 128), flat),
-        pl.BlockSpec((slots, 128), flat),
-    ]
-    operands = [lengths, pieces, attended, grads, lse, cosine, signed_sine]
-    out_specs = [pl.BlockSpec(pieces.shape, lambda s, i: (0, 0, 0, 0, 0, 0))]
+    flat = lambda i: (0, 0)
+    table = pl.BlockSpec((slots, 128), flat)
+    in_specs = [SMEM, ANY, ANY, ANY, pl.BlockSpec((8, slots), flat), table, table]
+    operands = [length, pieces, attended, grads, lse, cosine, signed_sine]
+    out_specs = [pl.BlockSpec(pieces.shape, lambda i: (0, 0, 0, 0, 0))]
     out_shape = [jax.ShapeDtypeStruct(pieces.shape, BF)]
-    carried = pl.BlockSpec((2, slots, 128), cube)
     if upper:
-        out_specs.append(carried)
-        out_shape.append(jax.ShapeDtypeStruct((2, slots, 128), F32))
+        out_specs.append(table)
+        out_shape.append(jax.ShapeDtypeStruct((slots, 128), F32))
     else:
-        in_specs.append(carried)
+        in_specs.append(table)
         operands.append(passed)
     outs = pl.pallas_call(
         kernel,
-        grid=(2, tiles),
+        grid=(tiles,),
         in_specs=in_specs,
         out_specs=out_specs,
         out_shape=out_shape,
         scratch_shapes=[
-            pltpu.VMEM((3, 2, slots // 128, 8, 16, 128), BF),
-            pltpu.VMEM((2, slots // 128, 8, 16, 128), BF),
-            pltpu.VMEM((2, slots // 128, 8, 16, 128), BF),
+            pltpu.VMEM((3, slots // 128, 8, 16, 128), BF),
+            pltpu.VMEM((slots // 128, 8, 16, 128), BF),
+            pltpu.VMEM((slots // 128, 8, 16, 128), BF),
             pltpu.VMEM((8, slots), F32),
             pltpu.VMEM((8, slots), F32),
             pltpu.VMEM((slots, 128), F32),
             pltpu.VMEM((tile, 128), F32),
             pltpu.VMEM((tile, 128), F32),
-            pltpu.SemaphoreType.DMA((3, 2, 8)),
+            pltpu.SemaphoreType.DMA((3, 8)),
         ],
-        compiler_params=params(dimension_semantics=("arbitrary", "arbitrary")),
+        compiler_params=params(dimension_semantics=("arbitrary",)),
         name="attend_back",
     )(*operands)
     return outs if upper else (outs[0], None)
@@ -911,42 +927,94 @@
     lane = c * 4 + y * 2 + x
     where = jnp.stack([y, c, z, x]).astype(jnp.int32)
     rows = seqs * stretch
-
-    def to_plane(field):
-        field = jnp.transpose(field.reshape(seqs, 2, 8, 16, width), (2, 0, 1, 3, 4))
-        field = lax.all_to_all(field, PLANE, 0, 0, tiled=True)
-        field = lax.all_to_all(field.reshape((4, 2) + field.shape[1:]), "z", 0, 0, tiled=True)
-        return jnp.transpose(field.reshape(8, seqs, 2, 16, width), (1, 0, 2, 3, 4)).reshape(rows, width)
-
-    def from_plane(field):
-        field = jnp.transpose(field.reshape(seqs, 8, 2, 16, width), (1, 0, 2, 3, 4))
-        field = lax.all_to_all(field.reshape((4, 2) + field.shape[1:]), "z", 0, 0, tiled=True)
-        field = lax.all_to_all(field.reshape(8, seqs, 2, 16, width), PLANE, 0, 0, tiled=True)
+    ffn = w_gate.shape[2]
+
+    def exchange(field):
+        return lax.all_to_all(field, PLANE, 0, 0, tiled=True)
+
+    def exchange_z(field):
+        shape = field.shape
+        moved = lax.all_to_all(field.reshape((4, 2) + shape[1:]), "z", 0, 0, tiled=True)
+        return moved.reshape(shape)
+
+    def cut_blocks(field):
+        field = field.reshape(seqs, 2, 8, 16, width)
+        return jnp.transpose(field, (2, 0, 1, 3, 4))
+
+    def join_stripes(field):
+        return jnp.transpose(field, (1, 0, 2, 3, 4)).reshape(rows, width)
+
+    def cut_stripes(field):
+        return jnp.transpose(field.reshape(seqs, 8, 2, 16, width), (1, 0, 2, 3, 4))
+
+    def join_blocks(field):
         return jnp.transpose(field, (1, 2, 0, 3, 4)).reshape(seqs, stretch, width)
 
-    def gather_attn(layer):
+    def gather_all(shard):
+        return lax.all_gather(shard, ALL, axis=0, tiled=True)
+
+    def gain_shard(layer):
         gain = jnp.stack([norm_attn[layer], norm_ffn[layer]], axis=1)
-        gain = jnp.pad(gain, ((0, 0), (0, 126)))
-        shard = jnp.concatenate([w_qkv[layer, :, : 2 * width], gain], axis=1)
-        w_qk = gather_z_first(where, shard, "x", "y")
-        shard = jnp.concatenate([w_qkv[layer, :, 2 * width :], w_out[layer]], axis=1)
-        w_vo = gather_z_first(where, shard, "y", "x")
-        gain = jnp.transpose(w_qk[:, 2 * width : 2 * width + 128])[:2].astype(F32)
-        return w_qk, w_vo, gain
-
-    def gather_ffn(layer):
-        shard = jnp.concatenate([w_gate[layer], w_up[layer]], axis=1)
-        w_gu = gather_z_first(where, shard, "y", "x")
-        w_d = gather_x_first(where, w_down[layer])
-        return w_gu, w_d
-
-    route = []
-    for sy in range(2):
-        for sc in range(2):
-            for sb in range(8):
-                ty, tc, tx = (sb >> 1) & 1, sb >> 2, sb & 1
-                route.append(((sy * 2 + sc) * 8 + sb, ((ty * 2 + tc) * 4 + 2 * sc + sy) * 2 + tx))
-    lengths = lax.ppermute(seq_lens, ALL, route)[0]
+        return jnp.pad(gain, ((0, 0), (0, 126)))
+
+    def gains(columns):
+        return jnp.transpose(columns)[:2].astype(F32)
+
+    def gather_ffn(layer, *after):
+        cuts = [w_gate[layer], w_up[layer], pack(w_down[layer])]
+        if layer == 0:
+            cuts.append(w_out[layer])
+        shard = jnp.concatenate(cuts, axis=1)
+        if after:
+            shard, *_ = fence(shard, *after)
+        gathered = gather_all(shard)
+        packed = gathered[:, 2 * ffn : 2 * ffn + 3 * width]
+        w_d = unpack(packed.reshape(32, -1, 3 * width)).reshape(-1, width)
+        return gathered, w_d
+
+    def pack(rows_of_down):
+        tall = w_qkv.shape[1]
+        spare = 3 * tall - rows_of_down.shape[-2]
+        lead = [(0, 0)] * (rows_of_down.ndim - 2)
+        padded = jnp.pad(rows_of_down, lead + [(0, spare), (0, 0)])
+        cuts = [padded[..., n * tall : n * tall + tall, :] for n in range(3)]
+        return jnp.concatenate(cuts, axis=-1)
+
+    def unpack(packed):
+        cols = packed.shape[-1] // 3
+        cuts = [packed[..., n * cols : n * cols + cols] for n in range(3)]
+        return jnp.concatenate(cuts, axis=-2)[..., : w_down.shape[1], :]
+
+    def gather_first():
+        shard = w_qkv[0]
+        first = jnp.concatenate([shard[:, :width], gain_shard(0)], axis=1)
+        w_q = gather_z_first(where, first, "x", "y")
+        w_k = gather_z_first(where, shard[:, width : 2 * width], "y", "x")
+        w_v = gather_z_first(where, shard[:, 2 * width :], "x", "y")
+        weights = [(w_q, 0), (w_k, 0), (w_v, 0)]
+        return weights, [w_q[:, :width], w_k, w_v], gains(w_q[:, width:])
+
+    def gather_second(*after):
+        shard = jnp.concatenate([w_qkv[1], w_out[1], gain_shard(1)], axis=1)
+        shard, *_ = fence(shard, *after)
+        whole = gather_all(shard)
+        weights = [(whole, 0), (whole, 1), (whole, 2)]
+        turned = [whole[:, : 3 * width]]
+        return weights, turned, whole[:, 3 * width : 4 * width], gains(whole[:, 4 * width :])
+
+    here = z * 2 + x
+    routes = []
+    for k in range(8):
+        route = []
+        for sy in range(2):
+            for sc in range(2):
+                for sb in range(8):
+                    to = sb ^ k
+                    target = (((to >> 1) & 1) * 2 + (to >> 2)) * 4 + 2 * sc + sy
+                    route.append(((sy * 2 + sc) * 8 + sb, target * 2 + (to & 1)))
+        routes.append(route)
+    lengths = lax.ppermute(seq_lens, ALL, routes[0])[0]
+    length = [lengths[n : n + 1] for n in range(2)]
     slots = stretch * 8
     half_dim = width // HEADS // 2
     freqs = 10000.0 ** (-jnp.arange(half_dim, dtype=F32) / half_dim)
@@ -959,147 +1027,269 @@
         own = lax.dynamic_index_in_dim(
             table.reshape(slots // 128, 8, 16, 128), lane, 1, keepdims=False
         )
-        return jnp.concatenate([own.reshape(stretch, 128)] * seqs)
+        return own.reshape(stretch, 128)
 
     my_cos, my_sin = mine(cosine), mine(sine)
     step = jnp.arange(stretch, dtype=jnp.int32)
     places = (step // 16) * 128 + lane * 16 + step % 16
     valid = (places[None, :] < lengths[:, None]).astype(F32).reshape(rows, 1)
 
-    def exchange(field):
-        return lax.all_to_all(field, PLANE, 0, 0, tiled=True)
-
-    def forward_layer(inputs, layer, w_attn, w_ffn, first_value):
-        w_qk, w_vo, gain_all = w_attn
+    def halves(field):
+        return field[:stretch], field[stretch:]
+
+    def forward_attention(inputs, weights, gain, first_value, *after):
+        rms_one = lax.rsqrt(jnp.mean(inputs * inputs, axis=-1, keepdims=True) + EPSILON)
+        normed = (inputs * rms_one * gain[0]).astype(BF)
+        top, bottom = halves(normed)
+        parts_a = project_qkv(top, weights, my_cos, my_sin, first_value and first_value[0])
+        parts_b = project_qkv(bottom, weights, my_cos, my_sin, first_value and first_value[1])
+        shape = (8, 3, stretch // 16, 16, 128)
+        pieces_a = exchange(parts_a)
+        pieces_a, sent_b = fence(pieces_a, parts_b)
+        pieces_a = pieces_a.reshape(shape)
+        pieces_b = exchange(sent_b)
+        attended_a, lse_a = attend(length[0], pieces_a)
+        attended_a, pieces_b, *_ = fence(attended_a, pieces_b, *after)
+        pieces_b = pieces_b.reshape(shape)
+        low_a = exchange(attended_a.reshape(8, stretch, 128))
+        attended_b, lse_b = attend(length[1], pieces_b)
+        low_a, sent_b = fence(low_a, attended_b)
+        low_b = exchange(sent_b.reshape(8, stretch, 128))
+        attn_low = jnp.concatenate(
+            [jnp.transpose(low, (1, 0, 2)).reshape(stretch, width) for low in (low_a, low_b)]
+        )
+        kept = (
+            inputs, rms_one, normed, (pieces_a, pieces_b), (attended_a, attended_b), attn_low,
+            (lse_a, lse_b),
+        )
+        return attn_low, (parts_a, parts_b), kept
+
+    def forward_ffn(inputs, attn_low, w_o, w_ffn, gain):
         w_gu, w_d = w_ffn
-        ffn = w_gu.shape[1] // 2
-        rms_one = lax.rsqrt(jnp.mean(inputs * inputs, axis=-1, keepdims=True) + EPSILON)
-        normed = (inputs * rms_one * gain_all[0]).astype(BF)
-        parts = project_qkv(normed, w_qk, w_vo, my_cos, my_sin, first_value)
-        pieces = exchange(parts).reshape(8, 3, seqs, stretch // 16, 16, 128)
-        attended, lse = attend(lengths, pieces)
-        attn_low = exchange(attended.reshape(8, rows, 128))
-        attn_low = jnp.transpose(attn_low, (1, 0, 2)).reshape(rows, width)
-        middle = inputs + jnp.dot(attn_low, w_vo[:, width:], preferred_element_type=F32)
+        middle = inputs + jnp.dot(attn_low, w_o, preferred_element_type=F32)
         rms_two = lax.rsqrt(jnp.mean(middle * middle, axis=-1, keepdims=True) + EPSILON)
-        normed_two = (middle * rms_two * gain_all[1]).astype(BF)
+        normed_two = (middle * rms_two * gain[1]).astype(BF)
         gate = jnp.dot(normed_two, w_gu[:, :ffn], preferred_element_type=F32)
-        up = jnp.dot(normed_two, w_gu[:, ffn:], preferred_element_type=F32)
+        up = jnp.dot(normed_two, w_gu[:, ffn : 2 * ffn], preferred_element_type=F32)
         hidden = (jax.nn.silu(gate) * up).astype(BF)
         result = middle + jnp.dot(hidden, w_d, preferred_element_type=F32)
-        kept = (
-            inputs, rms_one, normed, pieces, attended, attn_low, lse, middle, rms_two,
-            normed_two, gate, up, hidden,
-        )
-        return result, parts, kept
-
-    def own_half(field):
-        view = field.reshape(rows, 2, 2, -1)
-        own = lax.dynamic_index_in_dim(view, c, 2, keepdims=False).reshape(rows, -1)
-        other = lax.dynamic_index_in_dim(view, 1 - c, 2, keepdims=False).reshape(rows, -1)
-        return own, swap(other, "c")
-
-    def row_grad(left, right, right_near, tile):
-        own, near = own_half(left)
-        grad = weight_grad(own, near, right, right_near, tile)
-        return grad.reshape(2, 4, 2, -1, grad.shape[1])
+        return result, (middle, rms_two, normed_two, gate, up, hidden)
+
+    def near(field):
+        return swap(field, "c")
 
     def norm_back(grad_normed, source, rms, gain):
         scaled = source * rms
-        grad_gain = jnp.sum(grad_normed * scaled, axis=0)
         weighted = grad_normed * gain
-        grad = rms * (weighted - scaled * jnp.mean(weighted * scaled, axis=-1, keepdims=True))
-        return grad, grad_gain
-
-    def backward_layer(grad_in, layer, w_attn, w_ffn, kept, passed):
-        w_qk, w_vo, gain_all = w_attn
+        return rms * (weighted - scaled * jnp.mean(weighted * scaled, axis=-1, keepdims=True))
+
+    def chip_grad(left, right, tile):
+        grad = weight_grad(core, left[0], left[1], right[0], right[1], tile)
+        return grad.reshape(4, 2, 2, -1, grad.shape[-1])
+
+    def start_sum(left, right, tile, order):
+        return Reduction(chip_grad(left, right, tile), order)
+
+    def dots(grads, weights):
+        total = None
+        for grad, weight in zip(grads, weights):
+            part = lax.dot_general(grad, weight, NT, preferred_element_type=F32)
+            total = part if total is None else total + part
+        return total
+
+    def qkv_sums(one, proj):
+        half = 3 * width // 2
+        sums = []
+        for lo, order in ((0, "yxz"), (half, "xyz")):
+            right = (proj[0][:, lo : lo + half], proj[1][:, lo : lo + half])
+            sums.append(start_sum(one, right, 512, order))
+        return sums
+
+    def ffn_grads(two, gates, ups, hid, low):
+        grads = [chip_grad(two, gates, 256), chip_grad(two, ups, 256)]
+        return jnp.concatenate(grads + [pack(chip_grad(hid, low, 512))], axis=-1)
+
+    def backward_layer(grad_in, w_attn, w_ffn, kept, passed, pending, upper_sum, beside):
+        w_turned, w_o, gain = w_attn
         w_gu, w_d = w_ffn
-        ffn = w_gu.shape[1] // 2
         (
             inputs, rms_one, normed, pieces, attended, attn_low, lse, middle, rms_two,
             normed_two, gate, up, hidden,
         ) = kept
         grad_low = grad_in.astype(BF)
-        near_low = swap(grad_low, "c")
+        low = (grad_low, near(grad_low))
+        hid = (hidden, near(hidden))
+        two = (normed_two, near(normed_two))
+        att = (attn_low, near(attn_low))
+        one = (normed, near(normed))
         grad_hidden = lax.dot_general(grad_low, w_d, NT, preferred_element_type=F32)
         sigma = jax.nn.sigmoid(gate)
         grad_gate = (grad_hidden * up * sigma * (1.0 + gate * (1.0 - sigma))).astype(BF)
         grad_up = (grad_hidden * gate * sigma).astype(BF)
-        near_gate, near_up = swap(grad_gate, "c"), swap(grad_up, "c")
-        down = reduce_rows(row_grad(hidden, grad_low, near_low, 512).reshape(2, 4, 2, -1, width), "yzx")
-        gates = reduce_rows(row_grad(normed_two, grad_gate, near_gate, 256), "xyz")
-        ups = reduce_rows(row_grad(normed_two, grad_up, near_up, 256), "yxz")
-        grad_normed = lax.dot_general(
-            grad_gate, w_gu[:, :ffn], NT, preferred_element_type=F32
-        ) + lax.dot_general(grad_up, w_gu[:, ffn:], NT, preferred_element_type=F32)
-        grad, gain_two = norm_back(grad_normed, middle, rms_two, gain_all[1])
-        grad_middle = grad_in + grad
+        gates = (grad_gate, near(grad_gate))
+        ups = (grad_up, near(grad_up))
+        if upper_sum is not None:
+            summed = ffn_grads(two, gates, ups, hid, low)
+            summed, grad_gate, grad_up = add_all(pending, summed, grad_gate, grad_up)
+            summed, grad_gate, grad_up = send_all(pending, summed, grad_gate, grad_up)
+            summed = lax.psum_scatter(summed, "z", scatter_dimension=0, tiled=True)[0]
+        grad_normed = dots([grad_gate, grad_up], [w_gu[:, :ffn], w_gu[:, ffn : 2 * ffn]])
+        grad_middle = grad_in + norm_back(grad_normed, middle, rms_two, gain[1])
         grad_attn = grad_middle.astype(BF)
-        near_attn = swap(grad_attn, "c")
-        out = reduce_rows(row_grad(attn_low, grad_attn, near_attn, 512), "xyz")
-        grad_o = lax.dot_general(
-            grad_attn, w_vo[:, width:], NT, preferred_element_type=F32
-        ).astype(BF)
+        mid = (grad_attn, near(grad_attn))
+        grad_o = lax.dot_general(grad_attn, w_o, NT, preferred_element_type=F32).astype(BF)
         grad_o = jnp.transpose(grad_o.reshape(rows, 8, 128), (1, 0, 2))
-        grad_o = exchange(grad_o).reshape(attended.shape)
-        parts, passed = attend_back(
-            lengths, pieces, attended, grad_o, lse, cosine, sine, passed
-        )
-        parts = exchange(parts.reshape(8, 3, rows, 128))
-        grad_proj = jnp.transpose(parts, (2, 1, 0, 3)).reshape(rows, 3 * width)
-        near_proj = swap(grad_proj, "c")
-        half = 3 * width // 2
-        left, near_left = own_half(normed)
-
-        def qkv_grad(lo, order):
-            grad = weight_grad(
-                left, near_left, grad_proj[:, lo : lo + half], near_proj[:, lo : lo + half], 512
-            )
-            return reduce_rows(grad.reshape(2, 4, 2, -1, half), order)
-
-        qkv = jnp.concatenate([qkv_grad(0, "yxz"), qkv_grad(half, "xyz")], axis=1)
-        grad_normed = lax.dot_general(
-            grad_proj[:, : 2 * width], w_qk[:, : 2 * width], NT, preferred_element_type=F32
-        ) + lax.dot_general(
-            grad_proj[:, 2 * width :], w_vo[:, :width], NT, preferred_element_type=F32
-        )
-        grad, gain_one = norm_back(grad_normed, inputs, rms_one, gain_all[0])
-        return grad_middle + grad, (gain_one, qkv, out, gain_two, gates, ups, down), passed
-
-    state = to_plane(tokens).astype(F32)
-    attn_one = gather_attn(0)
+        grad_o, beside = fence(grad_o, beside)
+
+        if upper_sum is None:
+            held = fence(grad_o, *two, *gates, *ups, *hid, *low)
+            grad_o, two, gates, ups = held[0], held[1:3], held[3:5], held[5:7]
+            hid, low = held[7:9], held[9:11]
+            grad_o = exchange(grad_o)
+            summed = ffn_grads(two, gates, ups, hid, low)
+            summed, grad_o = fence(summed, grad_o)
+            summed = lax.psum_scatter(summed, "z", scatter_dimension=0, tiled=True)[0]
+        else:
+            grad_o = exchange(grad_o)
+        (grad_o,) = add_all(pending, grad_o)
+        if upper_sum is not None:
+            upper_sum, grad_o = fence(upper_sum, grad_o)
+            half = upper_sum.shape[-1] // 2
+            pending.append(Reduction(upper_sum[..., :half], "xy", "yx"))
+            pending.append(Reduction(upper_sum[..., half:], "yx", "yx"))
+        (grad_o,) = send_all(pending, grad_o)
+        grad_o = grad_o.reshape(8, 2, stretch // 16, 16, 128)
+        cos_sin = (cosine, sine)
+        parts_a, pass_a = attend_back(
+            length[0], pieces[0], attended[0], grad_o[:, 0], lse[0], *cos_sin, passed and passed[0]
+        )
+        parts_a, grad_b = fence(parts_a, grad_o[:, 1])
+        if upper_sum is not None:
+            parts_a, grad_b = add_all(pending[3:], parts_a, grad_b)
+            parts_a, grad_b = send_all(pending[3:], parts_a, grad_b)
+        moved_a = exchange(parts_a.reshape(8, 3, stretch, 128))
+        parts_b, pass_b = attend_back(
+            length[1], pieces[1], attended[1], grad_b, lse[1], *cos_sin, passed and passed[1]
+        )
+        moved_a, parts_b, *held = fence(moved_a, parts_b, *att, *mid)
+        att, mid = held[:2], held[2:4]
+        moved_b = exchange(parts_b.reshape(8, 3, stretch, 128))
+        out = start_sum(att, mid, 512, "xyz")
+        if upper_sum is not None:
+            summed, moved_b = add_all(pending, summed, moved_b)
+            half = summed.shape[-1] // 2
+            summed = [
+                Reduction(summed[..., :half], "xy", "yx"),
+                Reduction(summed[..., half:], "yx", "yx"),
+            ]
+            (moved_b,) = send_all([out] + summed, moved_b)
+        else:
+            (moved_b,) = send_all([out], moved_b)
+        grad_proj = jnp.concatenate(
+            [
+                jnp.transpose(moved, (2, 1, 0, 3)).reshape(stretch, 3 * width)
+                for moved in (moved_a, moved_b)
+            ]
+        )
+        proj = (grad_proj, near(grad_proj))
+        cuts, at = [], 0
+        for weight in w_turned:
+            cuts.append(grad_proj[:, at : at + weight.shape[1]])
+            at += weight.shape[1]
+        grad_normed = dots(cuts, w_turned)
+        grad = grad_middle + norm_back(grad_normed, inputs, rms_one, gain[0])
+        return grad, summed, out, one + proj, (pass_a, pass_b), beside
+
+    core = c.astype(jnp.int32).reshape(1)
     ffn_one = gather_ffn(0)
-    attn_two = gather_attn(1)
-    ffn_two = gather_ffn(1)
-    grad = to_plane(cotangent).astype(F32) * valid
-    middle, first_value, kept_one = forward_layer(state, 0, attn_one, ffn_one, None)
-    final, _, kept_two = forward_layer(middle, 1, attn_two, ffn_two, first_value)
-    layer_out = from_plane(final.astype(BF))
-    grad, grads_two, passed = backward_layer(grad, 1, attn_two, ffn_two, kept_two, None)
-    grad, grads_one, _ = backward_layer(grad, 0, attn_one, ffn_one, kept_one, passed)
-    input_grad = from_plane(grad.astype(BF)).astype(F32)
-
-    sums = jnp.stack([grads_one[0], grads_two[0], grads_one[3], grads_two[3]])
-    sums = sums + swap(sums, "c")
-    sums = sums + swap(sums, "x")
-    sums = sums + swap(sums, "y")
-    sums = sums + hop(sums, 1)
-    sums = sums + hop(sums, 2)
-    sums = sums.reshape(4, 32, width // 32)
-    mine_sums = lax.dynamic_index_in_dim(
-        sums, ((y * 2 + c) * 4 + z) * 2 + x, 1, keepdims=False
+    state = join_stripes(exchange_z(exchange(cut_blocks(tokens)))).astype(F32)
+    qkv_one, turned_one, gain_one = gather_first()
+    low_one, first_value, kept_one = forward_attention(
+        state, qkv_one, gain_one, None, ffn_one[0]
     )
-    pairs = [jnp.stack([one, two]) for one, two in zip(grads_one, grads_two)]
+    qkv_two, turned_two, out_two, gain_two = gather_second(ffn_one[0], kept_one[4][0])
+    ffn_two = gather_ffn(1, low_one)
+    out_one = ffn_one[0][:, 2 * ffn + 3 * width :]
+    low_one, other = fence(low_one, cut_blocks(cotangent))
+    other = [
+        lax.ppermute(lax.dynamic_index_in_dim(other, here ^ k, 0, keepdims=False), ALL, routes[k])
+        for k in range(8)
+    ]
+    middle, more = forward_ffn(state, low_one, out_one, ffn_one, gain_one)
+    kept_one += more
+    low_two, _, kept_two = forward_attention(middle, qkv_two, gain_two, first_value)
+    final, more = forward_ffn(middle, low_two, out_two, ffn_two, gain_two)
+    kept_two += more
+    final, *other = fence(final, *other)
+    grad = jnp.zeros((8, seqs, 2, 16, width), BF)
+    for k in range(8):
+        grad = lax.dynamic_update_index_in_dim(grad, other[k], lane ^ k, 0)
+    grad = join_stripes(grad).astype(F32) * valid
+    layer_out = exchange_z(cut_stripes(final.astype(BF)))
+    grad, ffn_two_sum, out_sum, todo, passed, layer_out = backward_layer(
+        grad, (turned_two, out_two, gain_two), ffn_two, kept_two, None, [], None, layer_out
+    )
+    grad, *todo = fence(grad, *todo)
+    sums_two = [out_sum] + qkv_sums(todo[:2], todo[2:])
+    grad, layer_out = send_all(sums_two[1:], grad, layer_out)
+    layer_out = exchange(layer_out)
+    grad, ffn_one_sum, out_sum, todo, _, layer_out = backward_layer(
+        grad,
+        (turned_one, out_one, gain_one),
+        ffn_one,
+        kept_one,
+        passed,
+        sums_two,
+        ffn_two_sum,
+        layer_out,
+    )
+    layer_out = join_blocks(layer_out)
+    grad, *todo = fence(grad, *todo)
+    input_grad = exchange_z(cut_stripes(grad.astype(BF)))
+    last = qkv_sums(todo[:2], todo[2:])
+    (input_grad,) = send_all(last, input_grad)
+    input_grad = exchange(input_grad)
+    rest = ffn_one_sum + [out_sum]
+    add_all(rest, *[r.partial for r in last])
+    send_all(rest)
+    for _ in range(2):
+        add_all(last)
+        send_all(last)
+        add_all(rest, *[r.partial for r in last])
+        send_all(rest)
+    add_all(last + rest)
+    input_grad = join_blocks(input_grad).astype(F32)
+    sums_one = [out_sum] + last
+    sums_two, late, lower = sums_two[:3], sums_two[3:], ffn_one_sum
+
+    out_grad, qkv_grad, gate_grad, up_grad, down_grad = [], [], [], [], []
+    for sums, halves_of in ((sums_one, lower), (sums_two, late)):
+        out_grad.append(sums[0].partial)
+        qkv_grad.append(jnp.concatenate([sums[1].partial, sums[2].partial], axis=1))
+        field = jnp.concatenate([r.partial for r in halves_of], axis=1)
+        gate_grad.append(field[:, :ffn])
+        up_grad.append(field[:, ffn : 2 * ffn])
+        down_grad.append(unpack(field[:, 2 * ffn :]))
+
+    def gain_grad(pairs, gain):
+        total = sum(jnp.sum(w.astype(F32) * grad, axis=1) for w, grad in pairs)
+        return total / gain.astype(F32)
+
+    attn_gain = [gain_grad([(w_qkv[n], qkv_grad[n])], norm_attn[n]) for n in range(2)]
+    ffn_gain = [
+        gain_grad([(w_gate[n], gate_grad[n]), (w_up[n], up_grad[n])], norm_ffn[n])
+        for n in range(2)
+    ]
     return (
         layer_out,
         input_grad,
-        mine_sums[:2],
-        pairs[1],
-        pairs[2],
-        mine_sums[2:],
-        pairs[4],
-        pairs[5],
-        pairs[6],
+        jnp.stack(attn_gain),
+        jnp.stack(qkv_grad),
+        jnp.stack(out_grad),
+        jnp.stack(ffn_gain),
+        jnp.stack(gate_grad),
+        jnp.stack(up_grad),
+        jnp.stack(down_grad),
     )
 
 

time: 1430 us -> 1110 us (0.78)
  waiting for transfers between devices: 457 us -> 230 us
  starting transfers between devices: 269 us -> 222 us
  local copies, waits for them, and re-layouts: 188 us -> 149 us
  Pallas kernels: 310 us -> 290 us
    ppermute x95 -> x59, waiting for transfers between devices: 326 us -> 78.3 us  [swap(): return lax.ppermute(value, axis, [(0, 1), (1, 0)])]
    ppermute x62 -> x27, waiting for transfers between devices: 125 us -> 19.1 us  [hop(): return lax.ppermute(value, 'z', [(i, i ^ offset) for i in range(4)])]
    all_to_all x8 -> x17, waiting for transfers between devices: 5.67 us -> 75.9 us  [exchange(): return lax.all_to_all(field, PLANE, 0, 0, tiled=True)]
    ppermute x62 -> x27, starting transfers between devices: 130 us -> 60.6 us  [hop(): return lax.ppermute(value, 'z', [(i, i ^ offset) for i in range(4)])]
    all_to_all x8 -> x17, starting transfers between devices: 36.3 us -> 85.9 us  [exchange(): return lax.all_to_all(field, PLANE, 0, 0, tiled=True)]
    all_gather x0 -> x3, waiting for transfers between devices: none -> 47.7 us  [gather_all(): return lax.all_gather(shard, ALL, axis=0, tiled=True)]
    pallas_call x8 -> x3, Pallas kernels: 61.4 us -> 15.8 us  [assemble(): pl.pallas_call(kernel, in_specs=[SMEM] + [ANY] * count, out_specs=ANY, ou...]
    dynamic_slice x18 -> x0, local copies, waits for them, and re-layouts: 37.6 us -> none  [the longest x9 27.2 us: own_half(): lax.dynamic_index_in_dim(view, 1 - c, 2, keepdims=False).reshape(rows, -1)]
  transfers between devices with their start and end apart: 174 -> 120, of which waited for: 47 -> 36; matrix products, arithmetic and copies ran while one was open for 22% -> 25% of each run, Pallas kernels for 22% -> 25%
where the time goes in v2:
time: 1110 us; the launch traced here: 1100 us
  Pallas kernels  290 us (26%)
  waiting for transfers between devices  230 us (21%)
  starting transfers between devices  222 us (20%)
  local copies, waits for them, and re-layouts  149 us (13%)
  matrix products  113 us (10%)
  other arithmetic  78.5 us (7%)
  between operations  16.8 us (2%)
    pallas_call x12, Pallas kernels, weight_grad(): pl.pallas_call(kernel, grid=(cols // tile,), in_specs=[SMEM, ANY, ANY, bl...  89.6 us
    all_to_all x17, starting transfers between devices, exchange(): return lax.all_to_all(field, PLANE, 0, 0, tiled=True)  85.9 us
    pallas_call x4, Pallas kernels, attend(): pl.pallas_call(kernel, grid=(tiles,), in_specs=[SMEM, ANY], out_specs=[pl...  85 us
    ppermute x59, waiting for transfers between devices, swap(): return lax.ppermute(value, axis, [(0, 1), (1, 0)])  78.3 us
    all_to_all x17, waiting for transfers between devices, exchange(): return lax.all_to_all(field, PLANE, 0, 0, tiled=True)  75.9 us
    pallas_call x4, Pallas kernels, attend_back(): pl.pallas_call(kernel, grid=(tiles,), in_specs=in_specs, out_specs=out_sp...  73.1 us
    unnamed x384, local copies, waits for them, and re-layouts  63.1 us
    ppermute x27, starting transfers between devices, hop(): return lax.ppermute(value, 'z', [(i, i ^ offset) for i in range(4)])  60.6 us
  transfers between devices with their start and end apart: 120, of which 36 were waited for; matrix products, arithmetic and copies ran while one was open for 25% of the time, Pallas kernels for 25%

profile of v2, /device:TPU:0, one launch (start us, length us, event | category | flops | bytes accessed | tf_op | source)
XLA Modules:
  0.0 1098.9 jit_solution(8479408100794197422)
XLA Ops:
  68.4 8.8 collective-permute-done.29.rest_6_
  127.1 15.6 %all-to-all-start.2 = ((bf16[8,3,256,128]{3,2,1,0:T(8,128)(2,1)}), bf16[8,3,256,128]{3,2,1,0:T(8,128)(2,1)S(1)}, u32[]{:S(2)}, u32[]{:S(2)}) async-start(bf16[8,3,256,128]{3,2,1,0:T(8,128)(2,1)} %project_qkv.4.rest_0_), calls=%async_computation.2 | async-start | bytes 3145728 | tf_op jit(solution)/shard_map/all_to_all | solution.py:933
  149.3 19.8 %all-to-all-done.2 = bf16[8,3,256,128]{3,2,1,0:T(8,128)(2,1)S(1)} async-done(((bf16[8,3,256,128]{3,2,1,0:T(8,128)(2,1)}), bf16[8,3,256,128]{3,2,1,0:T(8,128)(2,1)S(1)}, u32[]{:S(2)}, u32[]{:S(2)}) %all-to-all-start.2) | async-done | bytes 1572896 | tf_op jit(solution)/shard_map/all_to_all | solution.py:933
  177.0 20.8 %attend.4 = (bf16[8,16,16,128]{3,2,1,0:T(8,128)(2,1)S(1)}, f32[8,2048]{1,0:T(8,128)S(1)}) custom-call(s32[1]{0:T(128)} %bitcast.7.len_ref.refs_0_, bf16[8,3,16,16,128]{4,3,2,1,0:T(8,128)(2,1)S(1)} %bitcast.474), custom_call_target="tpu_custom_call" | custom-call | tf_op jit(solution)/shard_map/attend/pallas_call | solution.py:348
  198.7 8.0 all-to-all-start.4
  206.7 20.1 %attend.5 = (bf16[8,16,16,128]{3,2,1,0:T(8,128)(2,1)}, f32[8,2048]{1,0:T(8,128)S(1)}) custom-call(s32[1]{0:T(128)} %bitcast.42.len_ref.refs_0_, bf16[8,3,16,16,128]{4,3,2,1,0:T(8,128)(2,1)S(1)} %bitcast.472), custom_call_target="tpu_custom_call" | custom-call | tf_op jit(solution)/shard_map/attend/pallas_call | solution.py:348
  231.8 13.4 %all-to-all-done.5 = bf16[8,256,128]{2,1,0:T(8,128)(2,1)S(1)} async-done(((bf16[8,256,128]{2,1,0:T(8,128)(2,1)}), bf16[8,256,128]{2,1,0:T(8,128)(2,1)S(1)}, u32[]{:S(2)}, u32[]{:S(2)}) %all-to-all-start.5) | async-done | bytes 524320 | tf_op jit(solution)/shard_map/all_to_all | solution.py:933
  306.5 15.1 %all-to-all-done.6 = bf16[8,3,256,128]{3,2,1,0:T(8,128)(2,1)} async-done(((bf16[8,3,256,128]{3,2,1,0:T(8,128)(2,1)}), bf16[8,3,256,128]{3,2,1,0:T(8,128)(2,1)}, u32[]{:S(2)}, u32[]{:S(2)}) %all-to-all-start.6) | async-done | bytes 1572896 | tf_op jit(solution)/shard_map/all_to_all | solution.py:933
  326.3 22.7 %attend.6 = (bf16[8,16,16,128]{3,2,1,0:T(8,128)(2,1)}, f32[8,2048]{1,0:T(8,128)S(1)}) custom-call(s32[1]{0:T(128)} %bitcast.7.len_ref.refs_0_, bf16[8,3,16,16,128]{4,3,2,1,0:T(8,128)(2,1)} %bitcast.56.piece_ref.refs_1_), custom_call_target="tpu_custom_call" | custom-call | tf_op jit(solution)/shard_map/attend/pallas_call | solution.py:348
  349.1 12.9 %all-to-all-done.7 = bf16[8,3,256,128]{3,2,1,0:T(8,128)(2,1)} async-done(((bf16[8,3,256,128]{3,2,1,0:T(8,128)(2,1)}), bf16[8,3,256,128]{3,2,1,0:T(8,128)(2,1)}, u32[]{:S(2)}, u32[]{:S(2)}) %all-to-all-start.7) | async-done | bytes 1572896 | tf_op jit(solution)/shard_map/all_to_all | solution.py:933
  365.7 21.3 %attend.7 = (bf16[8,16,16,128]{3,2,1,0:T(8,128)(2,1)}, f32[8,2048]{1,0:T(8,128)S(1)}) custom-call(s32[1]{0:T(128)} %bitcast.42.len_ref.refs_0_, bf16[8,3,16,16,128]{4,3,2,1,0:T(8,128)(2,1)} %bitcast.58.piece_ref.refs_1_), custom_call_target="tpu_custom_call" | custom-call | tf_op jit(solution)/shard_map/attend/pallas_call | solution.py:348
  411.9 39.9 %all-gather.8.cloned.1.call-done = bf16[1024,8704]{1,0:T(8,128)(2,1)} async-done(((bf16[32,8704]{1,0:T(8,128)(2,1)}), bf16[1024,8704]{1,0:T(8,128)(2,1)}) %all-gather.8.cloned.1.call-update) | async-done | bytes 17825808 | tf_op jit(solution)/shard_map/all_gather | solution.py:954
  498.8 11.1 %multiply_convert_fusion.3 = (bf16[512,2816]{1,0:T(8,128)(2,1)}, bf16[512,2816]{1,0:T(8,128)(2,1)}) fusion(f32[512,2816]{1,0:T(8,128)} %fusion.8, f32[512,2816]{1,0:T(8,128)} %get-tuple-element.508, bf16[512,1024]{1,0:T(8,128)(2,1)S(1)} %bitcast.555, bf16[2816,1024]{1,0:T(8,128)(2,1)} %bitcast.537), kind=kOutput, calls=%fused_computation.9 | convolution fusion | flops 2971533312 | bytes 24117248 | tf_op jit(solution)/shard_map/dot_general | solution.py:1125
  535.8 11.8 %weight_grad.12 = bf16[4,2,64,2816]{3,2,1,0:T(8,128)(2,1)} custom-call(s32[1]{0:T(128)} %bitcast.core_ref, bf16[512,1024]{1,0:T(8,128)(2,1)S(1)} %multiply_convert_fusion.6.lo, bf16[512,1024]{1,0:T(8,128)(2,1)} %collective-permute-done.39.ln, bf16[512,2816]{1,0:T(8,128)(2,1)} %get-tuple-element.221.ro, bf16[512,2816]{1,0:T(8,128)(2,1)} %collective-permute-done.40.rn), custom_call_target="tpu_custom_call" | custom-call | tf_op jit(solution)/shard_map/weight_grad/pallas_call | solution.py:246
  555.9 11.8 %weight_grad.13 = bf16[4,2,64,2816]{3,2,1,0:T(8,128)(2,1)} custom-call(s32[1]{0:T(128)} %bitcast.core_ref, bf16[512,1024]{1,0:T(8,128)(2,1)S(1)} %multiply_convert_fusion.6.lo, bf16[512,1024]{1,0:T(8,128)(2,1)} %collective-permute-done.39.ln, bf16[512,2816]{1,0:T(8,128)(2,1)} %get-tuple-element.223.ro, bf16[512,2816]{1,0:T(8,128)(2,1)} %collective-permute-done.41.rn), custom_call_target="tpu_custom_call" | custom-call | tf_op jit(solution)/shard_map/weight_grad/pallas_call | solution.py:246
  571.4 8.5 weight_grad.14
  595.6 19.9 %attend_back.4 = (bf16[8,3,16,16,128]{4,3,2,1,0:T(8,128)(2,1)}, f32[2048,128]{1,0:T(8,128)S(1)}) custom-call(s32[1]{0:T(128)} %bitcast.7.len_ref.refs_0_, bf16[8,3,16,16,128]{4,3,2,1,0:T(8,128)(2,1)} %bitcast.56.piece_ref.refs_1_, bf16[8,16,16,128]{3,2,1,0:T(8,128)(2,1)} %get-tuple-element.202.refs_2_, ...), custom_call_target="tpu_custom_call" | custom-call | tf_op jit(solution)/shard_map/attend_back/pallas_call | solution.py:520
  622.6 16.6 %attend_back.5 = (bf16[8,3,16,16,128]{4,3,2,1,0:T(8,128)(2,1)}, f32[2048,128]{1,0:T(8,128)S(1)}) custom-call(s32[1]{0:T(128)} %bitcast.42.len_ref.refs_0_, bf16[8,3,16,16,128]{4,3,2,1,0:T(8,128)(2,1)} %bitcast.58.piece_ref.refs_1_, bf16[8,16,16,128]{3,2,1,0:T(8,128)(2,1)} %get-tuple-element.206.refs_2_, bf16[8,16,16,128]{3,2,1,0:T(8,128)(2,1)S(1)} %copy-done.25, ...), custom_call_target="tpu_custom_call" | custom-call | tf_op jit(solution)/shard_map/attend_back/pallas_call | solution.py:520
  653.2 13.0 %all-to-all-done.13 = bf16[8,3,256,128]{3,2,1,0:T(8,128)(2,1)} async-done(((bf16[8,3,256,128]{3,2,1,0:T(8,128)(2,1)}), bf16[8,3,256,128]{3,2,1,0:T(8,128)(2,1)}, u32[]{:S(2)}, u32[]{:S(2)}) %all-to-all-start.13) | async-done | bytes 1572896 | tf_op jit(solution)/shard_map/all_to_all | solution.py:933
  696.0 11.4 %multiply_convert_fusion = (bf16[512,2816]{1,0:T(8,128)(2,1)}, bf16[512,2816]{1,0:T(8,128)(2,1)}) fusion(f32[512,2816]{1,0:T(8,128)} %fusion.16, f32[512,2816]{1,0:T(8,128)} %get-tuple-element.502, bf16[512,1024]{1,0:T(8,128)(2,1)} %convert_element_type.490.ro, bf16[2816,1024]{1,0:T(8,128)(2,1)} %bitcast.535), kind=kOutput, calls=%fused_computation.6 | convolution fusion | flops 2971533312 | bytes 24117248 | tf_op jit(solution)/shard_map/dot_general | solution.py:1125
  720.9 8.6 weight_grad.20
  730.3 12.0 %weight_grad.19 = bf16[4,2,64,2816]{3,2,1,0:T(8,128)(2,1)} custom-call(s32[1]{0:T(128)} %bitcast.core_ref, bf16[512,1024]{1,0:T(8,128)(2,1)S(1)} %copy-done.6, bf16[512,1024]{1,0:T(8,128)(2,1)} %collective-permute-done.51.ln, bf16[512,2816]{1,0:T(8,128)(2,1)} %get-tuple-element.261.ro, bf16[512,2816]{1,0:T(8,128)(2,1)} %collective-permute-done.53.rn), custom_call_target="tpu_custom_call" | custom-call | tf_op jit(solution)/shard_map/weight_grad/pallas_call | solution.py:246
  742.3 11.8 %weight_grad.18 = bf16[4,2,64,2816]{3,2,1,0:T(8,128)(2,1)} custom-call(s32[1]{0:T(128)} %bitcast.core_ref, bf16[512,1024]{1,0:T(8,128)(2,1)S(1)} %copy-done.6, bf16[512,1024]{1,0:T(8,128)(2,1)} %collective-permute-done.51.ln, bf16[512,2816]{1,0:T(8,128)(2,1)} %get-tuple-element.260.ro, bf16[512,2816]{1,0:T(8,128)(2,1)} %collective-permute-done.52.rn), custom_call_target="tpu_custom_call" | custom-call | tf_op jit(solution)/shard_map/weight_grad/pallas_call | solution.py:246
  774.7 8.2 fusion.10
  782.9 9.0 multiply_reduce_fusion.1
  809.6 21.2 %collective-permute-done.56 = bf16[4,32,1024]{2,1,0:T(8,128)(2,1)S(1)} collective-permute-done((bf16[4,32,1024]{2,1,0:T(8,128)(2,1)S(1)}, bf16[4,32,1024]{2,1,0:T(8,128)(2,1)S(1)}, u32[]{:S(2)}, u32[]{:S(2)}) %collective-permute-start.56) | collective-permute-done | bytes 262176 | tf_op jit(solution)/shard_map/ppermute | solution.py:68
  843.2 20.0 %attend_back.6 = bf16[8,3,16,16,128]{4,3,2,1,0:T(8,128)(2,1)} custom-call(s32[1]{0:T(128)} %bitcast.7.len_ref.refs_0_, bf16[8,3,16,16,128]{4,3,2,1,0:T(8,128)(2,1)} %bitcast.475, bf16[8,16,16,128]{3,2,1,0:T(8,128)(2,1)S(1)} %copy-done.23, bf16[8,16,16,128]{3,2,1,0:T(8,128)(2,1)S(1)} %get-tuple-element.423.refs_3_, f32[8,2048]{1,0:T(8,128)S(1)} %get-tuple-element.282.refs_4_, ...), custom_call_target="tpu_custom_call" | custom-call | tf_op jit(solution)/shard_map/attend_back/pallas_call | solution.py:520
  871.9 11.4 %collective-permute-start.67 = (bf16[32,1536]{1,0:T(8,128)(2,1)}, bf16[32,1536]{1,0:T(8,128)(2,1)}, u32[]{:S(2)}, u32[]{:S(2)}) collective-permute-start(bf16[32,1536]{1,0:T(8,128)(2,1)} %get-tuple-element.456), channel_id=1, source_target_pairs={{0,4},{2,6},{4,0},{6,2},{1,5},{3,7},{5,1},{7,3},{8,12},{10,14},{12... | collective-permute-start | bytes 294920 | tf_op jit(solution)/shard_map/ppermute | solution.py:72
  888.2 16.6 %attend_back.7 = bf16[8,3,16,16,128]{4,3,2,1,0:T(8,128)(2,1)} custom-call(s32[1]{0:T(128)} %bitcast.42.len_ref.refs_0_, bf16[8,3,16,16,128]{4,3,2,1,0:T(8,128)(2,1)} %bitcast.473, bf16[8,16,16,128]{3,2,1,0:T(8,128)(2,1)} %get-tuple-element.196.refs_2_, bf16[8,16,16,128]{3,2,1,0:T(8,128)(2,1)S(1)} %copy-done.24, f32[8,2048]{1,0:T(8,128)S(1)} %get-tuple-element.292.refs_4_, ...), custom_call_target="tpu_custom_call" | custom-call | tf_op jit(solution)/shard_map/attend_back/pallas_call | solution.py:520
  904.8 8.0 collective-permute-start.63
  1015.9 12.5 %collective-permute-done.76 = bf16[4,2,32,1536]{3,2,1,0:T(8,128)(2,1)} collective-permute-done((bf16[4,2,32,1536]{3,2,1,0:T(8,128)(2,1)}, bf16[4,2,32,1536]{3,2,1,0:T(8,128)(2,1)}, u32[]{:S(2)}, u32[]{:S(2)}) %collective-permute-start.76) | collective-permute-done | bytes 786464 | tf_op jit(solution)/shard_map/ppermute | solution.py:68
  1048.1 9.4 collective-permute-done.79
  (822 shorter events, 610.9 us)
Async XLA Ops:
  7.2 191.4 %all-gather.4.cloned.1.call-start = ((), (), s32[]{:S(2)}) async-start(), calls=%async_computation.22 | async-start | bytes 20545536 | tf_op jit(solution)/shard_map/all_gather | solution.py:954
  61.0 53.8 %all-to-all-start.1 = ((bf16[4,2,2,2,16,1024]{5,4,3,1,2,0:T(8,128)(2,1)}), bf16[4,2,2,2,16,1024]{5,4,3,1,2,0:T(8,128)(2,1)}, u32[]{:S(2)}, u32[]{:S(2)}) async-start(bf16[4,2,2,2,16,1024]{5,4,3,1,2,0:T(8,128)(2,1)} %copy.161), calls=%async_computation.1 | async-start | bytes 2097152 | tf_op jit(solution)/shard_map/all_to_all | solution.py:937
  127.1 42.0 %all-to-all-start.2 = ((bf16[8,3,256,128]{3,2,1,0:T(8,128)(2,1)}), bf16[8,3,256,128]{3,2,1,0:T(8,128)(2,1)S(1)}, u32[]{:S(2)}, u32[]{:S(2)}) async-start(bf16[8,3,256,128]{3,2,1,0:T(8,128)(2,1)} %project_qkv.4.rest_0_), calls=%async_computation.2 | async-start | bytes 3145728 | tf_op jit(solution)/shard_map/all_to_all | solution.py:933
  172.6 113.9 %all-gather.6.cloned.1.call-start = ((), (), s32[]{:S(2)}) async-start(), calls=%async_computation.23 | async-start | bytes 8921088 | tf_op jit(solution)/shard_map/all_gather | solution.py:954
  231.0 220.7 %all-gather.8.cloned.1.call-start = ((), (), s32[]{:S(2)}) async-start(), calls=%async_computation.24 | async-start | bytes 18382848 | tf_op jit(solution)/shard_map/all_gather | solution.py:954
  321.6 40.4 %all-to-all-start.7 = ((bf16[8,3,256,128]{3,2,1,0:T(8,128)(2,1)}), bf16[8,3,256,128]{3,2,1,0:T(8,128)(2,1)}, u32[]{:S(2)}, u32[]{:S(2)}) async-start(bf16[8,3,256,128]{3,2,1,0:T(8,128)(2,1)} %project_qkv.7), calls=%async_computation.7 | async-start | bytes 3145728 | tf_op jit(solution)/shard_map/all_to_all | solution.py:933
  392.7 81.3 %collective-permute-start.31 = (bf16[2,2,16,1024]{3,2,1,0:T(8,128)(2,1)}, bf16[2,2,16,1024]{3,2,1,0:T(8,128)(2,1)}, u32[]{:S(2)}, u32[]{:S(2)}) collective-permute-start(bf16[2,2,16,1024]{3,2,1,0:T(8,128)(2,1)} %get-tuple-element.433), channel_id=1, source_target_pairs={{0,0},{1,1},{2,16},{3,17},{4,8},{5,9},{6,24},{7,25},{8,4},{9,5},{1... | collective-permute-start | bytes 393224 | tf_op jit(solution)/shard_map/ppermute | solution.py:1215
  394.8 80.6 %collective-permute-start.32 = (bf16[2,2,16,1024]{3,2,1,0:T(8,128)(2,1)}, bf16[2,2,16,1024]{3,2,1,0:T(8,128)(2,1)}, u32[]{:S(2)}, u32[]{:S(2)}) collective-permute-start(bf16[2,2,16,1024]{3,2,1,0:T(8,128)(2,1)} %get-tuple-element.432), channel_id=1, source_target_pairs={{0,1},{1,0},{2,17},{3,16},{4,9},{5,8},{6,25},{7,24},{8,5},{9,4},{1... | collective-permute-start | bytes 393224 | tf_op jit(solution)/shard_map/ppermute | solution.py:1215
  396.8 78.9 %collective-permute-start.33 = (bf16[2,2,16,1024]{3,2,1,0:T(8,128)(2,1)}, bf16[2,2,16,1024]{3,2,1,0:T(8,128)(2,1)}, u32[]{:S(2)}, u32[]{:S(2)}) collective-permute-start(bf16[2,2,16,1024]{3,2,1,0:T(8,128)(2,1)} %get-tuple-element.431), channel_id=1, source_target_pairs={{0,16},{1,17},{2,0},{3,1},{4,24},{5,25},{6,8},{7,9},{8,20},{9,21},... | collective-permute-start | bytes 393224 | tf_op jit(solution)/shard_map/ppermute | solution.py:1215
  401.4 82.5 %collective-permute-start.34 = (bf16[2,2,16,1024]{3,2,1,0:T(8,128)(2,1)}, bf16[2,2,16,1024]{3,2,1,0:T(8,128)(2,1)}, u32[]{:S(2)}, u32[]{:S(2)}) collective-permute-start(bf16[2,2,16,1024]{3,2,1,0:T(8,128)(2,1)} %get-tuple-element.430), channel_id=1, source_target_pairs={{0,17},{1,16},{2,1},{3,0},{4,25},{5,24},{6,9},{7,8},{8,21},{9,20},... | collective-permute-start | bytes 393224 | tf_op jit(solution)/shard_map/ppermute | solution.py:1215
  402.1 81.8 %collective-permute-start.35 = (bf16[2,2,16,1024]{3,2,1,0:T(8,128)(2,1)}, bf16[2,2,16,1024]{3,2,1,0:T(8,128)(2,1)}, u32[]{:S(2)}, u32[]{:S(2)}) collective-permute-start(bf16[2,2,16,1024]{3,2,1,0:T(8,128)(2,1)} %get-tuple-element.429), channel_id=1, source_target_pairs={{0,8},{1,9},{2,24},{3,25},{4,0},{5,1},{6,16},{7,17},{8,12},{9,13},... | collective-permute-start | bytes 393224 | tf_op jit(solution)/shard_map/ppermute | solution.py:1215
  483.8 51.9 %collective-permute-start.39 = (bf16[512,1024]{1,0:T(8,128)(2,1)S(1)}, bf16[512,1024]{1,0:T(8,128)(2,1)}, u32[]{:S(2)}, u32[]{:S(2)}) collective-permute-start(bf16[512,1024]{1,0:T(8,128)(2,1)S(1)} %multiply_convert_fusion.6.lo), channel_id=1, source_target_pairs={{0,8},{8,0},{1,9},{9,1},{2,10},{10,2},{3,11},{11,3},{4,12},{12,4},... | collective-permute-start | bytes 3145736 | tf_op jit(solution)/shard_map/ppermute | solution.py:68
  483.9 51.8 %collective-permute-start.42 = (bf16[512,2816]{1,0:T(8,128)(2,1)}, bf16[512,2816]{1,0:T(8,128)(2,1)}, u32[]{:S(2)}, u32[]{:S(2)}) collective-permute-start(bf16[512,2816]{1,0:T(8,128)(2,1)} %get-tuple-element.225.lo), channel_id=1, source_target_pairs={{0,8},{8,0},{1,9},{9,1},{2,10},{10,2},{3,11},{11,3},{4,12},{12,4},... | collective-permute-start | bytes 8650760 | tf_op jit(solution)/shard_map/ppermute | solution.py:68
  489.0 44.4 %all-to-all-start.10 = ((bf16[4,2,2,2,16,1024]{5,4,3,1,2,0:T(8,128)(2,1)}), bf16[4,2,2,2,16,1024]{5,4,3,1,2,0:T(8,128)(2,1)}, u32[]{:S(2)}, u32[]{:S(2)}) async-start(bf16[4,2,2,2,16,1024]{5,4,3,1,2,0:T(8,128)(2,1)} %copy.173), calls=%async_computation.10 | async-start | bytes 2097152 | tf_op jit(solution)/shard_map/all_to_all | solution.py:937
  551.2 34.7 %all-to-all-start.11 = ((bf16[8,512,128]{2,1,0:T(8,128)(2,1)}), bf16[8,512,128]{2,1,0:T(8,128)(2,1)}, u32[]{:S(2)}, u32[]{:S(2)}) async-start(bf16[8,512,128]{2,1,0:T(8,128)(2,1)} %bitcast.541), calls=%async_computation.11 | async-start | bytes 2097152 | tf_op jit(solution)/shard_map/all_to_all | solution.py:933
  555.5 282.9 %reduce-scatter.3.cloned.1.call-start = ((), (), s32[]{:S(2)}) async-start(), calls=%async_computation.25 | async-start | bytes 11141120 | tf_op jit(solution)/shard_map/reduce_scatter | solution.py:1151
  645.8 301.4 %reduce-scatter.5.cloned.1.call-start = ((), (), s32[]{:S(2)}) async-start(), calls=%async_computation.26 | async-start | bytes 11141120 | tf_op jit(solution)/shard_map/reduce_scatter | solution.py:1135
  669.9 42.3 %collective-permute-start.54 = (bf16[512,2816]{1,0:T(8,128)(2,1)}, bf16[512,2816]{1,0:T(8,128)(2,1)}, u32[]{:S(2)}, u32[]{:S(2)}) collective-permute-start(bf16[512,2816]{1,0:T(8,128)(2,1)} %copy-done.92), channel_id=1, source_target_pairs={{0,8},{8,0},{1,9},{9,1},{2,10},{10,2},{3,11},{11,3},{4,12},{12,4},... | collective-permute-start | bytes 8650760 | tf_op jit(solution)/shard_map/ppermute | solution.py:68
  707.7 34.6 %collective-permute-start.52 = (bf16[512,2816]{1,0:T(8,128)(2,1)}, bf16[512,2816]{1,0:T(8,128)(2,1)}, u32[]{:S(2)}, u32[]{:S(2)}) collective-permute-start(bf16[512,2816]{1,0:T(8,128)(2,1)} %get-tuple-element.260.ro), channel_id=1, source_target_pairs={{0,8},{8,0},{1,9},{9,1},{2,10},{10,2},{3,11},{11,3},{4,12},{12,4},... | collective-permute-start | bytes 8650760 | tf_op jit(solution)/shard_map/ppermute | solution.py:68
  712.3 51.8 %collective-permute-start.48 = (bf16[4,2,32,1024]{3,2,0,1:T(8,128)(2,1)}, bf16[4,2,32,1024]{3,2,0,1:T(8,128)(2,1)}, u32[]{:S(2)}, u32[]{:S(2)}) collective-permute-start(bf16[4,2,32,1024]{3,2,0,1:T(8,128)(2,1)} %copy_bitcast_fusion.3), channel_id=1, source_target_pairs={{0,1},{1,0},{2,3},{3,2},{4,5},{5,4},{6,7},{7,6},{8,9},{9,8},{10,11... | collective-permute-start | bytes 1572872 | tf_op jit(solution)/shard_map/ppermute | solution.py:68
  720.1 43.9 %collective-permute-start.49 = (bf16[4,2,32,1536]{3,2,0,1:T(8,128)(2,1)}, bf16[4,2,32,1536]{3,2,0,1:T(8,128)(2,1)}, u32[]{:S(2)}, u32[]{:S(2)}) collective-permute-start(bf16[4,2,32,1536]{3,2,0,1:T(8,128)(2,1)} %copy_bitcast_fusion.1), channel_id=1, source_target_pairs={{0,16},{16,0},{1,17},{17,1},{2,18},{18,2},{3,19},{19,3},{4,20},{20... | collective-permute-start | bytes 2359304 | tf_op jit(solution)/shard_map/ppermute | solution.py:68
  729.6 34.5 %collective-permute-start.50 = (bf16[4,2,32,1536]{3,2,0,1:T(8,128)(2,1)}, bf16[4,2,32,1536]{3,2,0,1:T(8,128)(2,1)}, u32[]{:S(2)}, u32[]{:S(2)}) collective-permute-start(bf16[4,2,32,1536]{3,2,0,1:T(8,128)(2,1)} %copy_bitcast_fusion), channel_id=1, source_target_pairs={{0,1},{1,0},{2,3},{3,2},{4,5},{5,4},{6,7},{7,6},{8,9},{9,8},{10,11... | collective-permute-start | bytes 2359304 | tf_op jit(solution)/shard_map/ppermute | solution.py:68
  797.8 34.4 %all-to-all-start.15 = ((bf16[8,512,128]{2,1,0:T(8,128)(2,1)}), bf16[8,512,128]{2,1,0:T(8,128)(2,1)S(1)}, u32[]{:S(2)}, u32[]{:S(2)}) async-start(bf16[8,512,128]{2,1,0:T(8,128)(2,1)} %bitcast.542), calls=%async_computation.15 | async-start | bytes 2097152 | tf_op jit(solution)/shard_map/all_to_all | solution.py:933
  865.1 50.0 %all-to-all-start.16 = ((bf16[8,3,256,128]{3,2,1,0:T(8,128)(2,1)}), bf16[8,3,256,128]{3,2,1,0:T(8,128)(2,1)}, u32[]{:S(2)}, u32[]{:S(2)}) async-start(bf16[8,3,256,128]{3,2,1,0:T(8,128)(2,1)} %bitcast.532), calls=%async_computation.17 | async-start | bytes 3145728 | tf_op jit(solution)/shard_map/all_to_all | solution.py:933
  869.6 35.2 %collective-permute-start.61 = (bf16[512,1024]{1,0:T(8,128)(2,1)S(1)}, bf16[512,1024]{1,0:T(8,128)(2,1)}, u32[]{:S(2)}, u32[]{:S(2)}) collective-permute-start(bf16[512,1024]{1,0:T(8,128)(2,1)S(1)} %copy-done.18), channel_id=1, source_target_pairs={{0,8},{8,0},{1,9},{9,1},{2,10},{10,2},{3,11},{11,3},{4,12},{12,4},... | collective-permute-start | bytes 3145736 | tf_op jit(solution)/shard_map/ppermute | solution.py:68
  870.0 42.8 %collective-permute-start.62 = (bf16[512,1024]{1,0:T(8,128)(2,1)}, bf16[512,1024]{1,0:T(8,128)(2,1)}, u32[]{:S(2)}, u32[]{:S(2)}) collective-permute-start(bf16[512,1024]{1,0:T(8,128)(2,1)} %copy-done.82), channel_id=1, source_target_pairs={{0,8},{8,0},{1,9},{9,1},{2,10},{10,2},{3,11},{11,3},{4,12},{12,4},... | collective-permute-start | bytes 3145736 | tf_op jit(solution)/shard_map/ppermute | solution.py:68
  871.9 59.0 %collective-permute-start.66 = (bf16[32,1536]{1,0:T(8,128)(2,1)}, bf16[32,1536]{1,0:T(8,128)(2,1)}, u32[]{:S(2)}, u32[]{:S(2)}) collective-permute-start(bf16[32,1536]{1,0:T(8,128)(2,1)} %get-tuple-element.457), channel_id=1, source_target_pairs={{0,2},{2,0},{4,6},{6,4},{1,3},{3,1},{5,7},{7,5},{8,10},{10,8},{12,... | collective-permute-start | bytes 294920 | tf_op jit(solution)/shard_map/ppermute | solution.py:72
  871.9 62.9 %collective-permute-start.67 = (bf16[32,1536]{1,0:T(8,128)(2,1)}, bf16[32,1536]{1,0:T(8,128)(2,1)}, u32[]{:S(2)}, u32[]{:S(2)}) collective-permute-start(bf16[32,1536]{1,0:T(8,128)(2,1)} %get-tuple-element.456), channel_id=1, source_target_pairs={{0,4},{2,6},{4,0},{6,2},{1,5},{3,7},{5,1},{7,3},{8,12},{10,14},{12... | collective-permute-start | bytes 294920 | tf_op jit(solution)/shard_map/ppermute | solution.py:72
  883.3 53.3 %collective-permute-start.68 = (bf16[32,1536]{1,0:T(8,128)(2,1)}, bf16[32,1536]{1,0:T(8,128)(2,1)}, u32[]{:S(2)}, u32[]{:S(2)}) collective-permute-start(bf16[32,1536]{1,0:T(8,128)(2,1)} %get-tuple-element.455), channel_id=1, source_target_pairs={{0,6},{2,4},{4,2},{6,0},{1,7},{3,5},{5,3},{7,1},{8,14},{10,12},{12... | collective-permute-start | bytes 294920 | tf_op jit(solution)/shard_map/ppermute | solution.py:72
  962.9 70.2 %collective-permute-start.87 = (bf16[2,32,4352]{2,1,0:T(8,128)(2,1)}, bf16[2,32,4352]{2,1,0:T(8,128)(2,1)}, u32[]{:S(2)}, u32[]{:S(2)}) collective-permute-start(bf16[2,32,4352]{2,1,0:T(8,128)(2,1)} %dynamic-slice_bitcast_fusion.4), channel_id=1, source_target_pairs={{0,16},{16,0},{1,17},{17,1},{2,18},{18,2},{3,19},{19,3},{4,20},{20... | collective-permute-start | bytes 1671176 | tf_op jit(solution)/shard_map/ppermute | solution.py:68
  979.5 53.6 %collective-permute-start.86 = (bf16[2,32,4352]{2,1,0:T(8,128)(2,1)}, bf16[2,32,4352]{2,1,0:T(8,128)(2,1)}, u32[]{:S(2)}, u32[]{:S(2)}) collective-permute-start(bf16[2,32,4352]{2,1,0:T(8,128)(2,1)} %dynamic-slice_bitcast_fusion.5), channel_id=1, source_target_pairs={{0,1},{1,0},{2,3},{3,2},{4,5},{5,4},{6,7},{7,6},{8,9},{9,8},{10,11... | collective-permute-start | bytes 1671176 | tf_op jit(solution)/shard_map/ppermute | solution.py:68
  981.8 51.2 %collective-permute-start.88 = (bf16[4,2,32,1024]{3,2,0,1:T(8,128)(2,1)}, bf16[4,2,32,1024]{3,2,0,1:T(8,128)(2,1)}, u32[]{:S(2)}, u32[]{:S(2)}) collective-permute-start(bf16[4,2,32,1024]{3,2,0,1:T(8,128)(2,1)} %copy_bitcast_fusion.2), channel_id=1, source_target_pairs={{0,1},{1,0},{2,3},{3,2},{4,5},{5,4},{6,7},{7,6},{8,9},{9,8},{10,11... | collective-permute-start | bytes 1572872 | tf_op jit(solution)/shard_map/ppermute | solution.py:68
  (272 other events, 3079.1 us)
Sparse Core Ops, SparseCore 0:
  13.0 163.8 all-gather.3
  198.8 87.6 all-gather.5
  290.0 161.7 all-gather.7
  586.0 154.2 reduce-scatter.2
  771.1 171.7 reduce-scatter.4

commit v3 on v2

--- a/solution.py
+++ b/solution.py
@@ -207,56 +207,128 @@
     )(*operands)
 
 
-def weight_grad(core, left_own, left_near, right_own, right_near, tile):
-    rows, width = left_own.shape
-    cols = right_own.shape[1]
-    size = width // 4
-    window = -(-size // 128) * 128
-    slack = window - size
-
-    def kernel(core_ref, lo, ln, ro, rn, out_ref, held, flipped, sems):
-        @pl.when(pl.program_id(0) == 0)
-        def _():
-            copies = []
-            for side, ref in enumerate((lo, ln)):
+def weight_grads(core, groups, chunks):
+    rows = groups[0][0][0].shape[0]
+    operands, scratch, plans = [], [], []
+    widths, count = {}, 0
+    for (left, rights), places in zip(groups, chunks):
+        size = left[0].shape[1] // 4
+        window = -(-size // 128) * 128
+        plan = {"size": size, "window": window, "left": len(operands), "held": len(scratch)}
+        operands += list(left)
+        scratch.append(pltpu.VMEM((2, 2 * rows, window), BF))
+        plan["rights"] = []
+        for right, parts in zip(rights, places):
+            cols = right[0].shape[1]
+            plan["rights"].append((len(operands), len(scratch), parts))
+            operands += list(right)
+            scratch.append(pltpu.VMEM((2 * rows, cols), BF))
+            for _, span, result, at in parts:
+                count += 1
+                spread = span if size == window else 3 * span
+                widths[result] = max(widths.get(result, 0), at + spread)
+        plans.append(plan)
+    shapes = [(4, 2, 64, widths[n]) for n in range(len(widths))]
+    first_stage = len(scratch)
+    scratch += [pltpu.VMEM(shape, BF) for shape in shapes]
+    scratch += [
+        pltpu.SemaphoreType.DMA((len(operands), 2)),
+        pltpu.SemaphoreType.DMA((count,)),
+    ]
+    inputs, results = len(operands), len(shapes)
+
+    def put_thirds(stage, part, total, at, span, size):
+        for z in range(4):
+            for x in range(2):
+                low = z * (size // 4) + x * (size // 8)
+                for third in range(3):
+                    first, last = low + 32 * third, low + min(32 * third + 32, size // 8)
+                    piece = total[first:last]
+                    missing = 32 - piece.shape[0]
+                    if missing:
+                        piece = jnp.concatenate([piece, jnp.zeros((missing, span), F32)])
+                    lane = at + third * span
+                    stage[z, part, 32 * x : 32 * x + 32, lane : lane + span] = piece.astype(BF)
+
+    def kernel(core_ref, *refs):
+        ins, outs, work = refs[:inputs], refs[inputs : inputs + results], refs[inputs + results :]
+        stages = work[first_stage : first_stage + results]
+        in_sems, out_sems = work[-2:]
+        loads = []
+        for plan in plans:
+            held, size, window = work[plan["held"]], plan["size"], plan["window"]
+            slack = window - size
+            left = []
+            for side in range(2):
                 for part in range(2):
                     start = 2 * part * size + core_ref[0] * (size - slack)
                     span = pl.ds(pl.multiple_of(start, 128), window)
-                    copies.append(
+                    at = plan["left"] + side
+                    left.append(
                         pltpu.make_async_copy(
-                            ref.at[:, span], held.at[side, part], sems.at[side, part]
+                            ins[at].at[:, span],
+                            held.at[part, pl.ds(side * rows, rows)],
+                            in_sems.at[at, part],
                         )
                     )
-            for copy in copies:
+            rights = []
+            for at, spot, _ in plan["rights"]:
+                rights.append(
+                    [
+                        pltpu.make_async_copy(
+                            ins[at + side],
+                            work[spot].at[pl.ds(side * rows, rows)],
+                            in_sems.at[at + side, 0],
+                        )
+                        for side in range(2)
+                    ]
+                )
+            loads.append((left, rights))
+            for copy in left + [copy for pair in rights for copy in pair]:
                 copy.start()
-            for copy in copies:
+        puts = []
+        for plan, (left, rights) in zip(plans, loads):
+            size, window = plan["size"], plan["window"]
+            held = work[plan["held"]]
+            for copy in left:
                 copy.wait()
-            for side in range(2):
-                for part in range(2):
-                    flipped[part, :, side * rows : side * rows + rows] = held[side, part].T
-
-        for part in range(2):
-            span = pl.ds(pl.multiple_of(core_ref[0] * slack, 16), size)
-            left = flipped[part, span, :]
-            total = jnp.dot(left[:, :rows], ro[...], preferred_element_type=F32)
-            total += jnp.dot(left[:, rows:], rn[...], preferred_element_type=F32)
-            out_ref[:, part] = total.astype(BF).reshape(4, size // 4, tile)
-
-    block = pl.BlockSpec((rows, tile), lambda n: (0, n))
+            for pair, (_, spot, parts) in zip(rights, plan["rights"]):
+                for copy in pair:
+                    copy.wait()
+                for first, span, result, at in parts:
+                    right = work[spot][:, first : first + span]
+                    stage = stages[result]
+                    wide = span if size == window else 3 * span
+                    for part in range(2):
+                        total = lax.dot_general(
+                            held[part], right, TN, preferred_element_type=F32
+                        )
+                        if size == window:
+                            total = total.astype(BF).reshape(4, size // 4, span)
+                            stage[:, part, :, at : at + span] = total
+                        else:
+                            own = jnp.where(core_ref[0] == 0, total[:size], total[window - size :])
+                            put_thirds(stage, part, own, at, span, size)
+                    lanes = pl.ds(at, wide)
+                    put = pltpu.make_async_copy(
+                        stage.at[:, :, :, lanes],
+                        outs[result].at[:, :, :, lanes],
+                        out_sems.at[len(puts)],
+                    )
+                    put.start()
+                    puts.append(put)
+        for put in puts:
+            put.wait()
+
     return pl.pallas_call(
         kernel,
-        grid=(cols // tile,),
-        in_specs=[SMEM, ANY, ANY, block, block],
-        out_specs=pl.BlockSpec((4, 2, size // 4, tile), lambda n: (0, 0, 0, n)),
-        out_shape=jax.ShapeDtypeStruct((4, 2, size // 4, cols), BF),
-        scratch_shapes=[
-            pltpu.VMEM((2, 2, rows, window), BF),
-            pltpu.VMEM((2, window, 2 * rows), BF),
-            pltpu.SemaphoreType.DMA((2, 2)),
-        ],
-        compiler_params=params(dimension_semantics=("arbitrary",)),
-        name="weight_grad",
-    )(core, left_own, left_near, right_own, right_near)
+        in_specs=[SMEM] + [ANY] * inputs,
+        out_specs=[ANY] * results,
+        out_shape=[jax.ShapeDtypeStruct(shape, BF) for shape in shapes],
+        scratch_shapes=scratch,
+        compiler_params=params(),
+        name="weight_grads",
+    )(core, *operands)
 
 
 def rows_of(block):
@@ -1083,12 +1155,8 @@
         weighted = grad_normed * gain
         return rms * (weighted - scaled * jnp.mean(weighted * scaled, axis=-1, keepdims=True))
 
-    def chip_grad(left, right, tile):
-        grad = weight_grad(core, left[0], left[1], right[0], right[1], tile)
-        return grad.reshape(4, 2, 2, -1, grad.shape[-1])
-
-    def start_sum(left, right, tile, order):
-        return Reduction(chip_grad(left, right, tile), order)
+    def blocks_of(grad):
+        return grad.reshape(4, 2, 2, 32, grad.shape[-1])
 
     def dots(grads, weights):
         total = None
@@ -1097,19 +1165,31 @@
             total = part if total is None else total + part
         return total
 
-    def qkv_sums(one, proj):
-        half = 3 * width // 2
-        sums = []
-        for lo, order in ((0, "yxz"), (half, "xyz")):
-            right = (proj[0][:, lo : lo + half], proj[1][:, lo : lo + half])
-            sums.append(start_sum(one, right, 512, order))
-        return sums
+    def attn_grads(one, att, proj, mid, places):
+        return weight_grads(core, [(one, [proj]), (att, [mid])], places)
+
+    def sum_z(grad):
+        flat = grad.reshape(4, 128, grad.shape[-1])
+        flat = lax.psum_scatter(flat, "z", scatter_dimension=0, tiled=True)
+        return flat.reshape(2, 2, 32, grad.shape[-1])
+
+    def pair_sums(summed):
+        half = summed.shape[-1] // 2
+        return [
+            Reduction(summed[..., :half], "xy", "yx"),
+            Reduction(summed[..., half:], "yx", "yx"),
+        ]
 
     def ffn_grads(two, gates, ups, hid, low):
-        grads = [chip_grad(two, gates, 256), chip_grad(two, ups, 256)]
-        return jnp.concatenate(grads + [pack(chip_grad(hid, low, 512))], axis=-1)
-
-    def backward_layer(grad_in, w_attn, w_ffn, kept, passed, pending, upper_sum, beside):
+        half = ffn // 2
+        parts = [[(0, half, 0, 0), (half, half, 0, half)]]
+        parts.append([(0, half, 0, ffn), (half, half, 0, ffn + half)])
+        (grad,) = weight_grads(
+            core, [(two, [gates, ups]), (hid, [low])], [parts, [[(0, width, 0, 2 * ffn)]]]
+        )
+        return grad
+
+    def backward_layer(grad_in, w_attn, w_ffn, kept, passed, upper, beside):
         w_turned, w_o, gain = w_attn
         w_gu, w_d = w_ffn
         (
@@ -1128,63 +1208,48 @@
         grad_up = (grad_hidden * gate * sigma).astype(BF)
         gates = (grad_gate, near(grad_gate))
         ups = (grad_up, near(grad_up))
-        if upper_sum is not None:
-            summed = ffn_grads(two, gates, ups, hid, low)
-            summed, grad_gate, grad_up = add_all(pending, summed, grad_gate, grad_up)
-            summed, grad_gate, grad_up = send_all(pending, summed, grad_gate, grad_up)
-            summed = lax.psum_scatter(summed, "z", scatter_dimension=0, tiled=True)[0]
+        if upper is None:
+            beside, grad_gate, grad_up, *gates = fence(beside, grad_gate, grad_up, *gates)
+        summed = ffn_grads(two, gates, ups, hid, low)
+        summed, grad_gate, grad_up = fence(summed, grad_gate, grad_up)
+        summed = sum_z(summed)
         grad_normed = dots([grad_gate, grad_up], [w_gu[:, :ffn], w_gu[:, ffn : 2 * ffn]])
         grad_middle = grad_in + norm_back(grad_normed, middle, rms_two, gain[1])
         grad_attn = grad_middle.astype(BF)
         mid = (grad_attn, near(grad_attn))
         grad_o = lax.dot_general(grad_attn, w_o, NT, preferred_element_type=F32).astype(BF)
         grad_o = jnp.transpose(grad_o.reshape(rows, 8, 128), (1, 0, 2))
-        grad_o, beside = fence(grad_o, beside)
-
-        if upper_sum is None:
-            held = fence(grad_o, *two, *gates, *ups, *hid, *low)
-            grad_o, two, gates, ups = held[0], held[1:3], held[3:5], held[5:7]
-            hid, low = held[7:9], held[9:11]
-            grad_o = exchange(grad_o)
-            summed = ffn_grads(two, gates, ups, hid, low)
-            summed, grad_o = fence(summed, grad_o)
-            summed = lax.psum_scatter(summed, "z", scatter_dimension=0, tiled=True)[0]
-        else:
-            grad_o = exchange(grad_o)
-        (grad_o,) = add_all(pending, grad_o)
-        if upper_sum is not None:
-            upper_sum, grad_o = fence(upper_sum, grad_o)
-            half = upper_sum.shape[-1] // 2
-            pending.append(Reduction(upper_sum[..., :half], "xy", "yx"))
-            pending.append(Reduction(upper_sum[..., half:], "yx", "yx"))
-        (grad_o,) = send_all(pending, grad_o)
+        if upper is not None:
+            grad_o, beside = fence(grad_o, beside)
+
+        grad_o = exchange(grad_o)
+        ffn_pair = []
+        if upper is not None:
+            upper_ffn, upper_attn = upper
+            upper_ffn, grad_o = fence(upper_ffn, grad_o)
+            ffn_pair = pair_sums(upper_ffn)
+            (grad_o,) = send_all(ffn_pair, grad_o)
         grad_o = grad_o.reshape(8, 2, stretch // 16, 16, 128)
         cos_sin = (cosine, sine)
         parts_a, pass_a = attend_back(
             length[0], pieces[0], attended[0], grad_o[:, 0], lse[0], *cos_sin, passed and passed[0]
         )
         parts_a, grad_b = fence(parts_a, grad_o[:, 1])
-        if upper_sum is not None:
-            parts_a, grad_b = add_all(pending[3:], parts_a, grad_b)
-            parts_a, grad_b = send_all(pending[3:], parts_a, grad_b)
+        if ffn_pair:
+            parts_a, grad_b = add_all(ffn_pair, parts_a, grad_b)
+            parts_a, grad_b = send_all(ffn_pair, parts_a, grad_b)
         moved_a = exchange(parts_a.reshape(8, 3, stretch, 128))
         parts_b, pass_b = attend_back(
             length[1], pieces[1], attended[1], grad_b, lse[1], *cos_sin, passed and passed[1]
         )
-        moved_a, parts_b, *held = fence(moved_a, parts_b, *att, *mid)
-        att, mid = held[:2], held[2:4]
+        moved_a, parts_b = fence(moved_a, parts_b)
         moved_b = exchange(parts_b.reshape(8, 3, stretch, 128))
-        out = start_sum(att, mid, 512, "xyz")
-        if upper_sum is not None:
-            summed, moved_b = add_all(pending, summed, moved_b)
-            half = summed.shape[-1] // 2
-            summed = [
-                Reduction(summed[..., :half], "xy", "yx"),
-                Reduction(summed[..., half:], "yx", "yx"),
-            ]
-            (moved_b,) = send_all([out] + summed, moved_b)
-        else:
-            (moved_b,) = send_all([out], moved_b)
+        attn_pair = []
+        if ffn_pair:
+            (moved_b,) = add_all(ffn_pair, moved_b)
+            upper_attn, moved_b = fence(upper_attn, moved_b)
+            attn_pair = pair_sums(upper_attn)
+            (moved_b,) = send_all(attn_pair, moved_b)
         grad_proj = jnp.concatenate(
             [
                 jnp.transpose(moved, (2, 1, 0, 3)).reshape(stretch, 3 * width)
@@ -1198,7 +1263,8 @@
             at += weight.shape[1]
         grad_normed = dots(cuts, w_turned)
         grad = grad_middle + norm_back(grad_normed, inputs, rms_one, gain[0])
-        return grad, summed, out, one + proj, (pass_a, pass_b), beside
+        todo = one + att + proj + mid
+        return grad, summed, todo, (pass_a, pass_b), ffn_pair, attn_pair, beside
 
     core = c.astype(jnp.int32).reshape(1)
     ffn_one = gather_ffn(0)
@@ -1226,47 +1292,58 @@
         grad = lax.dynamic_update_index_in_dim(grad, other[k], lane ^ k, 0)
     grad = join_stripes(grad).astype(F32) * valid
     layer_out = exchange_z(cut_stripes(final.astype(BF)))
-    grad, ffn_two_sum, out_sum, todo, passed, layer_out = backward_layer(
-        grad, (turned_two, out_two, gain_two), ffn_two, kept_two, None, [], None, layer_out
+    grad, ffn_two_sum, todo, passed, _, _, layer_out = backward_layer(
+        grad, (turned_two, out_two, gain_two), ffn_two, kept_two, None, None, layer_out
     )
     grad, *todo = fence(grad, *todo)
-    sums_two = [out_sum] + qkv_sums(todo[:2], todo[2:])
-    grad, layer_out = send_all(sums_two[1:], grad, layer_out)
+    todo = [tuple(todo[n : n + 2]) for n in (0, 2, 4, 6)]
+    (attn_two,) = attn_grads(*todo, [[[(0, 3 * width, 0, 0)]], [[(0, width, 0, 3 * width)]]])
+    attn_two, grad, layer_out = fence(attn_two, grad, layer_out)
+    attn_two = sum_z(attn_two)
     layer_out = exchange(layer_out)
-    grad, ffn_one_sum, out_sum, todo, _, layer_out = backward_layer(
+    grad, ffn_one_sum, todo, _, ffn_pair_two, attn_pair_two, layer_out = backward_layer(
         grad,
         (turned_one, out_one, gain_one),
         ffn_one,
         kept_one,
         passed,
-        sums_two,
-        ffn_two_sum,
+        (ffn_two_sum, attn_two),
         layer_out,
     )
     layer_out = join_blocks(layer_out)
     grad, *todo = fence(grad, *todo)
-    input_grad = exchange_z(cut_stripes(grad.astype(BF)))
-    last = qkv_sums(todo[:2], todo[2:])
-    (input_grad,) = send_all(last, input_grad)
+    todo = [tuple(todo[n : n + 2]) for n in (0, 2, 4, 6)]
+    places = [[[(0, 2 * width, 0, 0), (2 * width, width, 1, 0)]], [[(0, width, 1, width)]]]
+    attn_pair_one = [
+        Reduction(part.reshape(4, 2, 2, 32, -1), order)
+        for part, order in zip(attn_grads(*todo, places), ("yxz", "xyz"))
+    ]
+    (grad,) = send_all(attn_pair_one, grad)
+    input_grad = cut_stripes(grad.astype(BF))
+    add_all(attn_pair_two, *[r.partial for r in attn_pair_one])
+    send_all(attn_pair_two)
+    add_all(attn_pair_one, *[r.partial for r in attn_pair_two])
+    send_all(attn_pair_one)
+    mark = [r.partial for r in attn_pair_one]
+    ffn_one_sum, input_grad, *mark = fence(ffn_one_sum, input_grad, *mark)
+    ffn_pair_one = pair_sums(ffn_one_sum)
+    (input_grad,) = send_all(ffn_pair_one, input_grad)
+    input_grad = exchange_z(input_grad)
+    add_all(attn_pair_one)
+    send_all(attn_pair_one)
+    (input_grad,) = add_all(ffn_pair_one, input_grad)
+    (input_grad,) = send_all(ffn_pair_one, input_grad)
     input_grad = exchange(input_grad)
-    rest = ffn_one_sum + [out_sum]
-    add_all(rest, *[r.partial for r in last])
-    send_all(rest)
-    for _ in range(2):
-        add_all(last)
-        send_all(last)
-        add_all(rest, *[r.partial for r in last])
-        send_all(rest)
-    add_all(last + rest)
+    add_all(attn_pair_two + ffn_pair_one)
+    add_all(attn_pair_one)
     input_grad = join_blocks(input_grad).astype(F32)
-    sums_one = [out_sum] + last
-    sums_two, late, lower = sums_two[:3], sums_two[3:], ffn_one_sum
 
     out_grad, qkv_grad, gate_grad, up_grad, down_grad = [], [], [], [], []
-    for sums, halves_of in ((sums_one, lower), (sums_two, late)):
-        out_grad.append(sums[0].partial)
-        qkv_grad.append(jnp.concatenate([sums[1].partial, sums[2].partial], axis=1))
-        field = jnp.concatenate([r.partial for r in halves_of], axis=1)
+    for attn_pair, ffn_pair in ((attn_pair_one, ffn_pair_one), (attn_pair_two, ffn_pair_two)):
+        field = jnp.concatenate([r.partial for r in attn_pair], axis=1)
+        qkv_grad.append(field[:, : 3 * width])
+        out_grad.append(field[:, 3 * width :])
+        field = jnp.concatenate([r.partial for r in ffn_pair], axis=1)
         gate_grad.append(field[:, :ffn])
         up_grad.append(field[:, ffn : 2 * ffn])
         down_grad.append(unpack(field[:, 2 * ffn :]))

time: 1110 us -> 1030 us (0.928)
  waiting for transfers between devices: 230 us -> 301 us
  starting transfers between devices: 222 us -> 162 us
  Pallas kernels: 290 us -> 248 us
  local copies, waits for them, and re-layouts: 149 us -> 110 us
  other arithmetic: 78.5 us -> 64.4 us
    all_to_all x17, waiting for transfers between devices: 75.9 us -> 124 us  [exchange(): return lax.all_to_all(field, PLANE, 0, 0, tiled=True)]
    pallas_call x12 -> x4, Pallas kernels: 89.6 us -> 48.3 us  [weight_grads(): pl.pallas_call(kernel, in_specs=[SMEM] + [ANY] * inputs, out_specs=[ANY]...]
    ppermute x27 -> x15, starting transfers between devices: 60.6 us -> 23.4 us  [hop(): return lax.ppermute(value, 'z', [(i, i ^ offset) for i in range(4)])]
    all_to_all x3, waiting for transfers between devices: 5.88 us -> 31.3 us  [exchange_z(): lax.all_to_all(field.reshape((4, 2) + shape[1:]), 'z', 0, 0, tiled=True)]
    unnamed x384 -> x314, local copies, waits for them, and re-layouts: 63.1 us -> 38.2 us
    convert_element_type x16 -> x10, other arithmetic: 25.1 us -> 10.2 us  [add(): self.partial = total.astype(BF) if self.order else total]
    all_to_all x17, starting transfers between devices: 85.9 us -> 72.9 us  [exchange(): return lax.all_to_all(field, PLANE, 0, 0, tiled=True)]
    slice x6, local copies, waits for them, and re-layouts: 11.6 us -> 0.36 us  [the longest x3 0.18 us: pair_sums(): summed[..., :half]]
  transfers between devices with their start and end apart: 120 -> 105, of which waited for: 36 -> 38; matrix products, arithmetic and copies ran while one was open for 25% -> 23% of each run, Pallas kernels for 25% -> 23%
where the time goes in v3:
time: 1030 us; the launch traced here: 1010 us
  waiting for transfers between devices  301 us (29%)
  Pallas kernels  248 us (24%)
  starting transfers between devices  162 us (16%)
  matrix products  112 us (11%)
  local copies, waits for them, and re-layouts  110 us (11%)
  other arithmetic  64.4 us (6%)
  between operations  16.8 us (2%)
    all_to_all x17, waiting for transfers between devices, exchange(): return lax.all_to_all(field, PLANE, 0, 0, tiled=True)  124 us
    ppermute x55, waiting for transfers between devices, swap(): return lax.ppermute(value, axis, [(0, 1), (1, 0)])  84.1 us
    pallas_call x4, Pallas kernels, attend_back(): pl.pallas_call(kernel, grid=(tiles,), in_specs=in_specs, out_specs=out_sp...  80.1 us
    pallas_call x4, Pallas kernels, attend(): pl.pallas_call(kernel, grid=(tiles,), in_specs=[SMEM, ANY], out_specs=[pl...  78.2 us
    all_to_all x17, starting transfers between devices, exchange(): return lax.all_to_all(field, PLANE, 0, 0, tiled=True)  72.9 us
    pallas_call x4, Pallas kernels, weight_grads(): pl.pallas_call(kernel, in_specs=[SMEM] + [ANY] * inputs, out_specs=[ANY]...  48.3 us
    all_gather x3, waiting for transfers between devices, gather_all(): return lax.all_gather(shard, ALL, axis=0, tiled=True)  40.8 us
    dot_general x8, matrix products, dots(): part = lax.dot_general(grad, weight, NT, preferred_element_type=F32)  40.1 us
  transfers between devices with their start and end apart: 105, of which 38 were waited for; matrix products, arithmetic and copies ran while one was open for 23% of the time, Pallas kernels for 23%

profile of v3, /device:TPU:0, one launch (start us, length us, event | category | flops | bytes accessed | tf_op | source)
XLA Modules:
  0.0 1015.0 jit_solution(16164165238967570290)
XLA Ops:
  68.6 8.8 collective-permute-done.29.rest_6_
  138.3 30.1 %all-to-all-done.2 = bf16[8,3,256,128]{3,2,1,0:T(8,128)(2,1)S(1)} async-done(((bf16[8,3,256,128]{3,2,1,0:T(8,128)(2,1)}), bf16[8,3,256,128]{3,2,1,0:T(8,128)(2,1)S(1)}, u32[]{:S(2)}, u32[]{:S(2)}) %all-to-all-start.2) | async-done | bytes 1572896 | tf_op jit(solution)/shard_map/all_to_all | solution.py:1005
  176.3 15.2 %attend.4 = (bf16[8,16,16,128]{3,2,1,0:T(8,128)(2,1)S(1)}, f32[8,2048]{1,0:T(8,128)S(1)}) custom-call(s32[1]{0:T(128)} %bitcast.7.len_ref.refs_0_, bf16[8,3,16,16,128]{4,3,2,1,0:T(8,128)(2,1)S(1)} %bitcast.414), custom_call_target="tpu_custom_call" | custom-call | tf_op jit(solution)/shard_map/attend/pallas_call | solution.py:420
  192.4 8.0 all-to-all-start.4
  200.5 22.9 %attend.5 = (bf16[8,16,16,128]{3,2,1,0:T(8,128)(2,1)}, f32[8,2048]{1,0:T(8,128)S(1)}) custom-call(s32[1]{0:T(128)} %bitcast.42.len_ref.refs_0_, bf16[8,3,16,16,128]{4,3,2,1,0:T(8,128)(2,1)S(1)} %bitcast.412), custom_call_target="tpu_custom_call" | custom-call | tf_op jit(solution)/shard_map/attend/pallas_call | solution.py:420
  228.4 13.1 %all-to-all-done.5 = bf16[8,256,128]{2,1,0:T(8,128)(2,1)S(1)} async-done(((bf16[8,256,128]{2,1,0:T(8,128)(2,1)}), bf16[8,256,128]{2,1,0:T(8,128)(2,1)S(1)}, u32[]{:S(2)}, u32[]{:S(2)}) %all-to-all-start.5) | async-done | bytes 524320 | tf_op jit(solution)/shard_map/all_to_all | solution.py:1005
  269.1 8.1 multiply_reduce_fusion.5
  301.7 13.8 %all-to-all-done.6 = bf16[8,3,256,128]{3,2,1,0:T(8,128)(2,1)S(1)} async-done(((bf16[8,3,256,128]{3,2,1,0:T(8,128)(2,1)}), bf16[8,3,256,128]{3,2,1,0:T(8,128)(2,1)S(1)}, u32[]{:S(2)}, u32[]{:S(2)}) %all-to-all-start.6) | async-done | bytes 1572896 | tf_op jit(solution)/shard_map/all_to_all | solution.py:1005
  319.8 15.9 %attend.6 = (bf16[8,16,16,128]{3,2,1,0:T(8,128)(2,1)}, f32[8,2048]{1,0:T(8,128)S(1)}) custom-call(s32[1]{0:T(128)} %bitcast.7.len_ref.refs_0_, bf16[8,3,16,16,128]{4,3,2,1,0:T(8,128)(2,1)S(1)} %bitcast.410), custom_call_target="tpu_custom_call" | custom-call | tf_op jit(solution)/shard_map/attend/pallas_call | solution.py:420
  335.8 20.0 %all-to-all-done.7 = bf16[8,3,256,128]{3,2,1,0:T(8,128)(2,1)} async-done(((bf16[8,3,256,128]{3,2,1,0:T(8,128)(2,1)}), bf16[8,3,256,128]{3,2,1,0:T(8,128)(2,1)}, u32[]{:S(2)}, u32[]{:S(2)}) %all-to-all-start.7) | async-done | bytes 1572896 | tf_op jit(solution)/shard_map/all_to_all | solution.py:1005
  359.4 24.1 %attend.7 = (bf16[8,16,16,128]{3,2,1,0:T(8,128)(2,1)}, f32[8,2048]{1,0:T(8,128)S(1)}) custom-call(s32[1]{0:T(128)} %bitcast.42.len_ref.refs_0_, bf16[8,3,16,16,128]{4,3,2,1,0:T(8,128)(2,1)} %bitcast.58.piece_ref.refs_1_), custom_call_target="tpu_custom_call" | custom-call | tf_op jit(solution)/shard_map/attend/pallas_call | solution.py:420
  408.0 37.3 %all-gather.8.cloned.1.call-done = bf16[1024,8704]{1,0:T(8,128)(2,1)} async-done(((bf16[32,8704]{1,0:T(8,128)(2,1)}), bf16[1024,8704]{1,0:T(8,128)(2,1)}) %all-gather.8.cloned.1.call-update) | async-done | bytes 17825808 | tf_op jit(solution)/shard_map/all_gather | solution.py:1026
  450.3 7.8 fusion.8
  458.5 7.8 multiply_convert_fusion.4
  505.2 24.0 %all-to-all-done.10 = bf16[4,2,2,2,16,1024]{5,4,3,1,2,0:T(8,128)(2,1)} async-done(((bf16[4,2,2,2,16,1024]{5,4,3,1,2,0:T(8,128)(2,1)}), bf16[4,2,2,2,16,1024]{5,4,3,1,2,0:T(8,128)(2,1)}, u32[]{:S(2)}, u32[]{:S(2)}) %all-to-all-start.10) | async-done | bytes 1048608 | tf_op jit(solution)/shard_map/all_to_all | solution.py:1009
  531.6 15.2 %weight_grads.4 = bf16[4,2,64,8704]{3,2,1,0:T(8,128)(2,1)} custom-call(s32[1]{0:T(128)} %bitcast.core_ref, bf16[512,1024]{1,0:T(8,128)(2,1)S(1)} %multiply_convert_fusion.6.refs_0_, bf16[512,1024]{1,0:T(8,128)(2,1)} %collective-permute-done.39.refs_1_, bf16[512,2816]{1,0:T(8,128)(2,1)} %get-tuple-element.189.refs_2_, ...), custom_call_target="tpu_custom_call" | custom-call | tf_op jit(solution)/shard_map/weight_grads/pallas_call | solution.py:323
  576.4 8.2 all-to-all-done.11
  587.0 11.5 %attend_back.4 = (bf16[8,3,16,16,128]{4,3,2,1,0:T(8,128)(2,1)}, f32[2048,128]{1,0:T(8,128)S(1)}) custom-call(s32[1]{0:T(128)} %bitcast.7.len_ref.refs_0_, bf16[8,3,16,16,128]{4,3,2,1,0:T(8,128)(2,1)} %bitcast.411, bf16[8,16,16,128]{3,2,1,0:T(8,128)(2,1)} %get-tuple-element.169.refs_2_, bf16[8,16,16,128]{3,2,1,0:T(8,128)(2,1)S(1)} %get-tuple-element.342.refs_3_, ...), custom_call_target="tpu_custom_call" | custom-call | tf_op jit(solution)/shard_map/attend_back/pallas_call | solution.py:592
  604.2 28.5 %attend_back.5 = (bf16[8,3,16,16,128]{4,3,2,1,0:T(8,128)(2,1)}, f32[2048,128]{1,0:T(8,128)S(1)}) custom-call(s32[1]{0:T(128)} %bitcast.42.len_ref.refs_0_, bf16[8,3,16,16,128]{4,3,2,1,0:T(8,128)(2,1)} %bitcast.58.piece_ref.refs_1_, bf16[8,16,16,128]{3,2,1,0:T(8,128)(2,1)} %get-tuple-element.173.refs_2_, ...), custom_call_target="tpu_custom_call" | custom-call | tf_op jit(solution)/shard_map/attend_back/pallas_call | solution.py:592
  641.9 16.8 %all-to-all-done.13 = bf16[8,3,256,128]{3,2,1,0:T(8,128)(2,1)} async-done(((bf16[8,3,256,128]{3,2,1,0:T(8,128)(2,1)}), bf16[8,3,256,128]{3,2,1,0:T(8,128)(2,1)}, u32[]{:S(2)}, u32[]{:S(2)}) %all-to-all-start.13) | async-done | bytes 1572896 | tf_op jit(solution)/shard_map/all_to_all | solution.py:1005
  677.1 8.9 weight_grads.5
  686.2 11.0 %multiply_convert_fusion = (bf16[512,2816]{1,0:T(8,128)(2,1)}, bf16[512,2816]{1,0:T(8,128)(2,1)}) fusion(f32[512,2816]{1,0:T(8,128)} %fusion.16, f32[512,2816]{1,0:T(8,128)} %get-tuple-element.413, bf16[512,1024]{1,0:T(8,128)(2,1)S(1)} %convert_element_type.370.refs_8_, bf16[2816,1024]{1,0:T(8,128)(2,1)} %bitcast.454), kind=kOutput, calls=%fused_computation.6 | convolution fusion | flops 2971533312 | bytes 24117248 | tf_op jit(solution)/shard_map/dot_general | solution.py:1205
  710.0 15.2 %weight_grads.6 = bf16[4,2,64,8704]{3,2,1,0:T(8,128)(2,1)} custom-call(s32[1]{0:T(128)} %bitcast.core_ref, bf16[512,1024]{1,0:T(8,128)(2,1)S(1)} %copy-done.9, bf16[512,1024]{1,0:T(8,128)(2,1)} %collective-permute-done.48.refs_1_, bf16[512,2816]{1,0:T(8,128)(2,1)} %get-tuple-element.210.refs_2_, bf16[512,2816]{1,0:T(8,128)(2,1)} %collective-permute-done.49.refs_3_, ...), custom_call_target="tpu_custom_call" | custom-call | tf_op jit(solution)/shard_map/weight_grads/pallas_call | solution.py:323
  725.2 8.3 fusion.10
  733.6 9.0 multiply_reduce_fusion.1
  752.4 14.8 %all-to-all-done.15 = bf16[8,512,128]{2,1,0:T(8,128)(2,1)S(1)} async-done(((bf16[8,512,128]{2,1,0:T(8,128)(2,1)}), bf16[8,512,128]{2,1,0:T(8,128)(2,1)S(1)}, u32[]{:S(2)}, u32[]{:S(2)}) %all-to-all-start.15) | async-done | bytes 1048608 | tf_op jit(solution)/shard_map/all_to_all | solution.py:1005
  775.2 11.6 %attend_back.6 = bf16[8,3,16,16,128]{4,3,2,1,0:T(8,128)(2,1)} custom-call(s32[1]{0:T(128)} %bitcast.7.len_ref.refs_0_, bf16[8,3,16,16,128]{4,3,2,1,0:T(8,128)(2,1)} %bitcast.415, bf16[8,16,16,128]{3,2,1,0:T(8,128)(2,1)S(1)} %copy-done.13, bf16[8,16,16,128]{3,2,1,0:T(8,128)(2,1)S(1)} %get-tuple-element.340.refs_3_, f32[8,2048]{1,0:T(8,128)S(1)} %get-tuple-element.222.refs_4_, ...), custom_call_target="tpu_custom_call" | custom-call | tf_op jit(solution)/shard_map/attend_back/pallas_call | solution.py:592
  795.3 28.6 %attend_back.7 = bf16[8,3,16,16,128]{4,3,2,1,0:T(8,128)(2,1)} custom-call(s32[1]{0:T(128)} %bitcast.42.len_ref.refs_0_, bf16[8,3,16,16,128]{4,3,2,1,0:T(8,128)(2,1)} %bitcast.413, bf16[8,16,16,128]{3,2,1,0:T(8,128)(2,1)} %get-tuple-element.163.refs_2_, bf16[8,16,16,128]{3,2,1,0:T(8,128)(2,1)S(1)} %get-tuple-element.231.refs_3_, ...), custom_call_target="tpu_custom_call" | custom-call | tf_op jit(solution)/shard_map/attend_back/pallas_call | solution.py:592
  835.1 19.6 %collective-permute-done.55 = bf16[32,4352]{1,0:T(8,128)(2,1)S(1)} collective-permute-done((bf16[32,4352]{1,0:T(8,128)(2,1)S(1)}, bf16[32,4352]{1,0:T(8,128)(2,1)S(1)}, u32[]{:S(2)}, u32[]{:S(2)}) %collective-permute-start.55) | collective-permute-done | bytes 278560 | tf_op jit(solution)/shard_map/ppermute | solution.py:68
  877.2 9.0 weight_grads.7
  893.4 20.5 %collective-permute-done.61 = bf16[4,2,32,2048]{3,2,1,0:T(8,128)(2,1)S(1)} collective-permute-done((bf16[4,2,32,2048]{3,2,1,0:T(8,128)(2,1)S(1)}, bf16[4,2,32,2048]{3,2,1,0:T(8,128)(2,1)S(1)}, u32[]{:S(2)}, u32[]{:S(2)}) %collective-permute-start.61) | collective-permute-done | bytes 1048608 | tf_op jit(solution)/shard_map/ppermute | solution.py:68
  972.2 7.3 all-to-all-done.18
  (703 shorter events, 497.3 us)
Async XLA Ops:
  7.2 185.2 %all-gather.4.cloned.1.call-start = ((), (), s32[]{:S(2)}) async-start(), calls=%async_computation.23 | async-start | bytes 20545536 | tf_op jit(solution)/shard_map/all_gather | solution.py:1026
  24.8 33.9 %all-to-all-start = ((bf16[8,2,2,16,1024]{4,3,2,1,0:T(8,128)(2,1)}), bf16[8,2,2,16,1024]{4,3,2,1,0:T(8,128)(2,1)}, u32[]{:S(2)}, u32[]{:S(2)}) async-start(bf16[8,2,2,16,1024]{4,3,2,1,0:T(8,128)(2,1)} %copy.157), calls=%async_computation | async-start | bytes 2097152 | tf_op jit(solution)/shard_map/all_to_all | solution.py:1005
  61.0 52.7 %all-to-all-start.1 = ((bf16[4,2,2,2,16,1024]{5,4,3,1,2,0:T(8,128)(2,1)}), bf16[4,2,2,2,16,1024]{5,4,3,1,2,0:T(8,128)(2,1)}, u32[]{:S(2)}, u32[]{:S(2)}) async-start(bf16[4,2,2,2,16,1024]{5,4,3,1,2,0:T(8,128)(2,1)} %copy.158), calls=%async_computation.1 | async-start | bytes 2097152 | tf_op jit(solution)/shard_map/all_to_all | solution.py:1009
  126.8 41.6 %all-to-all-start.2 = ((bf16[8,3,256,128]{3,2,1,0:T(8,128)(2,1)}), bf16[8,3,256,128]{3,2,1,0:T(8,128)(2,1)S(1)}, u32[]{:S(2)}, u32[]{:S(2)}) async-start(bf16[8,3,256,128]{3,2,1,0:T(8,128)(2,1)} %project_qkv.4.rest_0_), calls=%async_computation.2 | async-start | bytes 3145728 | tf_op jit(solution)/shard_map/all_to_all | solution.py:1005
  172.0 108.8 %all-gather.6.cloned.1.call-start = ((), (), s32[]{:S(2)}) async-start(), calls=%async_computation.24 | async-start | bytes 8921088 | tf_op jit(solution)/shard_map/all_gather | solution.py:1026
  192.4 31.0 %all-to-all-start.4 = ((bf16[8,256,128]{2,1,0:T(8,128)(2,1)}), bf16[8,256,128]{2,1,0:T(8,128)(2,1)S(1)}, u32[]{:S(2)}, u32[]{:S(2)}) async-start(bf16[8,256,128]{2,1,0:T(8,128)(2,1)} %bitcast.424), calls=%async_computation.4 | async-start | bytes 1048576 | tf_op jit(solution)/shard_map/all_to_all | solution.py:1005
  227.6 217.6 %all-gather.8.cloned.1.call-start = ((), (), s32[]{:S(2)}) async-start(), calls=%async_computation.25 | async-start | bytes 18382848 | tf_op jit(solution)/shard_map/all_gather | solution.py:1026
  315.5 40.3 %all-to-all-start.7 = ((bf16[8,3,256,128]{3,2,1,0:T(8,128)(2,1)}), bf16[8,3,256,128]{3,2,1,0:T(8,128)(2,1)}, u32[]{:S(2)}, u32[]{:S(2)}) async-start(bf16[8,3,256,128]{3,2,1,0:T(8,128)(2,1)} %project_qkv.7), calls=%async_computation.7 | async-start | bytes 3145728 | tf_op jit(solution)/shard_map/all_to_all | solution.py:1005
  355.8 27.8 %all-to-all-start.8 = ((bf16[8,256,128]{2,1,0:T(8,128)(2,1)}), bf16[8,256,128]{2,1,0:T(8,128)(2,1)S(1)}, u32[]{:S(2)}, u32[]{:S(2)}) async-start(bf16[8,256,128]{2,1,0:T(8,128)(2,1)} %bitcast.57), calls=%async_computation.8 | async-start | bytes 1048576 | tf_op jit(solution)/shard_map/all_to_all | solution.py:1005
  389.7 77.5 %collective-permute-start.31 = (bf16[2,2,16,1024]{3,2,1,0:T(8,128)(2,1)}, bf16[2,2,16,1024]{3,2,1,0:T(8,128)(2,1)}, u32[]{:S(2)}, u32[]{:S(2)}) collective-permute-start(bf16[2,2,16,1024]{3,2,1,0:T(8,128)(2,1)} %get-tuple-element.350), channel_id=1, source_target_pairs={{0,0},{1,1},{2,16},{3,17},{4,8},{5,9},{6,24},{7,25},{8,4},{9,5},{1... | collective-permute-start | bytes 393224 | tf_op jit(solution)/shard_map/ppermute | solution.py:1281
  391.9 76.8 %collective-permute-start.32 = (bf16[2,2,16,1024]{3,2,1,0:T(8,128)(2,1)}, bf16[2,2,16,1024]{3,2,1,0:T(8,128)(2,1)}, u32[]{:S(2)}, u32[]{:S(2)}) collective-permute-start(bf16[2,2,16,1024]{3,2,1,0:T(8,128)(2,1)} %get-tuple-element.349), channel_id=1, source_target_pairs={{0,1},{1,0},{2,17},{3,16},{4,9},{5,8},{6,25},{7,24},{8,5},{9,4},{1... | collective-permute-start | bytes 393224 | tf_op jit(solution)/shard_map/ppermute | solution.py:1281
  393.9 75.2 %collective-permute-start.33 = (bf16[2,2,16,1024]{3,2,1,0:T(8,128)(2,1)}, bf16[2,2,16,1024]{3,2,1,0:T(8,128)(2,1)}, u32[]{:S(2)}, u32[]{:S(2)}) collective-permute-start(bf16[2,2,16,1024]{3,2,1,0:T(8,128)(2,1)} %get-tuple-element.348), channel_id=1, source_target_pairs={{0,16},{1,17},{2,0},{3,1},{4,24},{5,25},{6,8},{7,9},{8,20},{9,21},... | collective-permute-start | bytes 393224 | tf_op jit(solution)/shard_map/ppermute | solution.py:1281
  397.5 80.2 %collective-permute-start.34 = (bf16[2,2,16,1024]{3,2,1,0:T(8,128)(2,1)S(1)}, bf16[2,2,16,1024]{3,2,1,0:T(8,128)(2,1)}, u32[]{:S(2)}, u32[]{:S(2)}) collective-permute-start(bf16[2,2,16,1024]{3,2,1,0:T(8,128)(2,1)S(1)} %get-tuple-element.347), channel_id=1, source_target_pairs={{0,17},{1,16},{2,1},{3,0},{4,25},{5,24},{6,9},{7,8},{8,21},{9,20},... | collective-permute-start | bytes 393224 | tf_op jit(solution)/shard_map/ppermute | solution.py:1281
  397.5 80.2 %collective-permute-start.35 = (bf16[2,2,16,1024]{3,2,1,0:T(8,128)(2,1)S(1)}, bf16[2,2,16,1024]{3,2,1,0:T(8,128)(2,1)}, u32[]{:S(2)}, u32[]{:S(2)}) collective-permute-start(bf16[2,2,16,1024]{3,2,1,0:T(8,128)(2,1)S(1)} %get-tuple-element.346), channel_id=1, source_target_pairs={{0,8},{1,9},{2,24},{3,25},{4,0},{5,1},{6,16},{7,17},{8,12},{9,13},... | collective-permute-start | bytes 393224 | tf_op jit(solution)/shard_map/ppermute | solution.py:1281
  493.6 37.9 %collective-permute-start.40 = (bf16[512,2816]{1,0:T(8,128)(2,1)}, bf16[512,2816]{1,0:T(8,128)(2,1)}, u32[]{:S(2)}, u32[]{:S(2)}) collective-permute-start(bf16[512,2816]{1,0:T(8,128)(2,1)} %get-tuple-element.189.refs_2_), channel_id=1, source_target_pairs={{0,8},{8,0},{1,9},{9,1},{2,10},{10,2},{3,11},{11,3},{4,12},{12,4},... | collective-permute-start | bytes 8650760 | tf_op jit(solution)/shard_map/ppermute | solution.py:68
  497.1 34.4 %collective-permute-start.41 = (bf16[512,2816]{1,0:T(8,128)(2,1)}, bf16[512,2816]{1,0:T(8,128)(2,1)}, u32[]{:S(2)}, u32[]{:S(2)}) collective-permute-start(bf16[512,2816]{1,0:T(8,128)(2,1)} %get-tuple-element.190.refs_4_), channel_id=1, source_target_pairs={{0,8},{8,0},{1,9},{9,1},{2,10},{10,2},{3,11},{11,3},{4,12},{12,4},... | collective-permute-start | bytes 8650760 | tf_op jit(solution)/shard_map/ppermute | solution.py:68
  497.1 34.4 %collective-permute-start.42 = (bf16[512,2816]{1,0:T(8,128)(2,1)}, bf16[512,2816]{1,0:T(8,128)(2,1)}, u32[]{:S(2)}, u32[]{:S(2)}) collective-permute-start(bf16[512,2816]{1,0:T(8,128)(2,1)} %get-tuple-element.418.refs_6_), channel_id=1, source_target_pairs={{0,8},{8,0},{1,9},{9,1},{2,10},{10,2},{3,11},{11,3},{4,12},{12,4},... | collective-permute-start | bytes 8650760 | tf_op jit(solution)/shard_map/ppermute | solution.py:68
  498.7 30.5 %all-to-all-start.10 = ((bf16[4,2,2,2,16,1024]{5,4,3,1,2,0:T(8,128)(2,1)}), bf16[4,2,2,2,16,1024]{5,4,3,1,2,0:T(8,128)(2,1)}, u32[]{:S(2)}, u32[]{:S(2)}) async-start(bf16[4,2,2,2,16,1024]{5,4,3,1,2,0:T(8,128)(2,1)} %copy.169), calls=%async_computation.10 | async-start | bytes 2097152 | tf_op jit(solution)/shard_map/all_to_all | solution.py:1009
  503.0 264.2 %reduce-scatter.6.cloned.1.call-start = ((), (), s32[]{:S(2)}) async-start(), calls=%async_computation.27 | async-start | bytes 11141120 | tf_op jit(solution)/shard_map/reduce_scatter | solution.py:1173
  503.2 28.4 %collective-permute-start.39 = (bf16[512,1024]{1,0:T(8,128)(2,1)S(1)}, bf16[512,1024]{1,0:T(8,128)(2,1)}, u32[]{:S(2)}, u32[]{:S(2)}) collective-permute-start(bf16[512,1024]{1,0:T(8,128)(2,1)S(1)} %multiply_convert_fusion.6.refs_0_), channel_id=1, source_target_pairs={{0,8},{8,0},{1,9},{9,1},{2,10},{10,2},{3,11},{11,3},{4,12},{12,4},... | collective-permute-start | bytes 3145736 | tf_op jit(solution)/shard_map/ppermute | solution.py:68
  504.6 26.9 %collective-permute-start.43 = (bf16[512,1024]{1,0:T(8,128)(2,1)S(1)}, bf16[512,1024]{1,0:T(8,128)(2,1)}, u32[]{:S(2)}, u32[]{:S(2)}) collective-permute-start(bf16[512,1024]{1,0:T(8,128)(2,1)S(1)} %fusion.21.refs_8_), channel_id=1, source_target_pairs={{0,8},{8,0},{1,9},{9,1},{2,10},{10,2},{3,11},{11,3},{4,12},{12,4},... | collective-permute-start | bytes 3145736 | tf_op jit(solution)/shard_map/ppermute | solution.py:68
  599.5 34.2 %all-to-all-start.12 = ((bf16[8,3,256,128]{3,2,1,0:T(8,128)(2,1)}), bf16[8,3,256,128]{3,2,1,0:T(8,128)(2,1)}, u32[]{:S(2)}, u32[]{:S(2)}) async-start(bf16[8,3,256,128]{3,2,1,0:T(8,128)(2,1)} %bitcast.473), calls=%async_computation.12 | async-start | bytes 3145728 | tf_op jit(solution)/shard_map/all_to_all | solution.py:1005
  637.9 221.2 %reduce-scatter.8.cloned.1.call-start = ((), (), s32[]{:S(2)}) async-start(), calls=%async_computation.28 | async-start | bytes 5242880 | tf_op jit(solution)/shard_map/reduce_scatter | solution.py:1173
  662.2 43.5 %collective-permute-start.51 = (bf16[512,2816]{1,0:T(8,128)(2,1)}, bf16[512,2816]{1,0:T(8,128)(2,1)}, u32[]{:S(2)}, u32[]{:S(2)}) collective-permute-start(bf16[512,2816]{1,0:T(8,128)(2,1)} %copy-done.75), channel_id=1, source_target_pairs={{0,8},{8,0},{1,9},{9,1},{2,10},{10,2},{3,11},{11,3},{4,12},{12,4},... | collective-permute-start | bytes 8650760 | tf_op jit(solution)/shard_map/ppermute | solution.py:68
  698.2 50.6 %all-to-all-start.14 = ((bf16[8,2,2,16,1024]{4,3,2,1,0:T(8,128)(2,1)}), bf16[8,2,2,16,1024]{4,3,2,1,0:T(8,128)(2,1)}, u32[]{:S(2)}, u32[]{:S(2)}) async-start(bf16[8,2,2,16,1024]{4,3,2,1,0:T(8,128)(2,1)} %bitcast.462), calls=%async_computation.14 | async-start | bytes 2097152 | tf_op jit(solution)/shard_map/all_to_all | solution.py:1005
  752.4 187.7 %reduce-scatter.4.cloned.1.call-start = ((), (), s32[]{:S(2)}) async-start(), calls=%async_computation.26 | async-start | bytes 11141120 | tf_op jit(solution)/shard_map/reduce_scatter | solution.py:1173
  791.0 32.9 %all-to-all-start.16 = ((bf16[8,3,256,128]{3,2,1,0:T(8,128)(2,1)}), bf16[8,3,256,128]{3,2,1,0:T(8,128)(2,1)}, u32[]{:S(2)}, u32[]{:S(2)}) async-start(bf16[8,3,256,128]{3,2,1,0:T(8,128)(2,1)} %bitcast.452), calls=%async_computation.18 | async-start | bytes 3145728 | tf_op jit(solution)/shard_map/all_to_all | solution.py:1005
  823.9 31.5 %all-to-all-start.17 = ((bf16[8,3,256,128]{3,2,1,0:T(8,128)(2,1)}), bf16[8,3,256,128]{3,2,1,0:T(8,128)(2,1)}, u32[]{:S(2)}, u32[]{:S(2)}) async-start(bf16[8,3,256,128]{3,2,1,0:T(8,128)(2,1)} %bitcast.451), calls=%async_computation.20 | async-start | bytes 3145728 | tf_op jit(solution)/shard_map/all_to_all | solution.py:1005
  828.8 25.9 %collective-permute-start.55 = (bf16[32,4352]{1,0:T(8,128)(2,1)S(1)}, bf16[32,4352]{1,0:T(8,128)(2,1)S(1)}, u32[]{:S(2)}, u32[]{:S(2)}) collective-permute-start(bf16[32,4352]{1,0:T(8,128)(2,1)S(1)} %dynamic-slice_bitcast_fusion.15), channel_id=1, source_target_pairs={{0,16},{16,0},{1,17},{17,1},{2,18},{18,2},{3,19},{19,3},{4,20},{20... | collective-permute-start | bytes 835592 | tf_op jit(solution)/shard_map/ppermute | solution.py:68
  944.7 34.8 %all-to-all-start.18 = ((bf16[4,2,2,2,16,1024]{5,4,3,1,2,0:T(8,128)(2,1)}), bf16[4,2,2,2,16,1024]{5,4,3,1,2,0:T(8,128)(2,1)S(1)}, u32[]{:S(2)}, u32[]{:S(2)}) async-start(bf16[4,2,2,2,16,1024]{5,4,3,1,2,0:T(8,128)(2,1)} %copy.190), calls=%async_computation.21 | async-start | bytes 2097152 | tf_op jit(solution)/shard_map/all_to_all | solution.py:1009
  957.9 33.7 %collective-permute-start.76 = (bf16[32,2048]{1,0:T(8,128)(2,1)}, bf16[32,2048]{1,0:T(8,128)(2,1)}, u32[]{:S(2)}, u32[]{:S(2)}) collective-permute-start(bf16[32,2048]{1,0:T(8,128)(2,1)} %get-tuple-element.383), channel_id=1, source_target_pairs={{0,1},{1,0},{2,3},{3,2},{4,5},{5,4},{6,7},{7,6},{8,9},{9,8},{10,11... | collective-permute-start | bytes 393224 | tf_op jit(solution)/shard_map/ppermute | solution.py:68
  963.9 27.7 %collective-permute-start.75 = (bf16[32,2048]{1,0:T(8,128)(2,1)}, bf16[32,2048]{1,0:T(8,128)(2,1)}, u32[]{:S(2)}, u32[]{:S(2)}) collective-permute-start(bf16[32,2048]{1,0:T(8,128)(2,1)} %get-tuple-element.385), channel_id=1, source_target_pairs={{0,16},{16,0},{1,17},{17,1},{2,18},{18,2},{3,19},{19,3},{4,20},{20... | collective-permute-start | bytes 393224 | tf_op jit(solution)/shard_map/ppermute | solution.py:68
  (227 other events, 2415.1 us)
Sparse Core Ops, SparseCore 0:
  13.1 175.1 all-gather.3
  192.6 88.1 all-gather.5
  284.2 160.9 all-gather.7
  547.0 150.5 reduce-scatter.5
  699.7 77.6 reduce-scatter.7
  779.7 153.2 reduce-scatter.3

commit v4 on v3

--- a/solution.py
+++ b/solution.py
@@ -25,22 +25,29 @@
     return pltpu.CompilerParams(vmem_limit_bytes=VMEM_BYTES, **more)
 
 
-def assemble(where, pieces, relative, with_x):
-    rows, cols = pieces[0].shape[1:]
-    count = len(pieces)
-    lead = (2, 2, 4, 2) if with_x else (2, 2, 4)
+def assemble(where, sides, relatives):
+    rows = sides[0][0].shape[1]
+    widths = [side[0].shape[2] for side in sides]
+    kind = sides[0][0].dtype
+    flat = [piece for side in sides for piece in side]
+    count = len(flat)
 
     def kernel(where_ref, *rest):
-        ins, out, held, sems = rest[:count], rest[count], rest[count + 1], rest[count + 2]
+        ins, out, sems = rest[:count], rest[count], rest[-1]
         y, c, z, x = (where_ref[n] for n in range(4))
         copies, puts = [], []
-        for n in range(count):
-            dy, dc, dx = relative[n]
-            for dz in range(4):
-                slot = (y ^ dy, c ^ dc, z ^ dz) + ((x ^ dx,) if with_x else ())
-                spot = held.at[n, dz]
-                copies.append(pltpu.make_async_copy(ins[n].at[dz], spot, sems.at[0, n, dz]))
-                puts.append(pltpu.make_async_copy(spot, out.at[slot], sems.at[1, n, dz]))
+        n, first = 0, 0
+        for side, relative in enumerate(relatives):
+            held = rest[count + 1 + side]
+            lanes = pl.ds(first, widths[side])
+            first += widths[side]
+            for at, (dy, dc, dx) in enumerate(relative):
+                for dz in range(4):
+                    spot = held.at[at, dz]
+                    target = out.at[y ^ dy, c ^ dc, z ^ dz, x ^ dx, :, lanes]
+                    copies.append(pltpu.make_async_copy(ins[n].at[dz], spot, sems.at[0, n, dz]))
+                    puts.append(pltpu.make_async_copy(spot, target, sems.at[1, n, dz]))
+                n += 1
         for copy in copies:
             copy.start()
         for copy, put in zip(copies, puts):
@@ -53,15 +60,15 @@
         kernel,
         in_specs=[SMEM] + [ANY] * count,
         out_specs=ANY,
-        out_shape=jax.ShapeDtypeStruct(lead + (rows, cols), pieces[0].dtype),
+        out_shape=jax.ShapeDtypeStruct((2, 2, 4, 2, rows, sum(widths)), kind),
         scratch_shapes=[
-            pltpu.VMEM((count, 4, rows, cols), pieces[0].dtype),
-            pltpu.SemaphoreType.DMA((2, count, 4)),
-        ],
+            pltpu.VMEM((len(side), 4, rows, width), kind) for side, width in zip(sides, widths)
+        ]
+        + [pltpu.SemaphoreType.DMA((2, count, 4))],
         compiler_params=params(),
         name="assemble",
-    )(where, *pieces)
-    return out.reshape(-1, cols)
+    )(where, *flat)
+    return out.reshape(-1, sum(widths))
 
 
 def swap(value, axis):
@@ -83,7 +90,7 @@
         for dc, held in ((0, piece), (1, swap(piece, "c"))):
             pieces.append(held)
             relative.append((moved["y"], dc, moved["x"]))
-    return assemble(where, pieces, relative, True)
+    return assemble(where, [pieces], [relative])
 
 
 def fence(*values):
@@ -153,13 +160,19 @@
     return field * cosine + other * signed_sine
 
 
-def project_qkv(normed, weights, cosine, signed_sine, first_value):
-    rows, width = normed.shape
+def project_qkv(inputs, gain, weights, cosine, signed_sine, first_value):
+    rows, width = inputs.shape
     devices = width // 128
 
-    def kernel(normed_ref, w_q_ref, w_k_ref, w_v_ref, cos_ref, sin_ref, *rest):
-        out_ref = rest[-1]
+    def kernel(in_ref, gain_ref, w_q_ref, w_k_ref, w_v_ref, cos_ref, sin_ref, *rest):
+        out_ref, normed_ref = rest[-2:]
         step = pl.program_id(0)
+
+        @pl.when(step == 0)
+        def _():
+            field = in_ref[...].astype(F32)
+            rms = lax.rsqrt(jnp.mean(field * field, axis=1, keepdims=True) + EPSILON)
+            normed_ref[...] = (field * rms * gain_ref[0:1, :]).astype(BF)
 
         def product(w_ref):
             return jnp.dot(normed_ref[...], w_ref[...], preferred_element_type=F32)
@@ -188,11 +201,11 @@
                 out_ref[n, 0] = part.astype(BF)
 
     whole = lambda step: (0, 0)
-    in_specs = [pl.BlockSpec((rows, width), whole)]
+    in_specs = [pl.BlockSpec((rows, width), whole), pl.BlockSpec((2, width), whole)]
     for _, start in weights:
         in_specs.append(pl.BlockSpec((width, width), lambda step, start=start: (0, start)))
     in_specs += [pl.BlockSpec((rows, 128), whole)] * 2
-    operands = [normed] + [array for array, _ in weights] + [cosine, signed_sine]
+    operands = [inputs, gain] + [array for array, _ in weights] + [cosine, signed_sine]
     if first_value is not None:
         in_specs.append(pl.BlockSpec((devices, 1, rows, 128), lambda step: (0, 2, 0, 0)))
         operands.append(first_value)
@@ -200,11 +213,136 @@
         kernel,
         grid=(3,),
         in_specs=in_specs,
-        out_specs=pl.BlockSpec((devices, 1, rows, 128), lambda step: (0, step, 0, 0)),
-        out_shape=jax.ShapeDtypeStruct((devices, 3, rows, 128), BF),
+        out_specs=[
+            pl.BlockSpec((devices, 1, rows, 128), lambda step: (0, step, 0, 0)),
+            pl.BlockSpec((rows, width), whole),
+        ],
+        out_shape=[
+            jax.ShapeDtypeStruct((devices, 3, rows, 128), BF),
+            jax.ShapeDtypeStruct((rows, width), BF),
+        ],
         compiler_params=params(dimension_semantics=("arbitrary",)),
         name="project_qkv",
     )(*operands)
+
+
+def forward_ffn(low, inputs, w_o, w_gu, w_d, gain, ffn, kept, first_row, total_rows):
+    rows, width = inputs.shape
+    devices = low.shape[0]
+    half = ffn // 2
+    w_o, out_column = w_o
+    kinds = [
+        ((total_rows, width), BF),
+        ((total_rows, width), F32),
+        ((total_rows, width), BF),
+        ((total_rows, ffn), BF),
+        ((total_rows, ffn), BF),
+        ((total_rows, ffn), BF),
+    ]
+    count = len(kinds)
+
+    def kernel(low_ref, in_ref, wo_ref, wgu_ref, wd_ref, gain_ref, *refs):
+        if kept is not None:
+            refs = refs[count:]
+        outs, refs = refs[: count + 1], refs[count + 1 :]
+        att, wo, wg, wu, wd, mid, norm, gates, ups, hids, result, sems, out_sems = refs
+        spans = [slice(0, half), slice(half, ffn)]
+        loads = [
+            pltpu.make_async_copy(
+                low_ref.at[n], att.at[:, pl.ds(128 * n, 128)], sems.at[n]
+            )
+            for n in range(devices)
+        ]
+        loads.append(
+            pltpu.make_async_copy(wo_ref.at[:, pl.ds(out_column, width)], wo, sems.at[devices])
+        )
+        late = []
+        for n in range(2):
+            at = devices + 1 + 3 * n
+            column = pl.ds(n * half, half)
+            late.append(
+                [
+                    pltpu.make_async_copy(wgu_ref.at[:, column], wg.at[n], sems.at[at]),
+                    pltpu.make_async_copy(
+                        wgu_ref.at[:, pl.ds(ffn + n * half, half)], wu.at[n], sems.at[at + 1]
+                    ),
+                    pltpu.make_async_copy(wd_ref.at[column], wd.at[n], sems.at[at + 2]),
+                ]
+            )
+        for copy in loads + late[0] + late[1]:
+            copy.start()
+        puts = []
+
+        def put(source, target, index):
+            copy = pltpu.make_async_copy(source, target, out_sems.at[len(puts)])
+            copy.start()
+            puts.append(copy)
+
+        own = pl.ds(first_row, rows)
+        for copy in loads:
+            copy.wait()
+        put(att, outs[0].at[own], 0)
+        middle = in_ref[...] + jnp.dot(att[...], wo[...], preferred_element_type=F32)
+        mid[...] = middle
+        put(mid, outs[1].at[own], 1)
+        rms = lax.rsqrt(jnp.mean(middle * middle, axis=1, keepdims=True) + EPSILON)
+        normed = (middle * rms * gain_ref[1:2, :]).astype(BF)
+        norm[...] = normed
+        put(norm, outs[2].at[own], 2)
+        total = middle
+        for n in range(2):
+            late[n][0].wait()
+            gate = jnp.dot(norm[...], wg[n], preferred_element_type=F32)
+            late[n][1].wait()
+            up = jnp.dot(norm[...], wu[n], preferred_element_type=F32)
+            hidden = (gate * jax.nn.sigmoid(gate) * up).astype(BF)
+            gates[:, spans[n]] = gate.astype(BF)
+            ups[:, spans[n]] = up.astype(BF)
+            hids[:, spans[n]] = hidden
+            late[n][2].wait()
+            total = total + jnp.dot(hidden, wd[n], preferred_element_type=F32)
+        put(gates, outs[3].at[own], 3)
+        put(ups, outs[4].at[own], 4)
+        put(hids, outs[5].at[own], 5)
+        result[...] = total
+        put(result, outs[6], 6)
+        for copy in puts:
+            copy.wait()
+
+    vmem = pl.BlockSpec(memory_space=pltpu.VMEM)
+    operands = [low, inputs, w_o, w_gu, w_d, gain]
+    in_specs = [ANY, vmem, ANY, ANY, ANY, vmem]
+    aliases = {}
+    if kept is not None:
+        aliases = {len(operands) + n: n for n in range(count)}
+        operands += list(kept)
+        in_specs += [ANY] * count
+    outs = pl.pallas_call(
+        kernel,
+        in_specs=in_specs,
+        out_specs=[ANY] * (count + 1),
+        out_shape=[jax.ShapeDtypeStruct(*kind) for kind in kinds]
+        + [jax.ShapeDtypeStruct((rows, width), F32)],
+        scratch_shapes=[
+            pltpu.VMEM((rows, width), BF),
+            pltpu.VMEM((width, width), BF),
+            pltpu.VMEM((2, width, half), BF),
+            pltpu.VMEM((2, width, half), BF),
+            pltpu.VMEM((2, half, width), BF),
+            pltpu.VMEM((rows, width), F32),
+            pltpu.VMEM((rows, width), BF),
+            pltpu.VMEM((rows, ffn), BF),
+            pltpu.VMEM((rows, ffn), BF),
+            pltpu.VMEM((rows, ffn), BF),
+            pltpu.VMEM((rows, width), F32),
+            pltpu.SemaphoreType.DMA((devices + 7,)),
+            pltpu.SemaphoreType.DMA((count + 1,)),
+        ],
+        input_output_aliases=aliases,
+        compiler_params=params(),
+        name="forward_ffn",
+    )(*operands)
+    return outs[count], outs[:count]
 
 
 def weight_grads(core, groups, chunks):
@@ -336,10 +474,10 @@
 
 
 def attend(length, pieces):
-    tile = 256
+    tile, wide_tile = 256, 512
     slots = pieces.shape[2] * 128
-    tiles = slots // tile
-    per = tile // 128
+    tiles, steps = slots // tile, slots // wide_tile
+    per, wide_per, ratio = tile // 128, wide_tile // 128, wide_tile // tile
 
     def kernel(len_ref, piece_ref, out_ref, lse_ref, held, flipped, logit, sems):
         step = pl.program_id(0)
@@ -364,8 +502,8 @@
                 flipped[block] = key.T
 
         used = len_ref[0]
-        query = rows_of(held[0, pl.ds(per * step, per)]) * BF(0.125)
-        lane = lax.broadcasted_iota(jnp.int32, (tile, 128), 1)
+        query = rows_of(held[0, pl.ds(wide_per * step, wide_per)]) * BF(0.125)
+        lane = lax.broadcasted_iota(jnp.int32, (wide_tile, 128), 1)
         low = lane < 64
         zero = jnp.zeros_like(query)
         queries = [jnp.where(low, query, zero), jnp.where(low, zero, query)]
@@ -376,7 +514,7 @@
             for head in range(2):
                 field = jnp.dot(queries[head], key_t, preferred_element_type=F32)
                 if masked:
-                    query_pos = step * tile + lax.broadcasted_iota(jnp.int32, field.shape, 0)
+                    query_pos = step * wide_tile + lax.broadcasted_iota(jnp.int32, field.shape, 0)
                     key_pos = block * tile + lax.broadcasted_iota(jnp.int32, field.shape, 1)
                     seen = (key_pos <= query_pos) & (key_pos < used)
                     field = jnp.where(seen, field, NEGATIVE)
@@ -385,18 +523,19 @@
                 result.append(jnp.maximum(tops[head], top))
             return tuple(result)
 
-        full = jnp.minimum(step, used // tile)
-        end = jnp.minimum(step + 1, (used + tile - 1) // tile)
-        low_top = jnp.full((tile, 128), NEGATIVE, F32)
+        full = jnp.minimum(ratio * step, used // tile)
+        end = jnp.minimum(ratio * step + ratio, (used + tile - 1) // tile)
+        low_top = jnp.full((wide_tile, 128), NEGATIVE, F32)
         tops = lax.fori_loop(0, full, lambda b, s: score(b, s, False), (low_top, low_top))
         tops = lax.fori_loop(full, end, lambda b, s: score(b, s, True), tops)
         tops = [jnp.max(top, axis=1, keepdims=True) for top in tops]
-        wide = [jnp.broadcast_to(top, (tile, tile)) for top in tops]
-        one = jnp.ones_like(query)
+        wide = [jnp.broadcast_to(top, (wide_tile, tile)) for top in tops]
+        low_key = low[:tile]
+        one = jnp.ones((tile, 128), BF)
 
         def mix(block, sums):
             value = rows_of(held[2, pl.ds(per * block, per)])
-            values = [jnp.where(low, value, one), jnp.where(low, one, value)]
+            values = [jnp.where(low_key, value, one), jnp.where(low_key, one, value)]
             result = []
             for head in range(2):
                 probs = jnp.exp(logit[head, block] - wide[head]).astype(BF)
@@ -405,21 +544,21 @@
                 )
             return tuple(result)
 
-        nothing = jnp.zeros((tile, 128), F32)
+        nothing = jnp.zeros((wide_tile, 128), F32)
         sums = lax.fori_loop(0, end, mix, (nothing, nothing))
         totals = [sums[0][:, 64:65], sums[1][:, 0:1]]
         out = jnp.where(low, sums[0] / totals[0], sums[1] / totals[1])
-        out = out.astype(BF).reshape(per, 8, 16, 128)
+        out = out.astype(BF).reshape(wide_per, 8, 16, 128)
         for device in range(8):
-            out_ref[device, pl.ds(per * step, per)] = out[:, device]
+            out_ref[device, pl.ds(wide_per * step, wide_per)] = out[:, device]
         level = jnp.where(low, tops[0] + jnp.log(totals[0]), tops[1] + jnp.log(totals[1])).T
-        start = pl.multiple_of(step * tile, tile)
-        lse_ref[0:1, pl.ds(start, tile)] = level[0:1]
-        lse_ref[1:2, pl.ds(start, tile)] = level[64:65]
+        start = pl.multiple_of(step * wide_tile, wide_tile)
+        lse_ref[0:1, pl.ds(start, wide_tile)] = level[0:1]
+        lse_ref[1:2, pl.ds(start, wide_tile)] = level[64:65]
 
     return pl.pallas_call(
         kernel,
-        grid=(tiles,),
+        grid=(steps,),
         in_specs=[SMEM, ANY],
         out_specs=[
             pl.BlockSpec((8,) + pieces.shape[2:], lambda i: (0, 0, 0, 0)),
@@ -432,7 +571,7 @@
         scratch_shapes=[
             pltpu.VMEM((3, slots // 128, 8, 16, 128), BF),
             pltpu.VMEM((tiles, 128, tile), BF),
-            pltpu.VMEM((2, tiles, tile, tile), F32),
+            pltpu.VMEM((2, tiles, wide_tile, tile), F32),
             pltpu.SemaphoreType.DMA((8,)),
         ],
         compiler_params=params(dimension_semantics=("arbitrary",)),
@@ -441,10 +580,10 @@
 
 
 def attend_back(length, pieces, attended, grads, lse, cosine, signed_sine, passed):
-    tile = 256
+    tile, wide = 256, 512
     slots = pieces.shape[2] * 128
     tiles = slots // tile
-    per = tile // 128
+    per, wide_per, ratio = tile // 128, wide // 128, wide // tile
     upper = passed is None
 
     def kernel(*refs):
@@ -496,14 +635,15 @@
             place = lax.broadcasted_iota(jnp.int32, (8, slots), 1)
             level[...] = jnp.where(place < used, lse_ref[...], -NEGATIVE)
 
-        key = rows_of(held[1, pl.ds(per * step, per)])
-        value = rows_of(held[2, pl.ds(per * step, per)])
-        lane = lax.broadcasted_iota(jnp.int32, (tile, 128), 1)
+        key = rows_of(held[1, pl.ds(wide_per * step, wide_per)])
+        value = rows_of(held[2, pl.ds(wide_per * step, wide_per)])
+        lane = lax.broadcasted_iota(jnp.int32, (wide, 128), 1)
         low = lane < 64
 
         def head_part(field, head):
-            keep = low if head == 0 else jnp.logical_not(low)
-            return jnp.where(keep, field, jnp.zeros_like(field))
+            keep = low[: field.shape[0]]
+            nothing = jnp.zeros_like(field)
+            return jnp.where(keep, field, nothing) if head == 0 else jnp.where(keep, nothing, field)
 
         scaled = key * BF(0.125)
         keys = [head_part(scaled, head) for head in range(2)]
@@ -517,14 +657,14 @@
             start = pl.multiple_of(block * tile, tile)
             spans = pl.ds(start, tile)
             query_sum = jnp.zeros((tile, 128), F32)
-            key_sum = jnp.zeros((tile, 128), F32)
-            value_sum = jnp.zeros((tile, 128), F32)
+            key_sum = jnp.zeros((wide, 128), F32)
+            value_sum = jnp.zeros((wide, 128), F32)
             for head in range(2):
                 logits = lax.dot_general(keys[head], query, NT, preferred_element_type=F32)
                 probs = jnp.exp(logits - level[head : head + 1, spans])
                 if masked:
-                    key_pos = lax.broadcasted_iota(jnp.int32, probs.shape, 0)
-                    query_pos = lax.broadcasted_iota(jnp.int32, probs.shape, 1)
+                    key_pos = step * wide + lax.broadcasted_iota(jnp.int32, probs.shape, 0)
+                    query_pos = block * tile + lax.broadcasted_iota(jnp.int32, probs.shape, 1)
                     probs = jnp.where(key_pos <= query_pos, probs, 0.0)
                 grad_probs = lax.dot_general(
                     values[head], grad_out, NT, preferred_element_type=F32
@@ -545,23 +685,22 @@
 
         end = (used + tile - 1) // tile
 
-        @pl.when(step < end)
-        def _():
-            visit(step, True)
-
-            def body(block, carry):
-                visit(block, False)
-                return carry
-
-            lax.fori_loop(step + 1, end, body, 0)
+        def body(block, carry, masked):
+            visit(block, masked)
+            return carry
+
+        first = ratio * step
+        lax.fori_loop(first, jnp.minimum(first + ratio, end), lambda b, s: body(b, s, True), 0)
+        lax.fori_loop(first + ratio, end, lambda b, s: body(b, s, False), 0)
 
         def put(member, block, field):
-            field = field.astype(BF).reshape(per, 8, 16, 128)
+            count = field.shape[0] // 128
+            field = field.astype(BF).reshape(count, 8, 16, 128)
             for device in range(8):
-                out_ref[device, member, pl.ds(per * block, per)] = field[:, device]
-
-        start = pl.multiple_of(step * tile, tile)
-        spans = pl.ds(start, tile)
+                out_ref[device, member, pl.ds(count * block, count)] = field[:, device]
+
+        start = pl.multiple_of(step * wide, wide)
+        spans = pl.ds(start, wide)
         key_grad = key_acc[...] * 0.125
         put(1, step, turn(key_grad, cos_ref[spans, :], -sin_ref[spans, :]))
         if upper:
@@ -571,7 +710,7 @@
         else:
             put(2, step, value_acc[...] + passed_ref[spans, :])
 
-        @pl.when(step == tiles - 1)
+        @pl.when(step == slots // wide - 1)
         def _():
             for block in range(tiles):
                 part = slice(tile * block, tile * block + tile)
@@ -591,7 +730,7 @@
         operands.append(passed)
     outs = pl.pallas_call(
         kernel,
-        grid=(tiles,),
+        grid=(slots // wide,),
         in_specs=in_specs,
         out_specs=out_specs,
         out_shape=out_shape,
@@ -602,8 +741,8 @@
             pltpu.VMEM((8, slots), F32),
             pltpu.VMEM((8, slots), F32),
             pltpu.VMEM((slots, 128), F32),
-            pltpu.VMEM((tile, 128), F32),
-            pltpu.VMEM((tile, 128), F32),
+            pltpu.VMEM((wide, 128), F32),
+            pltpu.VMEM((wide, 128), F32),
             pltpu.SemaphoreType.DMA((3, 8)),
         ],
         compiler_params=params(dimension_semantics=("arbitrary",)),
@@ -1066,13 +1205,10 @@
         weights = [(w_q, 0), (w_k, 0), (w_v, 0)]
         return weights, [w_q[:, :width], w_k, w_v], gains(w_q[:, width:])
 
-    def gather_second(*after):
-        shard = jnp.concatenate([w_qkv[1], w_out[1], gain_shard(1)], axis=1)
-        shard, *_ = fence(shard, *after)
-        whole = gather_all(shard)
+    def second_weights(whole):
         weights = [(whole, 0), (whole, 1), (whole, 2)]
         turned = [whole[:, : 3 * width]]
-        return weights, turned, whole[:, 3 * width : 4 * width], gains(whole[:, 4 * width :])
+        return weights, turned, (whole, 3 * width), gains(whole[:, 4 * width :])
 
     here = z * 2 + x
     routes = []
@@ -1106,51 +1242,16 @@
     places = (step // 16) * 128 + lane * 16 + step % 16
     valid = (places[None, :] < lengths[:, None]).astype(F32).reshape(rows, 1)
 
-    def halves(field):
-        return field[:stretch], field[stretch:]
-
-    def forward_attention(inputs, weights, gain, first_value, *after):
-        rms_one = lax.rsqrt(jnp.mean(inputs * inputs, axis=-1, keepdims=True) + EPSILON)
-        normed = (inputs * rms_one * gain[0]).astype(BF)
-        top, bottom = halves(normed)
-        parts_a = project_qkv(top, weights, my_cos, my_sin, first_value and first_value[0])
-        parts_b = project_qkv(bottom, weights, my_cos, my_sin, first_value and first_value[1])
-        shape = (8, 3, stretch // 16, 16, 128)
-        pieces_a = exchange(parts_a)
-        pieces_a, sent_b = fence(pieces_a, parts_b)
-        pieces_a = pieces_a.reshape(shape)
-        pieces_b = exchange(sent_b)
-        attended_a, lse_a = attend(length[0], pieces_a)
-        attended_a, pieces_b, *_ = fence(attended_a, pieces_b, *after)
-        pieces_b = pieces_b.reshape(shape)
-        low_a = exchange(attended_a.reshape(8, stretch, 128))
-        attended_b, lse_b = attend(length[1], pieces_b)
-        low_a, sent_b = fence(low_a, attended_b)
-        low_b = exchange(sent_b.reshape(8, stretch, 128))
-        attn_low = jnp.concatenate(
-            [jnp.transpose(low, (1, 0, 2)).reshape(stretch, width) for low in (low_a, low_b)]
-        )
-        kept = (
-            inputs, rms_one, normed, (pieces_a, pieces_b), (attended_a, attended_b), attn_low,
-            (lse_a, lse_b),
-        )
-        return attn_low, (parts_a, parts_b), kept
-
-    def forward_ffn(inputs, attn_low, w_o, w_ffn, gain):
-        w_gu, w_d = w_ffn
-        middle = inputs + jnp.dot(attn_low, w_o, preferred_element_type=F32)
-        rms_two = lax.rsqrt(jnp.mean(middle * middle, axis=-1, keepdims=True) + EPSILON)
-        normed_two = (middle * rms_two * gain[1]).astype(BF)
-        gate = jnp.dot(normed_two, w_gu[:, :ffn], preferred_element_type=F32)
-        up = jnp.dot(normed_two, w_gu[:, ffn : 2 * ffn], preferred_element_type=F32)
-        hidden = (jax.nn.silu(gate) * up).astype(BF)
-        result = middle + jnp.dot(hidden, w_d, preferred_element_type=F32)
-        return result, (middle, rms_two, normed_two, gate, up, hidden)
+    shape = (8, 3, stretch // 16, 16, 128)
+
+    def project(inputs, weights, gain, first_value):
+        return project_qkv(inputs, gain, weights, my_cos, my_sin, first_value)
 
     def near(field):
         return swap(field, "c")
 
-    def norm_back(grad_normed, source, rms, gain):
+    def norm_back(grad_normed, source, gain):
+        rms = lax.rsqrt(jnp.mean(source * source, axis=-1, keepdims=True) + EPSILON)
         scaled = source * rms
         weighted = grad_normed * gain
         return rms * (weighted - scaled * jnp.mean(weighted * scaled, axis=-1, keepdims=True))
@@ -1191,11 +1292,13 @@
 
     def backward_layer(grad_in, w_attn, w_ffn, kept, passed, upper, beside):
         w_turned, w_o, gain = w_attn
+        w_o = w_o[0][:, w_o[1] : w_o[1] + width]
         w_gu, w_d = w_ffn
-        (
-            inputs, rms_one, normed, pieces, attended, attn_low, lse, middle, rms_two,
-            normed_two, gate, up, hidden,
-        ) = kept
+        inputs, normed, pieces, attended, lse, buffers = kept
+        attn_low, middle, normed_two, gate, up, hidden = buffers
+        inputs = jnp.concatenate(inputs).astype(F32)
+        normed = jnp.concatenate(normed)
+        gate, up = gate.astype(F32), up.astype(F32)
         grad_low = grad_in.astype(BF)
         low = (grad_low, near(grad_low))
         hid = (hidden, near(hidden))
@@ -1214,7 +1317,7 @@
         summed, grad_gate, grad_up = fence(summed, grad_gate, grad_up)
         summed = sum_z(summed)
         grad_normed = dots([grad_gate, grad_up], [w_gu[:, :ffn], w_gu[:, ffn : 2 * ffn]])
-        grad_middle = grad_in + norm_back(grad_normed, middle, rms_two, gain[1])
+        grad_middle = grad_in + norm_back(grad_normed, middle, gain[1])
         grad_attn = grad_middle.astype(BF)
         mid = (grad_attn, near(grad_attn))
         grad_o = lax.dot_general(grad_attn, w_o, NT, preferred_element_type=F32).astype(BF)
@@ -1262,36 +1365,108 @@
             cuts.append(grad_proj[:, at : at + weight.shape[1]])
             at += weight.shape[1]
         grad_normed = dots(cuts, w_turned)
-        grad = grad_middle + norm_back(grad_normed, inputs, rms_one, gain[0])
+        grad = grad_middle + norm_back(grad_normed, inputs, gain[0])
         todo = one + att + proj + mid
         return grad, summed, todo, (pass_a, pass_b), ffn_pair, attn_pair, beside
 
     core = c.astype(jnp.int32).reshape(1)
     ffn_one = gather_ffn(0)
-    state = join_stripes(exchange_z(exchange(cut_blocks(tokens)))).astype(F32)
+    state = join_stripes(exchange_z(exchange(cut_blocks(tokens))))
+    in_one = (state[:stretch], state[stretch:])
     qkv_one, turned_one, gain_one = gather_first()
-    low_one, first_value, kept_one = forward_attention(
-        state, qkv_one, gain_one, None, ffn_one[0]
+    out_one = (ffn_one[0], 2 * ffn + 3 * width)
+
+    shard = jnp.concatenate([w_qkv[1], w_out[1], gain_shard(1)], axis=1)
+    parts_a, normed_a = project(in_one[0], qkv_one, gain_one, None)
+    pieces_a = exchange(parts_a)
+    parts_b, normed_b = project(in_one[1], qkv_one, gain_one, None)
+    shard, pieces_a, sent_b = fence(shard, pieces_a, parts_b)
+    hops = [hop(shard, k) for k in (1, 2, 3)]
+    pieces_a = pieces_a.reshape(shape)
+    pieces_b = exchange(sent_b)
+    attended_a, lse_a = attend(length[0], pieces_a)
+    attended_a, pieces_b, ffn_one, *hops = fence(attended_a, pieces_b, ffn_one, *hops)
+    out_one = (ffn_one[0], out_one[1])
+    stack = jnp.stack([shard] + hops)
+    cut = stack.shape[2] // 256 * 128
+    stacks = [stack[..., :cut], stack[..., cut:]]
+    besides = [swap(stacks[0], "x"), swap(stacks[1], "y")]
+    pieces_b = pieces_b.reshape(shape)
+    low_a = exchange(attended_a.reshape(8, stretch, 128))
+    attended_b, lse_b = attend(length[1], pieces_b)
+    ffn_two = gather_ffn(1, attended_a)
+    low_a, sent_b, besides = fence(low_a, attended_b, besides)
+    rings = [
+        [((0, 0), stacks[0]), ((0, 1), besides[0])],
+        [((0, 0), stacks[1]), ((1, 0), besides[1])],
+    ]
+    for axis, ring in zip(("y", "x"), rings):
+        for (dy, dx), piece in list(ring):
+            place = (1, dx) if axis == "y" else (dy, 1)
+            ring.append((place, swap(piece, axis)))
+    low_b = exchange(sent_b.reshape(8, stretch, 128))
+    rest = (ffn_one[0], ffn_one[1], gain_one, ffn)
+    result_a, buffers = forward_ffn(
+        low_a, in_one[0].astype(F32), out_one, *rest, None, 0, rows
     )
-    qkv_two, turned_two, out_two, gain_two = gather_second(ffn_one[0], kept_one[4][0])
-    ffn_two = gather_ffn(1, low_one)
-    out_one = ffn_one[0][:, 2 * ffn + 3 * width :]
-    low_one, other = fence(low_one, cut_blocks(cotangent))
+    held = fence(result_a, *[piece for ring in rings for _, piece in ring])
+    result_a = held[0]
+    rings = [
+        [(place, piece) for (place, _), piece in zip(ring, held[1 + 4 * n : 5 + 4 * n])]
+        for n, ring in enumerate(rings)
+    ]
+    rings = [
+        [
+            ((dy, dc, dx), swap(piece, "c") if dc else piece)
+            for (dy, dx), piece in ring
+            for dc in (0, 1)
+        ]
+        for ring in rings
+    ]
+    relative = [[place for place, _ in ring] for ring in rings]
+    sides = [[piece for _, piece in ring] for ring in rings]
+    whole = assemble(where, sides, relative)
+    kept_one = (in_one, (normed_a, normed_b), (pieces_a, pieces_b), (attended_a, attended_b))
+    kept_one += ((lse_a, lse_b),)
+    qkv_two, turned_two, out_two, gain_two = second_weights(whole)
+
+    next_a, normed_a = project(result_a, qkv_two, gain_two, parts_a)
+    next_a, low_b = fence(next_a, low_b)
+    pieces_a = exchange(next_a)
+    result_b, buffers = forward_ffn(
+        low_b, in_one[1].astype(F32), out_one, *rest, buffers, stretch, rows
+    )
+    kept_one += (buffers,)
+    in_two = (result_a, result_b)
+    next_b, normed_b = project(result_b, qkv_two, gain_two, parts_b)
+    pieces_a, sent_b = fence(pieces_a, next_b)
+    pieces_a = pieces_a.reshape(shape)
+    pieces_b = exchange(sent_b)
+    attended_a, lse_a = attend(length[0], pieces_a)
+    attended_a, pieces_b, other = fence(attended_a, pieces_b, cut_blocks(cotangent))
     other = [
         lax.ppermute(lax.dynamic_index_in_dim(other, here ^ k, 0, keepdims=False), ALL, routes[k])
         for k in range(8)
     ]
-    middle, more = forward_ffn(state, low_one, out_one, ffn_one, gain_one)
-    kept_one += more
-    low_two, _, kept_two = forward_attention(middle, qkv_two, gain_two, first_value)
-    final, more = forward_ffn(middle, low_two, out_two, ffn_two, gain_two)
-    kept_two += more
-    final, *other = fence(final, *other)
+    pieces_b = pieces_b.reshape(shape)
+    low_a = exchange(attended_a.reshape(8, stretch, 128))
+    attended_b, lse_b = attend(length[1], pieces_b)
+    low_a, sent_b, *other = fence(low_a, attended_b, *other)
+    low_b = exchange(sent_b.reshape(8, stretch, 128))
+    rest = (ffn_two[0], ffn_two[1], gain_two, ffn)
+    final_a, buffers = forward_ffn(low_a, result_a, out_two, *rest, None, 0, rows)
+    final_a, low_b = fence(final_a, low_b)
+    moved_a = exchange_z(final_a.astype(BF).reshape(8, 2, 16, width))
+    final_b, buffers = forward_ffn(low_b, result_b, out_two, *rest, buffers, stretch, rows)
+    kept_two = (in_two, (normed_a, normed_b), (pieces_a, pieces_b), (attended_a, attended_b))
+    kept_two += ((lse_a, lse_b), buffers)
+    moved_a, final_b, *other = fence(moved_a, final_b, *other)
+    moved_b = exchange_z(final_b.astype(BF).reshape(8, 2, 16, width))
     grad = jnp.zeros((8, seqs, 2, 16, width), BF)
     for k in range(8):
         grad = lax.dynamic_update_index_in_dim(grad, other[k], lane ^ k, 0)
     grad = join_stripes(grad).astype(F32) * valid
-    layer_out = exchange_z(cut_stripes(final.astype(BF)))
+    layer_out = jnp.stack([moved_a, moved_b], axis=1)
     grad, ffn_two_sum, todo, passed, _, _, layer_out = backward_layer(
         grad, (turned_two, out_two, gain_two), ffn_two, kept_two, None, None, layer_out
     )

time: 1030 us -> 999 us (0.970)
  waiting for transfers between devices: 301 us -> 221 us
  matrix products: 112 us -> 59.9 us
  starting transfers between devices: 162 us -> 205 us
  Pallas kernels: 248 us -> 280 us
  blocking collectives: 0 us -> 17.5 us
    dot_general x8 -> x0, matrix products: 49.2 us -> none  [the longest x2 15 us: forward_ffn(): up = jnp.dot(normed_two, w_gu[:, ffn:2 * ffn], preferred_element_type=F32)]
    all_gather x3 -> x2, waiting for transfers between devices: 40.8 us -> 0.01 us  [gather_all(): return lax.all_gather(shard, ALL, axis=0, tiled=True)]
    all_to_all x17, waiting for transfers between devices: 124 us -> 95.2 us  [exchange(): return lax.all_to_all(field, PLANE, 0, 0, tiled=True)]
    all_to_all x3, waiting for transfers between devices: 31.3 us -> 6.57 us  [exchange_z(): lax.all_to_all(field.reshape((4, 2) + shape[1:]), 'z', 0, 0, tiled=True)]
    pallas_call x12 -> x16, Pallas kernels: 184 us -> 205 us  [the longest x4 68.2 us: attend_back(): pl.pallas_call(kernel, grid=(slots // wide,), in_specs=in_specs, out_spec...]
    ppermute x55 -> x69, waiting for transfers between devices: 84.1 us -> 103 us  [swap(): return lax.ppermute(value, axis, [(0, 1), (1, 0)])]
    all_to_all x0 -> x1, blocking collectives: none -> 17.5 us  [exchange_z(): lax.all_to_all(field.reshape((4, 2) + shape[1:]), 'z', 0, 0, tiled=True)]
    unnamed x314 -> x343, local copies, waits for them, and re-layouts: 38.2 us -> 55.7 us
  transfers between devices with their start and end apart: 105 -> 121, of which waited for: 38 -> 36; matrix products, arithmetic and copies ran while one was open for 23% -> 17% of each run, Pallas kernels for 23% -> 27%
where the time goes in v4:
time: 999 us; the launch traced here: 987 us
  Pallas kernels  280 us (28%)
  waiting for transfers between devices  221 us (22%)
  starting transfers between devices  205 us (21%)
  local copies, waits for them, and re-layouts  117 us (12%)
  other arithmetic  69 us (7%)
  matrix products  59.9 us (6%)
  blocking collectives  17.5 us (2%)
  between operations  17.1 us (2%)
    ppermute x69, waiting for transfers between devices, swap(): return lax.ppermute(value, axis, [(0, 1), (1, 0)])  103 us
    all_to_all x17, waiting for transfers between devices, exchange(): return lax.all_to_all(field, PLANE, 0, 0, tiled=True)  95.2 us
    all_to_all x17, starting transfers between devices, exchange(): return lax.all_to_all(field, PLANE, 0, 0, tiled=True)  71.7 us
    pallas_call x4, Pallas kernels, attend_back(): pl.pallas_call(kernel, grid=(slots // wide,), in_specs=in_specs, out_spec...  68.2 us
    pallas_call x4, Pallas kernels, attend(): pl.pallas_call(kernel, grid=(steps,), in_specs=[SMEM, ANY], out_specs=[pl...  67.8 us
    unnamed x343, local copies, waits for them, and re-layouts  55.7 us
    pallas_call x4, Pallas kernels, weight_grads(): pl.pallas_call(kernel, in_specs=[SMEM] + [ANY] * inputs, out_specs=[ANY]...  48.8 us
    ppermute x69, starting transfers between devices, swap(): return lax.ppermute(value, axis, [(0, 1), (1, 0)])  47.7 us
  transfers between devices with their start and end apart: 121, of which 36 were waited for; matrix products, arithmetic and copies ran while one was open for 17% of the time, Pallas kernels for 27%

profile of v4, /device:TPU:0, one launch (start us, length us, event | category | flops | bytes accessed | tf_op | source)
XLA Modules:
  0.0 987.1 jit_solution(15616509056894718678)
XLA Ops:
  61.3 10.6 %collective-permute-done.5.rest_2_ = bf16[4,32,1152]{2,1,0:T(8,128)(2,1)S(1)} collective-permute-done((bf16[4,32,1152]{2,1,0:T(8,128)(2,1)S(1)}, bf16[4,32,1152]{2,1,0:T(8,128)(2,1)S(1)}, u32[]{:S(2)}, u32[]{:S(2)}) %collective-permute-start.5) | collective-permute-done | bytes 294944 | tf_op jit(solution)/shard_map/ppermute | solution.py:75
  136.2 25.7 %all-to-all-done.2 = bf16[8,3,256,128]{3,2,1,0:T(8,128)(2,1)S(1)} async-done(((bf16[8,3,256,128]{3,2,1,0:T(8,128)(2,1)}), bf16[8,3,256,128]{3,2,1,0:T(8,128)(2,1)S(1)}, u32[]{:S(2)}, u32[]{:S(2)}) %all-to-all-start.2) | async-done | bytes 1572896 | tf_op jit(solution)/shard_map/all_to_all | solution.py:1144
  180.1 17.0 %attend.4 = (bf16[8,16,16,128]{3,2,1,0:T(8,128)(2,1)S(1)}, f32[8,2048]{1,0:T(8,128)S(1)}) custom-call(s32[1]{0:T(128)} %bitcast.1.len_ref.refs_0_, bf16[8,3,16,16,128]{4,3,2,1,0:T(8,128)(2,1)S(1)} %bitcast.385), custom_call_target="tpu_custom_call" | custom-call | tf_op jit(solution)/shard_map/attend/pallas_call | solution.py:559
  217.6 15.6 %attend.5 = (bf16[8,16,16,128]{3,2,1,0:T(8,128)(2,1)S(1)}, f32[8,2048]{1,0:T(8,128)S(1)}) custom-call(s32[1]{0:T(128)} %bitcast.48.len_ref.refs_0_, bf16[8,3,16,16,128]{4,3,2,1,0:T(8,128)(2,1)S(1)} %bitcast.382), custom_call_target="tpu_custom_call" | custom-call | tf_op jit(solution)/shard_map/attend/pallas_call | solution.py:559
  239.7 11.1 %forward_ffn.4 = (bf16[512,1024]{1,0:T(8,128)(2,1)S(1)}, f32[512,1024]{1,0:T(8,128)}, bf16[512,1024]{1,0:T(8,128)(2,1)S(1)}, bf16[512,2816]{1,0:T(8,128)(2,1)}, ...) custom-call(bf16[8,256,128]{2,1,0:T(8,128)(2,1)S(1)} %all-to-all-done.4.low_ref, ...), custom_call_target="tpu_custom_call" | custom-call | tf_op jit(solution)/shard_map/forward_ffn/pallas_call | solution.py:320
  257.8 10.7 %collective-permute-done.37.rest_6_ = bf16[4,32,2048]{2,1,0:T(8,128)(2,1)} collective-permute-done((bf16[4,32,2048]{2,1,0:T(8,128)(2,1)}, bf16[4,32,2048]{2,1,0:T(8,128)(2,1)}, u32[]{:S(2)}, u32[]{:S(2)}) %collective-permute-start.37) | collective-permute-done | bytes 524320 | tf_op jit(solution)/shard_map/ppermute | solution.py:75
  282.8 10.6 %assemble.7 = bf16[2,2,4,2,32,4224]{5,4,3,2,1,0:T(8,128)(2,1)} custom-call(s32[4]{0:T(128)S(1)} %pad_add_fusion.where_ref, bf16[4,32,2048]{2,1,0:T(8,128)(2,1)} %pad_maximum_fusion.15.rest_0_, bf16[4,32,2048]{2,1,0:T(8,128)(2,1)S(1)} %collective-permute-done.40.rest_1_, bf16[4,32,2048]{2,1,0:T(8,128)(2,1)} %collective-permute-done.34.rest_2_, ...), custom_call_target="tpu_custom_call" | custom-call | tf_op jit(solution)/shard_map/assemble/pallas_call | solution.py:59
  309.0 11.1 %forward_ffn.5 = (bf16[512,1024]{1,0:T(8,128)(2,1)S(1)}, f32[512,1024]{1,0:T(8,128)}, bf16[512,1024]{1,0:T(8,128)(2,1)S(1)}, bf16[512,2816]{1,0:T(8,128)(2,1)}, ...) custom-call(bf16[8,256,128]{2,1,0:T(8,128)(2,1)S(1)} %all-to-all-don, ...), custom_call_target="tpu_custom_call", output_to_operand_aliasing={{0}: (6, {}), {1}: (7, {}), {2}: (8, {}), {3}: (9, {}), {4}... | custom-call | tf_op jit(solution)/shard_map/forward_ffn/pallas_call | solution.py:320
  329.5 10.3 %all-to-all-done.6 = bf16[8,3,256,128]{3,2,1,0:T(8,128)(2,1)S(1)} async-done(((bf16[8,3,256,128]{3,2,1,0:T(8,128)(2,1)}), bf16[8,3,256,128]{3,2,1,0:T(8,128)(2,1)S(1)}, u32[]{:S(2)}, u32[]{:S(2)}) %all-to-all-start.6) | async-done | bytes 1572896 | tf_op jit(solution)/shard_map/all_to_all | solution.py:1144
  344.5 17.7 %attend.6 = (bf16[8,16,16,128]{3,2,1,0:T(8,128)(2,1)}, f32[8,2048]{1,0:T(8,128)S(1)}) custom-call(s32[1]{0:T(128)} %bitcast.1.len_ref.refs_0_, bf16[8,3,16,16,128]{4,3,2,1,0:T(8,128)(2,1)S(1)} %bitcast.380), custom_call_target="tpu_custom_call" | custom-call | tf_op jit(solution)/shard_map/attend/pallas_call | solution.py:559
  380.1 16.3 %collective-permute-start.54 = (bf16[2,2,16,1024]{3,2,1,0:T(8,128)(2,1)S(1)}, bf16[2,2,16,1024]{3,2,1,0:T(8,128)(2,1)S(1)}, u32[]{:S(2)}, u32[]{:S(2)}) collective-permute-start(bf16[2,2,16,1024]{3,2,1,0:T(8,128)(2,1)S(1)} %get-tuple-element.470), channel_id=1, source_target_pairs={{0,24},{1,25},{2,8},{3,9},{4,16},{5,17},{6,0},{7,1},{8,28},{9,29},... | collective-permute-start | bytes 393224 | tf_op jit(solution)/shard_map/ppermute | solution.py:1448
  396.4 17.5 %attend.7 = (bf16[8,16,16,128]{3,2,1,0:T(8,128)(2,1)}, f32[8,2048]{1,0:T(8,128)S(1)}) custom-call(s32[1]{0:T(128)} %bitcast.48.len_ref.refs_0_, bf16[8,3,16,16,128]{4,3,2,1,0:T(8,128)(2,1)} %bitcast.61.piece_ref.refs_1_), custom_call_target="tpu_custom_call" | custom-call | tf_op jit(solution)/shard_map/attend/pallas_call | solution.py:559
  429.2 11.1 %forward_ffn.6 = (bf16[512,1024]{1,0:T(8,128)(2,1)S(1)}, f32[512,1024]{1,0:T(8,128)}, bf16[512,1024]{1,0:T(8,128)(2,1)S(1)}, bf16[512,2816]{1,0:T(8,128)(2,1)}, ...) custom-call(bf16[8,256,128]{2,1,0:T(8,128)(2,1)S(1)} %all-to-all-done.8.low_ref, ...), custom_call_target="tpu_custom_call" | custom-call | tf_op jit(solution)/shard_map/forward_ffn/pallas_call | solution.py:320
  449.6 11.1 %forward_ffn.7 = (bf16[512,1024]{1,0:T(8,128)(2,1)S(1)}, f32[512,1024]{1,0:T(8,128)}, bf16[512,1024]{1,0:T(8,128)(2,1)S(1)}, bf16[512,2816]{1,0:T(8,128)(2,1)}, ...) custom-call(bf16[8,256,128]{2,1,0:T(8,128)(2,1)S(1)} %all-to-all-don, ...), custom_call_target="tpu_custom_call", output_to_operand_aliasing={{0}: (6, {}), {1}: (7, {}), {2}: (8, {}), {3}: (9, {}), {4}... | custom-call | tf_op jit(solution)/shard_map/forward_ffn/pallas_call | solution.py:320
  469.6 8.6 fusion.9
  480.3 17.5 %all_to_all.105 = bf16[4,2,2,16,1024]{4,3,2,1,0:T(8,128)(2,1)S(1)} all-to-all(bf16[4,2,2,16,1024]{4,3,2,1,0:T(8,128)(2,1)S(1)} %bitcast.453), channel_id=1, replica_groups=mesh['y'=2,'c'=2,'z'=4,'x'=2] {'z'}, dimensions={0} | all-to-all | bytes 1048576 | tf_op jit(solution)/shard_map/all_to_all | solution.py:1148
  501.8 15.1 %weight_grads.4 = bf16[4,2,64,8704]{3,2,1,0:T(8,128)(2,1)} custom-call(s32[1]{0:T(128)} %bitcast.core_ref, bf16[512,1024]{1,0:T(8,128)(2,1)S(1)} %get-tuple-element.296.refs_0_, bf16[512,1024]{1,0:T(8,128)(2,1)S(1)} %collective-permute-done.56.refs_1_, bf16[512,2816]{1,0:T(8,128)(2,1)} %copy-done.98, bf16[512,2816]{1,0:T(8,128)(2,1)} %copy-done.101, ...), custom_call_target="tpu_custom_call" | custom-call | tf_op jit(solution)/shard_map/weight_grads/pallas_call | solution.py:461
  548.2 8.3 all-to-all-done.12
  557.9 18.4 %attend_back.4 = (bf16[8,3,16,16,128]{4,3,2,1,0:T(8,128)(2,1)}, f32[2048,128]{1,0:T(8,128)S(1)}) custom-call(s32[1]{0:T(128)} %bitcast.1.len_ref.refs_0_, bf16[8,3,16,16,128]{4,3,2,1,0:T(8,128)(2,1)} %bitcast.381, bf16[8,16,16,128]{3,2,1,0:T(8,128)(2,1)} %get-tuple-element.262.refs_2_, bf16[8,16,16,128]{3,2,1,0:T(8,128)(2,1)S(1)} %get-tuple-element.468.refs_3_, ...), custom_call_target="tpu_custom_call" | custom-call | tf_op jit(solution)/shard_map/attend_back/pallas_call | solution.py:731
  581.8 15.8 %attend_back.5 = (bf16[8,3,16,16,128]{4,3,2,1,0:T(8,128)(2,1)}, f32[2048,128]{1,0:T(8,128)S(1)}) custom-call(s32[1]{0:T(128)} %bitcast.48.len_ref.refs_0_, bf16[8,3,16,16,128]{4,3,2,1,0:T(8,128)(2,1)} %bitcast.61.piece_ref.refs_1_, bf16[8,16,16,128]{3,2,1,0:T(8,128)(2,1)} %get-tuple-element.269.refs_2_, ...), custom_call_target="tpu_custom_call" | custom-call | tf_op jit(solution)/shard_map/attend_back/pallas_call | solution.py:731
  610.6 16.6 %all-to-all-done.14 = bf16[8,3,256,128]{3,2,1,0:T(8,128)(2,1)} async-done(((bf16[8,3,256,128]{3,2,1,0:T(8,128)(2,1)}), bf16[8,3,256,128]{3,2,1,0:T(8,128)(2,1)}, u32[]{:S(2)}, u32[]{:S(2)}) %all-to-all-start.14) | async-done | bytes 1572896 | tf_op jit(solution)/shard_map/all_to_all | solution.py:1144
  645.4 8.9 weight_grads.5
  656.1 8.5 fusion.17
  677.4 15.8 %weight_grads.6 = bf16[4,2,64,8704]{3,2,1,0:T(8,128)(2,1)} custom-call(s32[1]{0:T(128)} %bitcast.core_ref, bf16[512,1024]{1,0:T(8,128)(2,1)S(1)} %copy-done.22, bf16[512,1024]{1,0:T(8,128)(2,1)} %collective-permute-done.65.refs_1_, bf16[512,2816]{1,0:T(8,128)(2,1)} %get-tuple-element.335.refs_2_, bf16[512,2816]{1,0:T(8,128)(2,1)} %collective-permute-done.66.refs_3_, ...), custom_call_target="tpu_custom_call" | custom-call | tf_op jit(solution)/shard_map/weight_grads/pallas_call | solution.py:461
  693.3 8.1 fusion.22
  717.2 14.8 %all-to-all-done.16 = bf16[8,512,128]{2,1,0:T(8,128)(2,1)S(1)} async-done(((bf16[8,512,128]{2,1,0:T(8,128)(2,1)}), bf16[8,512,128]{2,1,0:T(8,128)(2,1)S(1)}, u32[]{:S(2)}, u32[]{:S(2)}) %all-to-all-start.16) | async-done | bytes 1048608 | tf_op jit(solution)/shard_map/all_to_all | solution.py:1144
  740.2 18.4 %attend_back.6 = bf16[8,3,16,16,128]{4,3,2,1,0:T(8,128)(2,1)} custom-call(s32[1]{0:T(128)} %bitcast.1.len_ref.refs_0_, bf16[8,3,16,16,128]{4,3,2,1,0:T(8,128)(2,1)} %bitcast.384, bf16[8,16,16,128]{3,2,1,0:T(8,128)(2,1)S(1)} %copy-done.24, bf16[8,16,16,128]{3,2,1,0:T(8,128)(2,1)S(1)} %get-tuple-element.466.refs_3_, f32[8,2048]{1,0:T(8,128)S(1)} %get-tuple-element.347.refs_4_, ...), custom_call_target="tpu_custom_call" | custom-call | tf_op jit(solution)/shard_map/attend_back/pallas_call | solution.py:731
  767.1 15.6 %attend_back.7 = bf16[8,3,16,16,128]{4,3,2,1,0:T(8,128)(2,1)} custom-call(s32[1]{0:T(128)} %bitcast.48.len_ref.refs_0_, bf16[8,3,16,16,128]{4,3,2,1,0:T(8,128)(2,1)} %bitcast.383, bf16[8,16,16,128]{3,2,1,0:T(8,128)(2,1)S(1)} %copy-done.26, bf16[8,16,16,128]{3,2,1,0:T(8,128)(2,1)S(1)} %get-tuple-element.356.refs_3_, ...), custom_call_target="tpu_custom_call" | custom-call | tf_op jit(solution)/shard_map/attend_back/pallas_call | solution.py:731
  798.4 19.6 %collective-permute-done.72 = bf16[32,4352]{1,0:T(8,128)(2,1)S(1)} collective-permute-done((bf16[32,4352]{1,0:T(8,128)(2,1)S(1)}, bf16[32,4352]{1,0:T(8,128)(2,1)S(1)}, u32[]{:S(2)}, u32[]{:S(2)}) %collective-permute-start.72) | collective-permute-done | bytes 278560 | tf_op jit(solution)/shard_map/ppermute | solution.py:75
  839.7 8.9 weight_grads.7
  854.8 21.0 %collective-permute-done.78 = bf16[4,2,32,2048]{3,2,1,0:T(8,128)(2,1)S(1)} collective-permute-done((bf16[4,2,32,2048]{3,2,1,0:T(8,128)(2,1)S(1)}, bf16[4,2,32,2048]{3,2,1,0:T(8,128)(2,1)S(1)}, u32[]{:S(2)}, u32[]{:S(2)}) %collective-permute-start.78) | collective-permute-done | bytes 1048608 | tf_op jit(solution)/shard_map/ppermute | solution.py:75
  930.5 13.2 %collective-permute-done.88 = bf16[32,2048]{1,0:T(8,128)(2,1)S(1)} collective-permute-done((bf16[32,2048]{1,0:T(8,128)(2,1)}, bf16[32,2048]{1,0:T(8,128)(2,1)S(1)}, u32[]{:S(2)}, u32[]{:S(2)}) %collective-permute-start.88) | collective-permute-done | bytes 131104 | tf_op jit(solution)/shard_map/ppermute | solution.py:79
  (756 shorter events, 520.4 us)
Async XLA Ops:
  7.2 190.6 %all-gather.3.cloned.1.call-start = ((), (), s32[]{:S(2)}) async-start(), calls=%async_computation.24 | async-start | bytes 20545536 | tf_op jit(solution)/shard_map/all_gather | solution.py:1165
  44.6 70.2 %all-to-all-start.1 = ((bf16[4,2,2,2,16,1024]{5,4,3,1,2,0:T(8,128)(2,1)}), bf16[4,2,2,2,16,1024]{5,4,3,1,2,0:T(8,128)(2,1)}, u32[]{:S(2)}, u32[]{:S(2)}) async-start(bf16[4,2,2,2,16,1024]{5,4,3,1,2,0:T(8,128)(2,1)} %copy.141), calls=%async_computation.1 | async-start | bytes 2097152 | tf_op jit(solution)/shard_map/all_to_all | solution.py:1148
  124.5 37.3 %all-to-all-start.2 = ((bf16[8,3,256,128]{3,2,1,0:T(8,128)(2,1)}), bf16[8,3,256,128]{3,2,1,0:T(8,128)(2,1)S(1)}, u32[]{:S(2)}, u32[]{:S(2)}) async-start(bf16[8,3,256,128]{3,2,1,0:T(8,128)(2,1)} %copy-done.14), calls=%async_computation.2 | async-start | bytes 3145728 | tf_op jit(solution)/shard_map/all_to_all | solution.py:1144
  163.0 41.6 %all-to-all-start.3 = ((bf16[8,3,256,128]{3,2,1,0:T(8,128)(2,1)}), bf16[8,3,256,128]{3,2,1,0:T(8,128)(2,1)S(1)}, u32[]{:S(2)}, u32[]{:S(2)}) async-start(bf16[8,3,256,128]{3,2,1,0:T(8,128)(2,1)} %copy-done.13), calls=%async_computation.3 | async-start | bytes 3145728 | tf_op jit(solution)/shard_map/all_to_all | solution.py:1144
  166.6 255.4 %all-gather.5.cloned.1.call-start = ((), (), s32[]{:S(2)}) async-start(), calls=%async_computation.25 | async-start | bytes 18382848 | tf_op jit(solution)/shard_map/all_gather | solution.py:1165
  168.7 35.9 %collective-permute-start.31 = (bf16[32,4224]{1,0:T(8,128)(2,1)S(1)}, bf16[32,4224]{1,0:T(8,128)(2,1)}, u32[]{:S(2)}, u32[]{:S(2)}) collective-permute-start(bf16[32,4224]{1,0:T(8,128)(2,1)S(1)} %fusion.77), channel_id=1, source_target_pairs={{0,2},{2,0},{4,6},{6,4},{1,3},{3,1},{5,7},{7,5},{8,10},{10,8},{12,... | collective-permute-start | bytes 811016 | tf_op jit(solution)/shard_map/ppermute | solution.py:79
  175.1 29.5 %collective-permute-start.32 = (bf16[32,4224]{1,0:T(8,128)(2,1)S(1)}, bf16[32,4224]{1,0:T(8,128)(2,1)}, u32[]{:S(2)}, u32[]{:S(2)}) collective-permute-start(bf16[32,4224]{1,0:T(8,128)(2,1)S(1)} %fusion.77), channel_id=1, source_target_pairs={{0,4},{2,6},{4,0},{6,2},{1,5},{3,7},{5,1},{7,3},{8,12},{10,14},{12... | collective-permute-start | bytes 811016 | tf_op jit(solution)/shard_map/ppermute | solution.py:79
  178.7 25.9 %collective-permute-start.33 = (bf16[32,4224]{1,0:T(8,128)(2,1)S(1)}, bf16[32,4224]{1,0:T(8,128)(2,1)}, u32[]{:S(2)}, u32[]{:S(2)}) collective-permute-start(bf16[32,4224]{1,0:T(8,128)(2,1)S(1)} %fusion.77), channel_id=1, source_target_pairs={{0,6},{2,4},{4,2},{6,0},{1,7},{3,5},{5,3},{7,1},{8,14},{10,12},{12... | collective-permute-start | bytes 811016 | tf_op jit(solution)/shard_map/ppermute | solution.py:79
  207.0 27.0 %collective-permute-start.35 = (bf16[4,32,2176]{2,1,0:T(8,128)(2,1)}, bf16[4,32,2176]{2,1,0:T(8,128)(2,1)}, u32[]{:S(2)}, u32[]{:S(2)}) collective-permute-start(bf16[4,32,2176]{2,1,0:T(8,128)(2,1)} %pad_maximum_fusion.12.rest_8_), channel_id=1, source_target_pairs={{0,16},{16,0},{1,17},{17,1},{2,18},{18,2},{3,19},{19,3},{4,20},{20... | collective-permute-start | bytes 1671176 | tf_op jit(solution)/shard_map/ppermute | solution.py:75
  215.6 42.1 %collective-permute-start.38 = (bf16[4,32,2176]{2,1,0:T(8,128)(2,1)}, bf16[4,32,2176]{2,1,0:T(8,128)(2,1)}, u32[]{:S(2)}, u32[]{:S(2)}) collective-permute-start(bf16[4,32,2176]{2,1,0:T(8,128)(2,1)} %pad_maximum_fusion.12.rest_8_), channel_id=1, source_target_pairs={{0,1},{1,0},{2,3},{3,2},{4,5},{5,4},{6,7},{7,6},{8,9},{9,8},{10,11... | collective-permute-start | bytes 1671176 | tf_op jit(solution)/shard_map/ppermute | solution.py:75
  234.0 39.8 %collective-permute-start.39 = (bf16[4,32,2176]{2,1,0:T(8,128)(2,1)}, bf16[4,32,2176]{2,1,0:T(8,128)(2,1)}, u32[]{:S(2)}, u32[]{:S(2)}) collective-permute-start(bf16[4,32,2176]{2,1,0:T(8,128)(2,1)} %collective-permute-done.35.rest_10_), channel_id=1, source_target_pairs={{0,1},{1,0},{2,3},{3,2},{4,5},{5,4},{6,7},{7,6},{8,9},{9,8},{10,11... | collective-permute-start | bytes 1671176 | tf_op jit(solution)/shard_map/ppermute | solution.py:75
  237.5 31.0 %collective-permute-start.37 = (bf16[4,32,2048]{2,1,0:T(8,128)(2,1)}, bf16[4,32,2048]{2,1,0:T(8,128)(2,1)}, u32[]{:S(2)}, u32[]{:S(2)}) collective-permute-start(bf16[4,32,2048]{2,1,0:T(8,128)(2,1)} %collective-permute-done.34.rest_2_), channel_id=1, source_target_pairs={{0,16},{16,0},{1,17},{17,1},{2,18},{18,2},{3,19},{19,3},{4,20},{20... | collective-permute-start | bytes 1572872 | tf_op jit(solution)/shard_map/ppermute | solution.py:75
  302.5 37.3 %all-to-all-start.6 = ((bf16[8,3,256,128]{3,2,1,0:T(8,128)(2,1)}), bf16[8,3,256,128]{3,2,1,0:T(8,128)(2,1)S(1)}, u32[]{:S(2)}, u32[]{:S(2)}) async-start(bf16[8,3,256,128]{3,2,1,0:T(8,128)(2,1)} %copy-done.27), calls=%async_computation.6 | async-start | bytes 3145728 | tf_op jit(solution)/shard_map/all_to_all | solution.py:1144
  339.8 25.2 %all-to-all-start.7 = ((bf16[8,3,256,128]{3,2,1,0:T(8,128)(2,1)}), bf16[8,3,256,128]{3,2,1,0:T(8,128)(2,1)}, u32[]{:S(2)}, u32[]{:S(2)}) async-start(bf16[8,3,256,128]{3,2,1,0:T(8,128)(2,1)} %copy-done.28), calls=%async_computation.7 | async-start | bytes 3145728 | tf_op jit(solution)/shard_map/all_to_all | solution.py:1144
  365.0 49.0 %all-to-all-start.8 = ((bf16[8,256,128]{2,1,0:T(8,128)(2,1)}), bf16[8,256,128]{2,1,0:T(8,128)(2,1)S(1)}, u32[]{:S(2)}, u32[]{:S(2)}) async-start(bf16[8,256,128]{2,1,0:T(8,128)(2,1)} %bitcast.60), calls=%async_computation.8 | async-start | bytes 1048576 | tf_op jit(solution)/shard_map/all_to_all | solution.py:1144
  371.2 25.1 %collective-permute-start.50 = (bf16[2,2,16,1024]{3,2,1,0:T(8,128)(2,1)S(1)}, bf16[2,2,16,1024]{3,2,1,0:T(8,128)(2,1)S(1)}, u32[]{:S(2)}, u32[]{:S(2)}) collective-permute-start(bf16[2,2,16,1024]{3,2,1,0:T(8,128)(2,1)S(1)} %get-tuple-element.474), channel_id=1, source_target_pairs={{0,16},{1,17},{2,0},{3,1},{4,24},{5,25},{6,8},{7,9},{8,20},{9,21},... | collective-permute-start | bytes 393224 | tf_op jit(solution)/shard_map/ppermute | solution.py:1448
  376.3 37.6 %collective-permute-start.51 = (bf16[2,2,16,1024]{3,2,1,0:T(8,128)(2,1)S(1)}, bf16[2,2,16,1024]{3,2,1,0:T(8,128)(2,1)S(1)}, u32[]{:S(2)}, u32[]{:S(2)}) collective-permute-start(bf16[2,2,16,1024]{3,2,1,0:T(8,128)(2,1)S(1)} %get-tuple-element.473), channel_id=1, source_target_pairs={{0,17},{1,16},{2,1},{3,0},{4,25},{5,24},{6,9},{7,8},{8,21},{9,20},... | collective-permute-start | bytes 393224 | tf_op jit(solution)/shard_map/ppermute | solution.py:1448
  376.3 37.6 %collective-permute-start.52 = (bf16[2,2,16,1024]{3,2,1,0:T(8,128)(2,1)S(1)}, bf16[2,2,16,1024]{3,2,1,0:T(8,128)(2,1)S(1)}, u32[]{:S(2)}, u32[]{:S(2)}) collective-permute-start(bf16[2,2,16,1024]{3,2,1,0:T(8,128)(2,1)S(1)} %get-tuple-element.472), channel_id=1, source_target_pairs={{0,8},{1,9},{2,24},{3,25},{4,0},{5,1},{6,16},{7,17},{8,12},{9,13},... | collective-permute-start | bytes 393224 | tf_op jit(solution)/shard_map/ppermute | solution.py:1448
  377.3 36.6 %collective-permute-start.53 = (bf16[2,2,16,1024]{3,2,1,0:T(8,128)(2,1)S(1)}, bf16[2,2,16,1024]{3,2,1,0:T(8,128)(2,1)S(1)}, u32[]{:S(2)}, u32[]{:S(2)}) collective-permute-start(bf16[2,2,16,1024]{3,2,1,0:T(8,128)(2,1)S(1)} %get-tuple-element.471), channel_id=1, source_target_pairs={{0,9},{1,8},{2,25},{3,24},{4,1},{5,0},{6,17},{7,16},{8,13},{9,12},... | collective-permute-start | bytes 393224 | tf_op jit(solution)/shard_map/ppermute | solution.py:1448
  380.1 33.9 %collective-permute-start.54 = (bf16[2,2,16,1024]{3,2,1,0:T(8,128)(2,1)S(1)}, bf16[2,2,16,1024]{3,2,1,0:T(8,128)(2,1)S(1)}, u32[]{:S(2)}, u32[]{:S(2)}) collective-permute-start(bf16[2,2,16,1024]{3,2,1,0:T(8,128)(2,1)S(1)} %get-tuple-element.470), channel_id=1, source_target_pairs={{0,24},{1,25},{2,8},{3,9},{4,16},{5,17},{6,0},{7,1},{8,28},{9,29},... | collective-permute-start | bytes 393224 | tf_op jit(solution)/shard_map/ppermute | solution.py:1448
  414.0 27.2 %all-to-all-start.9 = ((bf16[8,256,128]{2,1,0:T(8,128)(2,1)}), bf16[8,256,128]{2,1,0:T(8,128)(2,1)S(1)}, u32[]{:S(2)}, u32[]{:S(2)}) async-start(bf16[8,256,128]{2,1,0:T(8,128)(2,1)} %bitcast.77), calls=%async_computation.9 | async-start | bytes 1048576 | tf_op jit(solution)/shard_map/all_to_all | solution.py:1144
  449.3 282.7 %reduce-scatter.6.cloned.1.call-start = ((), (), s32[]{:S(2)}) async-start(), calls=%async_computation.27 | async-start | bytes 11141120 | tf_op jit(solution)/shard_map/reduce_scatter | solution.py:1274
  606.6 215.3 %reduce-scatter.8.cloned.1.call-start = ((), (), s32[]{:S(2)}) async-start(), calls=%async_computation.28 | async-start | bytes 5242880 | tf_op jit(solution)/shard_map/reduce_scatter | solution.py:1274
  632.5 41.1 %collective-permute-start.68 = (bf16[512,2816]{1,0:T(8,128)(2,1)}, bf16[512,2816]{1,0:T(8,128)(2,1)}, u32[]{:S(2)}, u32[]{:S(2)}) collective-permute-start(bf16[512,2816]{1,0:T(8,128)(2,1)} %get-tuple-element.334.refs_6_), channel_id=1, source_target_pairs={{0,8},{8,0},{1,9},{9,1},{2,10},{10,2},{3,11},{11,3},{4,12},{12,4},... | collective-permute-start | bytes 8650760 | tf_op jit(solution)/shard_map/ppermute | solution.py:75
  669.3 44.3 %all-to-all-start.15 = ((bf16[8,2,2,16,1024]{4,3,2,1,0:T(8,128)(2,1)}), bf16[8,2,2,16,1024]{4,3,2,1,0:T(8,128)(2,1)}, u32[]{:S(2)}, u32[]{:S(2)}) async-start(bf16[8,2,2,16,1024]{4,3,2,1,0:T(8,128)(2,1)} %pad_maximum_fusion.4), calls=%async_computation.15 | async-start | bytes 2097152 | tf_op jit(solution)/shard_map/all_to_all | solution.py:1144
  717.2 191.9 %reduce-scatter.4.cloned.1.call-start = ((), (), s32[]{:S(2)}) async-start(), calls=%async_computation.26 | async-start | bytes 11141120 | tf_op jit(solution)/shard_map/reduce_scatter | solution.py:1274
  787.6 30.6 %all-to-all-start.18 = ((bf16[8,3,256,128]{3,2,1,0:T(8,128)(2,1)}), bf16[8,3,256,128]{3,2,1,0:T(8,128)(2,1)}, u32[]{:S(2)}, u32[]{:S(2)}) async-start(bf16[8,3,256,128]{3,2,1,0:T(8,128)(2,1)} %bitcast.436), calls=%async_computation.21 | async-start | bytes 3145728 | tf_op jit(solution)/shard_map/all_to_all | solution.py:1144
  792.1 25.9 %collective-permute-start.72 = (bf16[32,4352]{1,0:T(8,128)(2,1)S(1)}, bf16[32,4352]{1,0:T(8,128)(2,1)S(1)}, u32[]{:S(2)}, u32[]{:S(2)}) collective-permute-start(bf16[32,4352]{1,0:T(8,128)(2,1)S(1)} %dynamic-slice_bitcast_fusion.15), channel_id=1, source_target_pairs={{0,16},{16,0},{1,17},{17,1},{2,18},{18,2},{3,19},{19,3},{4,20},{20... | collective-permute-start | bytes 835592 | tf_op jit(solution)/shard_map/ppermute | solution.py:75
  902.2 25.1 %collective-permute-start.91 = (bf16[32,2048]{1,0:T(8,128)(2,1)}, bf16[32,2048]{1,0:T(8,128)(2,1)}, u32[]{:S(2)}, u32[]{:S(2)}) collective-permute-start(bf16[32,2048]{1,0:T(8,128)(2,1)} %get-tuple-element.489), channel_id=1, source_target_pairs={{0,6},{2,4},{4,2},{6,0},{1,7},{3,5},{5,3},{7,1},{8,14},{10,12},{12... | collective-permute-start | bytes 393224 | tf_op jit(solution)/shard_map/ppermute | solution.py:79
  912.6 36.8 %all-to-all-start.19 = ((bf16[4,2,2,2,16,1024]{5,4,3,1,2,0:T(8,128)(2,1)}), bf16[4,2,2,2,16,1024]{5,4,3,1,2,0:T(8,128)(2,1)S(1)}, u32[]{:S(2)}, u32[]{:S(2)}) async-start(bf16[4,2,2,2,16,1024]{5,4,3,1,2,0:T(8,128)(2,1)} %copy.164), calls=%async_computation.22 | async-start | bytes 2097152 | tf_op jit(solution)/shard_map/all_to_all | solution.py:1148
  930.4 33.4 %collective-permute-start.93 = (bf16[32,2048]{1,0:T(8,128)(2,1)}, bf16[32,2048]{1,0:T(8,128)(2,1)}, u32[]{:S(2)}, u32[]{:S(2)}) collective-permute-start(bf16[32,2048]{1,0:T(8,128)(2,1)} %get-tuple-element.507), channel_id=1, source_target_pairs={{0,1},{1,0},{2,3},{3,2},{4,5},{5,4},{6,7},{7,6},{8,9},{9,8},{10,11... | collective-permute-start | bytes 393224 | tf_op jit(solution)/shard_map/ppermute | solution.py:75
  930.4 33.4 %collective-permute-start.92 = (bf16[32,2048]{1,0:T(8,128)(2,1)}, bf16[32,2048]{1,0:T(8,128)(2,1)}, u32[]{:S(2)}, u32[]{:S(2)}) collective-permute-start(bf16[32,2048]{1,0:T(8,128)(2,1)} %get-tuple-element.509), channel_id=1, source_target_pairs={{0,16},{16,0},{1,17},{17,1},{2,18},{18,2},{3,19},{19,3},{4,20},{20... | collective-permute-start | bytes 393224 | tf_op jit(solution)/shard_map/ppermute | solution.py:75
  (256 other events, 2675.6 us)
Sparse Core Ops, SparseCore 0:
  13.1 167.4 all-gather.2
  204.7 150.5 all-gather.4
  517.0 151.9 reduce-scatter.5
  671.2 77.6 reduce-scatter.7
  751.2 157.8 reduce-scatter.3

commit v5 on v4

--- a/solution.py
+++ b/solution.py
@@ -1502,13 +1502,13 @@
     mark = [r.partial for r in attn_pair_one]
     ffn_one_sum, input_grad, *mark = fence(ffn_one_sum, input_grad, *mark)
     ffn_pair_one = pair_sums(ffn_one_sum)
-    (input_grad,) = send_all(ffn_pair_one, input_grad)
     input_grad = exchange_z(input_grad)
+    send_all(ffn_pair_one)
     add_all(attn_pair_one)
     send_all(attn_pair_one)
-    (input_grad,) = add_all(ffn_pair_one, input_grad)
-    (input_grad,) = send_all(ffn_pair_one, input_grad)
     input_grad = exchange(input_grad)
+    add_all(ffn_pair_one)
+    send_all(ffn_pair_one)
     add_all(attn_pair_two + ffn_pair_one)
     add_all(attn_pair_one)
     input_grad = join_blocks(input_grad).astype(F32)

time: 999 us -> 1010 us (1.011)
    ppermute x18, starting transfers between devices: 40.5 us -> 52 us  [hop(): return lax.ppermute(value, 'z', [(i, i ^ offset) for i in range(4)])]
    unnamed x343 -> x341, local copies, waits for them, and re-layouts: 55.7 us -> 55.3 us
  transfers between devices with their start and end apart: 121 -> 121, of which waited for: 36 -> 37; matrix products, arithmetic and copies ran while one was open for 17% -> 16% of each run, Pallas kernels for 27% -> 27%
where the time goes in v5:
time: 1010 us; the launch traced here: 996 us
  Pallas kernels  280 us (28%)
  waiting for transfers between devices  226 us (22%)
  starting transfers between devices  213 us (21%)
  local copies, waits for them, and re-layouts  114 us (11%)
  other arithmetic  67.7 us (7%)
  matrix products  59.9 us (6%)
  blocking collectives  17.5 us (2%)
  between operations  17.1 us (2%)
    ppermute x69, waiting for transfers between devices, swap(): return lax.ppermute(value, axis, [(0, 1), (1, 0)])  106 us
    all_to_all x17, waiting for transfers between devices, exchange(): return lax.all_to_all(field, PLANE, 0, 0, tiled=True)  96.6 us
    all_to_all x17, starting transfers between devices, exchange(): return lax.all_to_all(field, PLANE, 0, 0, tiled=True)  69.1 us
    pallas_call x4, Pallas kernels, attend_back(): pl.pallas_call(kernel, grid=(slots // wide,), in_specs=in_specs, out_spec...  68.2 us
    pallas_call x4, Pallas kernels, attend(): pl.pallas_call(kernel, grid=(steps,), in_specs=[SMEM, ANY], out_specs=[pl...  67.9 us
    unnamed x341, local copies, waits for them, and re-layouts  55.3 us
    ppermute x18, starting transfers between devices, hop(): return lax.ppermute(value, 'z', [(i, i ^ offset) for i in range(4)])  52 us
    pallas_call x4, Pallas kernels, weight_grads(): pl.pallas_call(kernel, in_specs=[SMEM] + [ANY] * inputs, out_specs=[ANY]...  48.3 us
  transfers between devices with their start and end apart: 121, of which 37 were waited for; matrix products, arithmetic and copies ran while one was open for 16% of the time, Pallas kernels for 27%

profile of v5, /device:TPU:0, one launch (start us, length us, event | category | flops | bytes accessed | tf_op | source)
XLA Modules:
  0.0 996.1 jit_solution(14585229241558923868)
XLA Ops:
  61.3 10.6 %collective-permute-done.5.rest_2_ = bf16[4,32,1152]{2,1,0:T(8,128)(2,1)S(1)} collective-permute-done((bf16[4,32,1152]{2,1,0:T(8,128)(2,1)S(1)}, bf16[4,32,1152]{2,1,0:T(8,128)(2,1)S(1)}, u32[]{:S(2)}, u32[]{:S(2)}) %collective-permute-start.5) | collective-permute-done | bytes 294944 | tf_op jit(solution)/shard_map/ppermute | solution.py:75
  136.2 25.6 %all-to-all-done.2 = bf16[8,3,256,128]{3,2,1,0:T(8,128)(2,1)S(1)} async-done(((bf16[8,3,256,128]{3,2,1,0:T(8,128)(2,1)}), bf16[8,3,256,128]{3,2,1,0:T(8,128)(2,1)S(1)}, u32[]{:S(2)}, u32[]{:S(2)}) %all-to-all-start.2) | async-done | bytes 1572896 | tf_op jit(solution)/shard_map/all_to_all | solution.py:1144
  180.0 15.6 %attend.4 = (bf16[8,16,16,128]{3,2,1,0:T(8,128)(2,1)S(1)}, f32[8,2048]{1,0:T(8,128)S(1)}) custom-call(s32[1]{0:T(128)} %bitcast.1.len_ref.refs_0_, bf16[8,3,16,16,128]{4,3,2,1,0:T(8,128)(2,1)S(1)} %bitcast.385), custom_call_target="tpu_custom_call" | custom-call | tf_op jit(solution)/shard_map/attend/pallas_call | solution.py:559
  216.3 17.0 %attend.5 = (bf16[8,16,16,128]{3,2,1,0:T(8,128)(2,1)S(1)}, f32[8,2048]{1,0:T(8,128)S(1)}) custom-call(s32[1]{0:T(128)} %bitcast.48.len_ref.refs_0_, bf16[8,3,16,16,128]{4,3,2,1,0:T(8,128)(2,1)S(1)} %bitcast.382), custom_call_target="tpu_custom_call" | custom-call | tf_op jit(solution)/shard_map/attend/pallas_call | solution.py:559
  239.2 11.1 %forward_ffn.4 = (bf16[512,1024]{1,0:T(8,128)(2,1)S(1)}, f32[512,1024]{1,0:T(8,128)}, bf16[512,1024]{1,0:T(8,128)(2,1)S(1)}, bf16[512,2816]{1,0:T(8,128)(2,1)}, ...) custom-call(bf16[8,256,128]{2,1,0:T(8,128)(2,1)S(1)} %all-to-all-done.4.low_ref, ...), custom_call_target="tpu_custom_call" | custom-call | tf_op jit(solution)/shard_map/forward_ffn/pallas_call | solution.py:320
  258.6 8.9 collective-permute-done.37.rest_6_
  281.4 11.1 %assemble.7 = bf16[2,2,4,2,32,4224]{5,4,3,2,1,0:T(8,128)(2,1)} custom-call(s32[4]{0:T(128)S(1)} %pad_add_fusion.where_ref, bf16[4,32,2048]{2,1,0:T(8,128)(2,1)} %pad_maximum_fusion.15.rest_0_, bf16[4,32,2048]{2,1,0:T(8,128)(2,1)S(1)} %collective-permute-done.40.rest_1_, bf16[4,32,2048]{2,1,0:T(8,128)(2,1)} %collective-permute-done.34.rest_2_, ...), custom_call_target="tpu_custom_call" | custom-call | tf_op jit(solution)/shard_map/assemble/pallas_call | solution.py:59
  308.2 11.1 %forward_ffn.5 = (bf16[512,1024]{1,0:T(8,128)(2,1)S(1)}, f32[512,1024]{1,0:T(8,128)}, bf16[512,1024]{1,0:T(8,128)(2,1)S(1)}, bf16[512,2816]{1,0:T(8,128)(2,1)}, ...) custom-call(bf16[8,256,128]{2,1,0:T(8,128)(2,1)S(1)} %all-to-all-don, ...), custom_call_target="tpu_custom_call", output_to_operand_aliasing={{0}: (6, {}), {1}: (7, {}), {2}: (8, {}), {3}: (9, {}), {4}... | custom-call | tf_op jit(solution)/shard_map/forward_ffn/pallas_call | solution.py:320
  328.8 9.6 all-to-all-done.6
  343.1 16.4 %attend.6 = (bf16[8,16,16,128]{3,2,1,0:T(8,128)(2,1)}, f32[8,2048]{1,0:T(8,128)S(1)}) custom-call(s32[1]{0:T(128)} %bitcast.1.len_ref.refs_0_, bf16[8,3,16,16,128]{4,3,2,1,0:T(8,128)(2,1)S(1)} %bitcast.380), custom_call_target="tpu_custom_call" | custom-call | tf_op jit(solution)/shard_map/attend/pallas_call | solution.py:559
  378.7 18.9 %collective-permute-start.54 = (bf16[2,2,16,1024]{3,2,1,0:T(8,128)(2,1)S(1)}, bf16[2,2,16,1024]{3,2,1,0:T(8,128)(2,1)S(1)}, u32[]{:S(2)}, u32[]{:S(2)}) collective-permute-start(bf16[2,2,16,1024]{3,2,1,0:T(8,128)(2,1)S(1)} %get-tuple-element.464), channel_id=1, source_target_pairs={{0,24},{1,25},{2,8},{3,9},{4,16},{5,17},{6,0},{7,1},{8,28},{9,29},... | collective-permute-start | bytes 393224 | tf_op jit(solution)/shard_map/ppermute | solution.py:1448
  397.6 18.9 %attend.7 = (bf16[8,16,16,128]{3,2,1,0:T(8,128)(2,1)}, f32[8,2048]{1,0:T(8,128)S(1)}) custom-call(s32[1]{0:T(128)} %bitcast.48.len_ref.refs_0_, bf16[8,3,16,16,128]{4,3,2,1,0:T(8,128)(2,1)} %bitcast.61.piece_ref.refs_1_), custom_call_target="tpu_custom_call" | custom-call | tf_op jit(solution)/shard_map/attend/pallas_call | solution.py:559
  429.0 11.1 %forward_ffn.6 = (bf16[512,1024]{1,0:T(8,128)(2,1)S(1)}, f32[512,1024]{1,0:T(8,128)}, bf16[512,1024]{1,0:T(8,128)(2,1)S(1)}, bf16[512,2816]{1,0:T(8,128)(2,1)}, ...) custom-call(bf16[8,256,128]{2,1,0:T(8,128)(2,1)S(1)} %all-to-all-done.8.low_ref, ...), custom_call_target="tpu_custom_call" | custom-call | tf_op jit(solution)/shard_map/forward_ffn/pallas_call | solution.py:320
  447.0 11.1 %forward_ffn.7 = (bf16[512,1024]{1,0:T(8,128)(2,1)S(1)}, f32[512,1024]{1,0:T(8,128)}, bf16[512,1024]{1,0:T(8,128)(2,1)S(1)}, bf16[512,2816]{1,0:T(8,128)(2,1)}, ...) custom-call(bf16[8,256,128]{2,1,0:T(8,128)(2,1)S(1)} %all-to-all-don, ...), custom_call_target="tpu_custom_call", output_to_operand_aliasing={{0}: (6, {}), {1}: (7, {}), {2}: (8, {}), {3}: (9, {}), {4}... | custom-call | tf_op jit(solution)/shard_map/forward_ffn/pallas_call | solution.py:320
  467.2 8.6 fusion.9
  478.0 17.5 %all_to_all.105 = bf16[4,2,2,16,1024]{4,3,2,1,0:T(8,128)(2,1)S(1)} all-to-all(bf16[4,2,2,16,1024]{4,3,2,1,0:T(8,128)(2,1)S(1)} %bitcast.453), channel_id=1, replica_groups=mesh['y'=2,'c'=2,'z'=4,'x'=2] {'z'}, dimensions={0} | all-to-all | bytes 1048576 | tf_op jit(solution)/shard_map/all_to_all | solution.py:1148
  499.4 15.1 %weight_grads.4 = bf16[4,2,64,8704]{3,2,1,0:T(8,128)(2,1)} custom-call(s32[1]{0:T(128)} %bitcast.core_ref, bf16[512,1024]{1,0:T(8,128)(2,1)S(1)} %get-tuple-element.293.refs_0_, bf16[512,1024]{1,0:T(8,128)(2,1)S(1)} %collective-permute-done.56.refs_1_, bf16[512,2816]{1,0:T(8,128)(2,1)} %copy-done.98, bf16[512,2816]{1,0:T(8,128)(2,1)} %copy-done.101, ...), custom_call_target="tpu_custom_call" | custom-call | tf_op jit(solution)/shard_map/weight_grads/pallas_call | solution.py:461
  555.6 15.7 %attend_back.4 = (bf16[8,3,16,16,128]{4,3,2,1,0:T(8,128)(2,1)}, f32[2048,128]{1,0:T(8,128)S(1)}) custom-call(s32[1]{0:T(128)} %bitcast.1.len_ref.refs_0_, bf16[8,3,16,16,128]{4,3,2,1,0:T(8,128)(2,1)} %bitcast.381, bf16[8,16,16,128]{3,2,1,0:T(8,128)(2,1)} %get-tuple-element.259.refs_2_, bf16[8,16,16,128]{3,2,1,0:T(8,128)(2,1)S(1)} %get-tuple-element.462.refs_3_, ...), custom_call_target="tpu_custom_call" | custom-call | tf_op jit(solution)/shard_map/attend_back/pallas_call | solution.py:731
  576.8 18.5 %attend_back.5 = (bf16[8,3,16,16,128]{4,3,2,1,0:T(8,128)(2,1)}, f32[2048,128]{1,0:T(8,128)S(1)}) custom-call(s32[1]{0:T(128)} %bitcast.48.len_ref.refs_0_, bf16[8,3,16,16,128]{4,3,2,1,0:T(8,128)(2,1)} %bitcast.61.piece_ref.refs_1_, bf16[8,16,16,128]{3,2,1,0:T(8,128)(2,1)} %get-tuple-element.266.refs_2_, ...), custom_call_target="tpu_custom_call" | custom-call | tf_op jit(solution)/shard_map/attend_back/pallas_call | solution.py:731
  605.6 16.6 %all-to-all-done.14 = bf16[8,3,256,128]{3,2,1,0:T(8,128)(2,1)} async-done(((bf16[8,3,256,128]{3,2,1,0:T(8,128)(2,1)}), bf16[8,3,256,128]{3,2,1,0:T(8,128)(2,1)}, u32[]{:S(2)}, u32[]{:S(2)}) %all-to-all-start.14) | async-done | bytes 1572896 | tf_op jit(solution)/shard_map/all_to_all | solution.py:1144
  640.6 9.0 weight_grads.5
  651.4 8.4 fusion.17
  672.6 15.3 %weight_grads.6 = bf16[4,2,64,8704]{3,2,1,0:T(8,128)(2,1)} custom-call(s32[1]{0:T(128)} %bitcast.core_ref, bf16[512,1024]{1,0:T(8,128)(2,1)S(1)} %copy-done.22, bf16[512,1024]{1,0:T(8,128)(2,1)} %collective-permute-done.65.refs_1_, bf16[512,2816]{1,0:T(8,128)(2,1)} %get-tuple-element.332.refs_2_, bf16[512,2816]{1,0:T(8,128)(2,1)} %collective-permute-done.66.refs_3_, ...), custom_call_target="tpu_custom_call" | custom-call | tf_op jit(solution)/shard_map/weight_grads/pallas_call | solution.py:461
  712.0 14.8 %all-to-all-done.16 = bf16[8,512,128]{2,1,0:T(8,128)(2,1)S(1)} async-done(((bf16[8,512,128]{2,1,0:T(8,128)(2,1)}), bf16[8,512,128]{2,1,0:T(8,128)(2,1)S(1)}, u32[]{:S(2)}, u32[]{:S(2)}) %all-to-all-start.16) | async-done | bytes 1048608 | tf_op jit(solution)/shard_map/all_to_all | solution.py:1144
  734.9 15.8 %attend_back.6 = bf16[8,3,16,16,128]{4,3,2,1,0:T(8,128)(2,1)} custom-call(s32[1]{0:T(128)} %bitcast.1.len_ref.refs_0_, bf16[8,3,16,16,128]{4,3,2,1,0:T(8,128)(2,1)} %bitcast.384, bf16[8,16,16,128]{3,2,1,0:T(8,128)(2,1)S(1)} %copy-done.24, bf16[8,16,16,128]{3,2,1,0:T(8,128)(2,1)S(1)} %get-tuple-element.460.refs_3_, f32[8,2048]{1,0:T(8,128)S(1)} %get-tuple-element.344.refs_4_, ...), custom_call_target="tpu_custom_call" | custom-call | tf_op jit(solution)/shard_map/attend_back/pallas_call | solution.py:731
  759.2 18.2 %attend_back.7 = bf16[8,3,16,16,128]{4,3,2,1,0:T(8,128)(2,1)} custom-call(s32[1]{0:T(128)} %bitcast.48.len_ref.refs_0_, bf16[8,3,16,16,128]{4,3,2,1,0:T(8,128)(2,1)} %bitcast.383, bf16[8,16,16,128]{3,2,1,0:T(8,128)(2,1)S(1)} %copy-done.26, bf16[8,16,16,128]{3,2,1,0:T(8,128)(2,1)S(1)} %get-tuple-element.353.refs_3_, ...), custom_call_target="tpu_custom_call" | custom-call | tf_op jit(solution)/shard_map/attend_back/pallas_call | solution.py:731
  790.5 19.6 %collective-permute-done.72 = bf16[32,4352]{1,0:T(8,128)(2,1)S(1)} collective-permute-done((bf16[32,4352]{1,0:T(8,128)(2,1)S(1)}, bf16[32,4352]{1,0:T(8,128)(2,1)S(1)}, u32[]{:S(2)}, u32[]{:S(2)}) %collective-permute-start.72) | collective-permute-done | bytes 278560 | tf_op jit(solution)/shard_map/ppermute | solution.py:75
  831.7 9.0 weight_grads.7
  846.9 20.9 %collective-permute-done.78 = bf16[4,2,32,2048]{3,2,1,0:T(8,128)(2,1)S(1)} collective-permute-done((bf16[4,2,32,2048]{3,2,1,0:T(8,128)(2,1)S(1)}, bf16[4,2,32,2048]{3,2,1,0:T(8,128)(2,1)S(1)}, u32[]{:S(2)}, u32[]{:S(2)}) %collective-permute-start.78) | collective-permute-done | bytes 1048608 | tf_op jit(solution)/shard_map/ppermute | solution.py:75
  887.5 19.2 %collective-permute-start.87 = (bf16[32,2048]{1,0:T(8,128)(2,1)S(1)}, bf16[32,2048]{1,0:T(8,128)(2,1)S(1)}, u32[]{:S(2)}, u32[]{:S(2)}) collective-permute-start(bf16[32,2048]{1,0:T(8,128)(2,1)S(1)} %get-tuple-element.485), channel_id=1, source_target_pairs={{0,2},{2,0},{4,6},{6,4},{1,3},{3,1},{5,7},{7,5},{8,10},{10,8},{12,... | collective-permute-start | bytes 393224 | tf_op jit(solution)/shard_map/ppermute | solution.py:79
  955.1 12.9 %all-to-all-done.19 = bf16[4,2,2,2,16,1024]{5,4,3,1,2,0:T(8,128)(2,1)S(1)} async-done(((bf16[4,2,2,2,16,1024]{5,4,3,1,2,0:T(8,128)(2,1)}), bf16[4,2,2,2,16,1024]{5,4,3,1,2,0:T(8,128)(2,1)S(1)}, u32[]{:S(2)}, u32[]{:S(2)}) %all-to-all-start.19) | async-done | bytes 1048608 | tf_op jit(solution)/shard_map/all_to_all | solution.py:1148
  977.1 10.5 %all-to-all-done.20 = bf16[8,2,2,16,1024]{4,3,2,1,0:T(8,128)(2,1)S(1)} async-done(((bf16[8,2,2,16,1024]{4,3,2,1,0:T(8,128)(2,1)}), bf16[8,2,2,16,1024]{4,3,2,1,0:T(8,128)(2,1)S(1)}, u32[]{:S(2)}, u32[]{:S(2)}) %all-to-all-start.20) | async-done | bytes 1048608 | tf_op jit(solution)/shard_map/all_to_all | solution.py:1144
  (754 shorter events, 516.3 us)
Async XLA Ops:
  7.2 189.3 %all-gather.3.cloned.1.call-start = ((), (), s32[]{:S(2)}) async-start(), calls=%async_computation.24 | async-start | bytes 20545536 | tf_op jit(solution)/shard_map/all_gather | solution.py:1165
  44.6 70.3 %all-to-all-start.1 = ((bf16[4,2,2,2,16,1024]{5,4,3,1,2,0:T(8,128)(2,1)}), bf16[4,2,2,2,16,1024]{5,4,3,1,2,0:T(8,128)(2,1)}, u32[]{:S(2)}, u32[]{:S(2)}) async-start(bf16[4,2,2,2,16,1024]{5,4,3,1,2,0:T(8,128)(2,1)} %copy.141), calls=%async_computation.1 | async-start | bytes 2097152 | tf_op jit(solution)/shard_map/all_to_all | solution.py:1148
  124.5 37.3 %all-to-all-start.2 = ((bf16[8,3,256,128]{3,2,1,0:T(8,128)(2,1)}), bf16[8,3,256,128]{3,2,1,0:T(8,128)(2,1)S(1)}, u32[]{:S(2)}, u32[]{:S(2)}) async-start(bf16[8,3,256,128]{3,2,1,0:T(8,128)(2,1)} %copy-done.14), calls=%async_computation.2 | async-start | bytes 3145728 | tf_op jit(solution)/shard_map/all_to_all | solution.py:1144
  162.9 40.3 %all-to-all-start.3 = ((bf16[8,3,256,128]{3,2,1,0:T(8,128)(2,1)}), bf16[8,3,256,128]{3,2,1,0:T(8,128)(2,1)S(1)}, u32[]{:S(2)}, u32[]{:S(2)}) async-start(bf16[8,3,256,128]{3,2,1,0:T(8,128)(2,1)} %copy-done.13), calls=%async_computation.3 | async-start | bytes 3145728 | tf_op jit(solution)/shard_map/all_to_all | solution.py:1144
  166.5 255.2 %all-gather.5.cloned.1.call-start = ((), (), s32[]{:S(2)}) async-start(), calls=%async_computation.25 | async-start | bytes 18382848 | tf_op jit(solution)/shard_map/all_gather | solution.py:1165
  168.7 34.6 %collective-permute-start.31 = (bf16[32,4224]{1,0:T(8,128)(2,1)S(1)}, bf16[32,4224]{1,0:T(8,128)(2,1)}, u32[]{:S(2)}, u32[]{:S(2)}) collective-permute-start(bf16[32,4224]{1,0:T(8,128)(2,1)S(1)} %fusion.77), channel_id=1, source_target_pairs={{0,2},{2,0},{4,6},{6,4},{1,3},{3,1},{5,7},{7,5},{8,10},{10,8},{12,... | collective-permute-start | bytes 811016 | tf_op jit(solution)/shard_map/ppermute | solution.py:79
  175.0 28.2 %collective-permute-start.32 = (bf16[32,4224]{1,0:T(8,128)(2,1)S(1)}, bf16[32,4224]{1,0:T(8,128)(2,1)}, u32[]{:S(2)}, u32[]{:S(2)}) collective-permute-start(bf16[32,4224]{1,0:T(8,128)(2,1)S(1)} %fusion.77), channel_id=1, source_target_pairs={{0,4},{2,6},{4,0},{6,2},{1,5},{3,7},{5,1},{7,3},{8,12},{10,14},{12... | collective-permute-start | bytes 811016 | tf_op jit(solution)/shard_map/ppermute | solution.py:79
  205.6 28.4 %collective-permute-start.35 = (bf16[4,32,2176]{2,1,0:T(8,128)(2,1)}, bf16[4,32,2176]{2,1,0:T(8,128)(2,1)}, u32[]{:S(2)}, u32[]{:S(2)}) collective-permute-start(bf16[4,32,2176]{2,1,0:T(8,128)(2,1)} %pad_maximum_fusion.12.rest_8_), channel_id=1, source_target_pairs={{0,16},{16,0},{1,17},{17,1},{2,18},{18,2},{3,19},{19,3},{4,20},{20... | collective-permute-start | bytes 1671176 | tf_op jit(solution)/shard_map/ppermute | solution.py:75
  208.9 25.2 %collective-permute-start.34 = (bf16[4,32,2048]{2,1,0:T(8,128)(2,1)}, bf16[4,32,2048]{2,1,0:T(8,128)(2,1)}, u32[]{:S(2)}, u32[]{:S(2)}) collective-permute-start(bf16[4,32,2048]{2,1,0:T(8,128)(2,1)} %pad_maximum_fusion.15.rest_0_), channel_id=1, source_target_pairs={{0,1},{1,0},{2,3},{3,2},{4,5},{5,4},{6,7},{7,6},{8,9},{9,8},{10,11... | collective-permute-start | bytes 1572872 | tf_op jit(solution)/shard_map/ppermute | solution.py:75
  214.3 44.2 %collective-permute-start.38 = (bf16[4,32,2176]{2,1,0:T(8,128)(2,1)}, bf16[4,32,2176]{2,1,0:T(8,128)(2,1)}, u32[]{:S(2)}, u32[]{:S(2)}) collective-permute-start(bf16[4,32,2176]{2,1,0:T(8,128)(2,1)} %pad_maximum_fusion.12.rest_8_), channel_id=1, source_target_pairs={{0,1},{1,0},{2,3},{3,2},{4,5},{5,4},{6,7},{7,6},{8,9},{9,8},{10,11... | collective-permute-start | bytes 1671176 | tf_op jit(solution)/shard_map/ppermute | solution.py:75
  234.1 38.4 %collective-permute-start.39 = (bf16[4,32,2176]{2,1,0:T(8,128)(2,1)}, bf16[4,32,2176]{2,1,0:T(8,128)(2,1)}, u32[]{:S(2)}, u32[]{:S(2)}) collective-permute-start(bf16[4,32,2176]{2,1,0:T(8,128)(2,1)} %collective-permute-done.35.rest_10_), channel_id=1, source_target_pairs={{0,1},{1,0},{2,3},{3,2},{4,5},{5,4},{6,7},{7,6},{8,9},{9,8},{10,11... | collective-permute-start | bytes 1671176 | tf_op jit(solution)/shard_map/ppermute | solution.py:75
  236.4 31.0 %collective-permute-start.37 = (bf16[4,32,2048]{2,1,0:T(8,128)(2,1)}, bf16[4,32,2048]{2,1,0:T(8,128)(2,1)}, u32[]{:S(2)}, u32[]{:S(2)}) collective-permute-start(bf16[4,32,2048]{2,1,0:T(8,128)(2,1)} %collective-permute-done.34.rest_2_), channel_id=1, source_target_pairs={{0,16},{16,0},{1,17},{17,1},{2,18},{18,2},{3,19},{19,3},{4,20},{20... | collective-permute-start | bytes 1572872 | tf_op jit(solution)/shard_map/ppermute | solution.py:75
  276.6 25.1 %all-to-all-start.5 = ((bf16[8,256,128]{2,1,0:T(8,128)(2,1)}), bf16[8,256,128]{2,1,0:T(8,128)(2,1)S(1)}, u32[]{:S(2)}, u32[]{:S(2)}) async-start(bf16[8,256,128]{2,1,0:T(8,128)(2,1)} %bitcast.395), calls=%async_computation.5 | async-start | bytes 1048576 | tf_op jit(solution)/shard_map/all_to_all | solution.py:1144
  301.7 36.7 %all-to-all-start.6 = ((bf16[8,3,256,128]{3,2,1,0:T(8,128)(2,1)}), bf16[8,3,256,128]{3,2,1,0:T(8,128)(2,1)S(1)}, u32[]{:S(2)}, u32[]{:S(2)}) async-start(bf16[8,3,256,128]{3,2,1,0:T(8,128)(2,1)} %copy-done.27), calls=%async_computation.6 | async-start | bytes 3145728 | tf_op jit(solution)/shard_map/all_to_all | solution.py:1144
  338.4 25.2 %all-to-all-start.7 = ((bf16[8,3,256,128]{3,2,1,0:T(8,128)(2,1)}), bf16[8,3,256,128]{3,2,1,0:T(8,128)(2,1)}, u32[]{:S(2)}, u32[]{:S(2)}) async-start(bf16[8,3,256,128]{3,2,1,0:T(8,128)(2,1)} %copy-done.28), calls=%async_computation.7 | async-start | bytes 3145728 | tf_op jit(solution)/shard_map/all_to_all | solution.py:1144
  363.6 53.0 %all-to-all-start.8 = ((bf16[8,256,128]{2,1,0:T(8,128)(2,1)}), bf16[8,256,128]{2,1,0:T(8,128)(2,1)S(1)}, u32[]{:S(2)}, u32[]{:S(2)}) async-start(bf16[8,256,128]{2,1,0:T(8,128)(2,1)} %bitcast.60), calls=%async_computation.8 | async-start | bytes 1048576 | tf_op jit(solution)/shard_map/all_to_all | solution.py:1144
  369.9 27.7 %collective-permute-start.50 = (bf16[2,2,16,1024]{3,2,1,0:T(8,128)(2,1)S(1)}, bf16[2,2,16,1024]{3,2,1,0:T(8,128)(2,1)S(1)}, u32[]{:S(2)}, u32[]{:S(2)}) collective-permute-start(bf16[2,2,16,1024]{3,2,1,0:T(8,128)(2,1)S(1)} %get-tuple-element.468), channel_id=1, source_target_pairs={{0,16},{1,17},{2,0},{3,1},{4,24},{5,25},{6,8},{7,9},{8,20},{9,21},... | collective-permute-start | bytes 393224 | tf_op jit(solution)/shard_map/ppermute | solution.py:1448
  375.0 41.5 %collective-permute-start.51 = (bf16[2,2,16,1024]{3,2,1,0:T(8,128)(2,1)S(1)}, bf16[2,2,16,1024]{3,2,1,0:T(8,128)(2,1)S(1)}, u32[]{:S(2)}, u32[]{:S(2)}) collective-permute-start(bf16[2,2,16,1024]{3,2,1,0:T(8,128)(2,1)S(1)} %get-tuple-element.467), channel_id=1, source_target_pairs={{0,17},{1,16},{2,1},{3,0},{4,25},{5,24},{6,9},{7,8},{8,21},{9,20},... | collective-permute-start | bytes 393224 | tf_op jit(solution)/shard_map/ppermute | solution.py:1448
  375.0 41.5 %collective-permute-start.52 = (bf16[2,2,16,1024]{3,2,1,0:T(8,128)(2,1)S(1)}, bf16[2,2,16,1024]{3,2,1,0:T(8,128)(2,1)S(1)}, u32[]{:S(2)}, u32[]{:S(2)}) collective-permute-start(bf16[2,2,16,1024]{3,2,1,0:T(8,128)(2,1)S(1)} %get-tuple-element.466), channel_id=1, source_target_pairs={{0,8},{1,9},{2,24},{3,25},{4,0},{5,1},{6,16},{7,17},{8,12},{9,13},... | collective-permute-start | bytes 393224 | tf_op jit(solution)/shard_map/ppermute | solution.py:1448
  377.6 39.0 %collective-permute-start.53 = (bf16[2,2,16,1024]{3,2,1,0:T(8,128)(2,1)S(1)}, bf16[2,2,16,1024]{3,2,1,0:T(8,128)(2,1)S(1)}, u32[]{:S(2)}, u32[]{:S(2)}) collective-permute-start(bf16[2,2,16,1024]{3,2,1,0:T(8,128)(2,1)S(1)} %get-tuple-element.465), channel_id=1, source_target_pairs={{0,9},{1,8},{2,25},{3,24},{4,1},{5,0},{6,17},{7,16},{8,13},{9,12},... | collective-permute-start | bytes 393224 | tf_op jit(solution)/shard_map/ppermute | solution.py:1448
  378.7 37.8 %collective-permute-start.54 = (bf16[2,2,16,1024]{3,2,1,0:T(8,128)(2,1)S(1)}, bf16[2,2,16,1024]{3,2,1,0:T(8,128)(2,1)S(1)}, u32[]{:S(2)}, u32[]{:S(2)}) collective-permute-start(bf16[2,2,16,1024]{3,2,1,0:T(8,128)(2,1)S(1)} %get-tuple-element.464), channel_id=1, source_target_pairs={{0,24},{1,25},{2,8},{3,9},{4,16},{5,17},{6,0},{7,1},{8,28},{9,29},... | collective-permute-start | bytes 393224 | tf_op jit(solution)/shard_map/ppermute | solution.py:1448
  446.6 280.1 %reduce-scatter.6.cloned.1.call-start = ((), (), s32[]{:S(2)}) async-start(), calls=%async_computation.27 | async-start | bytes 11141120 | tf_op jit(solution)/shard_map/reduce_scatter | solution.py:1274
  572.4 25.0 %all-to-all-start.13 = ((bf16[8,3,256,128]{3,2,1,0:T(8,128)(2,1)}), bf16[8,3,256,128]{3,2,1,0:T(8,128)(2,1)}, u32[]{:S(2)}, u32[]{:S(2)}) async-start(bf16[8,3,256,128]{3,2,1,0:T(8,128)(2,1)} %bitcast.458), calls=%async_computation.13 | async-start | bytes 3145728 | tf_op jit(solution)/shard_map/all_to_all | solution.py:1144
  601.6 212.4 %reduce-scatter.8.cloned.1.call-start = ((), (), s32[]{:S(2)}) async-start(), calls=%async_computation.28 | async-start | bytes 5242880 | tf_op jit(solution)/shard_map/reduce_scatter | solution.py:1274
  627.8 41.0 %collective-permute-start.68 = (bf16[512,2816]{1,0:T(8,128)(2,1)}, bf16[512,2816]{1,0:T(8,128)(2,1)}, u32[]{:S(2)}, u32[]{:S(2)}) collective-permute-start(bf16[512,2816]{1,0:T(8,128)(2,1)} %get-tuple-element.331.refs_6_), channel_id=1, source_target_pairs={{0,8},{8,0},{1,9},{9,1},{2,10},{10,2},{3,11},{11,3},{4,12},{12,4},... | collective-permute-start | bytes 8650760 | tf_op jit(solution)/shard_map/ppermute | solution.py:75
  664.6 43.8 %all-to-all-start.15 = ((bf16[8,2,2,16,1024]{4,3,2,1,0:T(8,128)(2,1)}), bf16[8,2,2,16,1024]{4,3,2,1,0:T(8,128)(2,1)}, u32[]{:S(2)}, u32[]{:S(2)}) async-start(bf16[8,2,2,16,1024]{4,3,2,1,0:T(8,128)(2,1)} %pad_maximum_fusion.4), calls=%async_computation.15 | async-start | bytes 2097152 | tf_op jit(solution)/shard_map/all_to_all | solution.py:1144
  712.0 199.9 %reduce-scatter.4.cloned.1.call-start = ((), (), s32[]{:S(2)}) async-start(), calls=%async_computation.26 | async-start | bytes 11141120 | tf_op jit(solution)/shard_map/reduce_scatter | solution.py:1274
  754.8 24.8 %all-to-all-start.17 = ((bf16[8,3,256,128]{3,2,1,0:T(8,128)(2,1)}), bf16[8,3,256,128]{3,2,1,0:T(8,128)(2,1)}, u32[]{:S(2)}, u32[]{:S(2)}) async-start(bf16[8,3,256,128]{3,2,1,0:T(8,128)(2,1)} %bitcast.437), calls=%async_computation.19 | async-start | bytes 3145728 | tf_op jit(solution)/shard_map/all_to_all | solution.py:1144
  779.6 30.6 %all-to-all-start.18 = ((bf16[8,3,256,128]{3,2,1,0:T(8,128)(2,1)}), bf16[8,3,256,128]{3,2,1,0:T(8,128)(2,1)}, u32[]{:S(2)}, u32[]{:S(2)}) async-start(bf16[8,3,256,128]{3,2,1,0:T(8,128)(2,1)} %bitcast.436), calls=%async_computation.21 | async-start | bytes 3145728 | tf_op jit(solution)/shard_map/all_to_all | solution.py:1144
  784.2 25.9 %collective-permute-start.72 = (bf16[32,4352]{1,0:T(8,128)(2,1)S(1)}, bf16[32,4352]{1,0:T(8,128)(2,1)S(1)}, u32[]{:S(2)}, u32[]{:S(2)}) collective-permute-start(bf16[32,4352]{1,0:T(8,128)(2,1)S(1)} %dynamic-slice_bitcast_fusion.15), channel_id=1, source_target_pairs={{0,16},{16,0},{1,17},{17,1},{2,18},{18,2},{3,19},{19,3},{4,20},{20... | collective-permute-start | bytes 835592 | tf_op jit(solution)/shard_map/ppermute | solution.py:75
  887.5 26.9 %collective-permute-start.87 = (bf16[32,2048]{1,0:T(8,128)(2,1)S(1)}, bf16[32,2048]{1,0:T(8,128)(2,1)S(1)}, u32[]{:S(2)}, u32[]{:S(2)}) collective-permute-start(bf16[32,2048]{1,0:T(8,128)(2,1)S(1)} %get-tuple-element.485), channel_id=1, source_target_pairs={{0,2},{2,0},{4,6},{6,4},{1,3},{3,1},{5,7},{7,5},{8,10},{10,8},{12,... | collective-permute-start | bytes 393224 | tf_op jit(solution)/shard_map/ppermute | solution.py:79
  940.6 27.4 %all-to-all-start.19 = ((bf16[4,2,2,2,16,1024]{5,4,3,1,2,0:T(8,128)(2,1)}), bf16[4,2,2,2,16,1024]{5,4,3,1,2,0:T(8,128)(2,1)S(1)}, u32[]{:S(2)}, u32[]{:S(2)}) async-start(bf16[4,2,2,2,16,1024]{5,4,3,1,2,0:T(8,128)(2,1)} %copy.163), calls=%async_computation.22 | async-start | bytes 2097152 | tf_op jit(solution)/shard_map/all_to_all | solution.py:1148
  (255 other events, 2562.0 us)
Sparse Core Ops, SparseCore 0:
  13.1 167.3 all-gather.2
  203.4 151.9 all-gather.4
  514.7 151.9 reduce-scatter.5
  668.9 77.6 reduce-scatter.7
  748.9 153.5 reduce-scatter.3
